TPU v7x, 256 devices: a whole 4x4x8 slice. The times are simulated.
256 devices in a mesh: mem: 64 (over y, z_hi, x, core), qry: 4 (over z_lo).
Axes of the slice: x: 4, y: 4, z: 8 (z_hi: 2, z_lo: 4; z = z_hi * 4 + z_lo), core: 2. Of those that a mesh axis runs over, the one named last changes fastest.
Arguments:
- queries: bfloat16 [1024, 4096], P('qry', 'mem'), may hold values from -6 to 6
- outputs: bfloat16 [1024, 4096], P('qry', 'mem'), may hold values from -6 to 6
- cotangent: bfloat16 [1024, 4096], P('qry', 'mem'), may hold values from -3072 to 3072
- log_norms: float32 [1024, 16], P('qry'), as said below
- memory_keys: bfloat16 [32768, 4096], P(('mem', 'qry')), may hold values from -6 to 6
- memory_values: bfloat16 [32768, 4096], P(('mem', 'qry')), may hold values from -6 to 6
Outputs:
- query_grads: bfloat16 [1024, 4096], P('qry', 'mem')
- key_grads: bfloat16 [32768, 4096], P(('mem', 'qry'))
- value_grads: bfloat16 [32768, 4096], P(('mem', 'qry'))
Inputs may be any that keep to these rules, and one draw needn't show every extreme that they name: `log_norms`: each entry lies within half a unit of log(32768) + 0.5.
All inputs are finite; a program needn't handle non-finite values.
Results may differ from a plain program's by a relative error of at most 0.018.
Values may be sent and summed in bfloat16 or wider, within the bound.
No kernel may reach another device: no remote copies, remote signals or barrier semaphores. Data moves between devices by JAX's collectives and lax.ppermute only.
A program may use at most 128 MiB of HBM per device.

v0:
```python
import jax
import jax.numpy as jnp
from jax import lax
from jax.sharding import PartitionSpec as P

group_heads = 4


def head_slice(matrix, leading, number, head_width):
    picked = matrix[:, leading * head_width : (leading + number) * head_width]
    return picked.reshape(matrix.shape[0], number, head_width)


def attention_terms(
    all_queries, all_cotangent, row_sums, log_norms, key_rows, value_rows, leading, number
):
    head_width = all_queries.shape[1] // log_norms.shape[1]
    factor = head_width ** (-0.5)
    head_queries = head_slice(all_queries, leading, number, head_width)
    head_cotangent = head_slice(all_cotangent, leading, number, head_width)
    head_keys = head_slice(key_rows, leading, number, head_width)
    head_values = head_slice(value_rows, leading, number, head_width)
    offsets = jnp.transpose(log_norms[:, leading : leading + number])[:, :, None]
    centres = jnp.transpose(row_sums[:, leading : leading + number])[:, :, None]
    scores = (
        jnp.einsum("qgd,kgd->gqk", head_queries, head_keys, preferred_element_type=jnp.float32)
        * factor
    )
    weights = jnp.exp(scores - offsets)
    slopes = jnp.einsum(
        "qgd,kgd->gqk", head_cotangent, head_values, preferred_element_type=jnp.float32
    )
    score_grads = (weights * (slopes - centres)).astype(jnp.bfloat16)
    return (
        weights.astype(jnp.bfloat16),
        score_grads,
        head_queries,
        head_cotangent,
        head_keys,
        factor,
    )


def memory_terms(weights, score_grads, head_queries, head_cotangent, factor):
    row_count = weights.shape[2]
    value_part = jnp.einsum(
        "gqk,qgd->kgd", weights, head_cotangent, preferred_element_type=jnp.float32
    )
    key_part = (
        jnp.einsum("gqk,qgd->kgd", score_grads, head_queries, preferred_element_type=jnp.float32)
        * factor
    )
    return (key_part.reshape(row_count, -1), value_part.reshape(row_count, -1))


def query_term(score_grads, head_keys, factor):
    query_part = (
        jnp.einsum("gqk,kgd->qgd", score_grads, head_keys, preferred_element_type=jnp.float32)
        * factor
    )
    return query_part.reshape(query_part.shape[0], -1)


def local(queries, outputs, cotangent, log_norms, memory_keys, memory_values):
    head_count = log_norms.shape[1]
    all_queries, all_cotangent = (
        lax.all_gather(queries, "mem", axis=1, tiled=True),
        lax.all_gather(cotangent, "mem", axis=1, tiled=True),
    )
    head_width = all_queries.shape[1] // head_count
    columns = queries.shape[1]
    owners = (lax.axis_index("mem") * columns + lax.iota(jnp.int32, columns)) // head_width
    selector = (owners[:, None] == lax.iota(jnp.int32, head_count)[None, :]).astype(jnp.float32)
    products = cotangent.astype(jnp.float32) * outputs.astype(jnp.float32)
    partial_sums = jnp.dot(products, selector, precision=lax.Precision.HIGHEST)
    row_sums = lax.psum(partial_sums, "mem")
    key_rows, value_rows = (
        lax.all_gather(memory_keys, "qry", axis=0, tiled=True),
        lax.all_gather(memory_values, "qry", axis=0, tiled=True),
    )
    query_parts = []
    key_parts = []
    value_parts = []
    for leading in range(0, head_count, group_heads):
        terms = attention_terms(
            all_queries,
            all_cotangent,
            row_sums,
            log_norms,
            key_rows,
            value_rows,
            leading,
            group_heads,
        )
        key_part, value_part = memory_terms(terms[0], terms[1], terms[2], terms[3], terms[5])
        key_parts.append(key_part)
        value_parts.append(value_part)
        query_parts.append(query_term(terms[1], terms[4], terms[5]))
    key_sums, value_sums = (
        lax.psum_scatter(
            jnp.concatenate(key_parts, axis=1).astype(jnp.bfloat16),
            "qry",
            scatter_dimension=0,
            tiled=True,
        ).astype(jnp.float32),
        lax.psum_scatter(
            jnp.concatenate(value_parts, axis=1).astype(jnp.bfloat16),
            "qry",
            scatter_dimension=0,
            tiled=True,
        ).astype(jnp.float32),
    )
    query_local = jnp.concatenate(query_parts, axis=1)
    query_sums = lax.psum_scatter(query_local, "mem", scatter_dimension=1, tiled=True)
    return (
        query_sums.astype(jnp.bfloat16),
        key_sums.astype(jnp.bfloat16),
        value_sums.astype(jnp.bfloat16),
    )


def solution(mesh):
    return jax.shard_map(
        local,
        mesh=mesh,
        in_specs=(
            P("qry", "mem"),
            P("qry", "mem"),
            P("qry", "mem"),
            P("qry", None),
            P(("mem", "qry"), None),
            P(("mem", "qry"), None),
        ),
        out_specs=(P("qry", "mem"), P(("mem", "qry"), None), P(("mem", "qry"), None)),
        check_vma=False,
    )
```

profile of v0, /device:TPU:1, one launch (start us, length us, event | category | flops | bytes accessed | tf_op | source)
XLA Modules:
  0.0 1076.2 jit_solution(10735077426425534980)
XLA Ops:
  7.2 0.7 all-gather.5.cloned.1.call-update
  8.0 0.7 all-gather.9.cloned.1.call-update
  8.7 2.3 copy.29
  11.1 1.3 copy.32
  12.8 408.3 %psum.7 = f32[256,16]{0,1:T(8,128)S(1)} all-reduce(f32[256,16]{0,1:T(8,128)S(1)} %fusion.16), channel_id=1, replica_groups=mesh['mem'=64,'qry'=4] {'mem'}, use_global_device_ids=true, to_apply=%region_0.1 | all-reduce | flops 4096 | bytes 32768 | tf_op jit(solution)/shard_map/psum | solution.py:76
  421.1 2.7 fusion.28
  423.8 3.0 fusion.27
  426.8 3.9 fusion.26
  430.7 1.0 copy-done.15
  431.8 0.5 fusion.32
  432.3 2.5 fusion.25
  434.8 0.7 multiply_convert_fusion.4
  436.5 0.7 copy-done.14
  437.9 0.8 multiply_convert_fusion.7
  438.7 0.5 copy-done
  439.7 1.1 copy-done.13
  440.9 0.5 fusion.31
  441.4 0.8 multiply_convert_fusion.5
  442.2 0.5 copy-done.2
  443.2 1.1 copy-done.12
  444.5 0.5 fusion.30
  445.0 0.8 multiply_convert_fusion.6
  445.8 0.6 copy-done.4
  446.9 0.5 copy-done.10
  447.4 2.2 pad_maximum_fusion
  449.7 2.5 multiply_convert_fusion
  452.1 2.4 copy.50
  454.5 2.5 multiply_convert_fusion.3
  456.9 2.4 copy.47
  459.3 2.5 multiply_convert_fusion.1
  461.8 2.4 copy.49
  464.1 2.5 multiply_convert_fusion.2
  466.6 2.4 copy.48
  469.0 3.6 pad_maximum_fusion.1
  472.8 0.8 copy-done.28
  473.6 1.6 convolution_convert_fusion
  475.1 2.4 copy.54
  477.6 1.6 convolution_convert_fusion.3
  479.2 2.4 copy.51
  481.6 1.6 convolution_convert_fusion.1
  483.2 2.4 copy.53
  485.6 1.6 convolution_convert_fusion.2
  487.2 1.6 copy.52
  489.0 4.7 pad_maximum_fusion.2
  493.7 404.2 %reduce-scatter.4.cloned.1.call-done = f32[256,64]{0,1:T(8,128)} async-done(((f32[256,4096]{0,1:T(8,128)}), f32[256,64]{0,1:T(8,128)}) %reduce-scatter.4.cloned.1.call-update) | async-done | bytes 65552 | tf_op jit(solution)/shard_map/reduce_scatter | solution.py:114
  897.9 1.5 convert_element_type.46
  899.4 84.1 %reduce-scatter.6.cloned.1.call-done = bf16[128,4096]{1,0:T(8,128)(2,1)} async-done(((bf16[512,4096]{1,0:T(8,128)(2,1)}), bf16[128,4096]{1,0:T(8,128)(2,1)}) %reduce-scatter.6.cloned.1.call-update) | async-done | bytes 1048592 | tf_op jit(solution)/shard_map/reduce_scatter | solution.py:100
  983.5 85.9 %reduce-scatter.8.cloned.1.call-done = bf16[128,4096]{1,0:T(8,128)(2,1)} async-done(((bf16[512,4096]{1,0:T(8,128)(2,1)}), bf16[128,4096]{1,0:T(8,128)(2,1)}) %reduce-scatter.8.cloned.1.call-update) | async-done | bytes 1048592 | tf_op jit(solution)/shard_map/reduce_scatter | solution.py:106
  (88 shorter events, 4.4 us)
Async XLA Ops:
  7.2 3.9 copy-start.32
  7.2 413.9 %all-gather.5.cloned.1.call-start = ((), (), s32[]{:S(2)}) async-start(), calls=%async_computation.3 | async-start | bytes 2129920 | tf_op jit(solution)/shard_map/all_gather | solution.py:67
  7.9 415.9 %all-gather.9.cloned.1.call-start = ((), (), s32[]{:S(2)}) async-start(), calls=%async_computation.5 | async-start | bytes 2129920 | tf_op jit(solution)/shard_map/all_gather | solution.py:68
  8.7 418.2 %all-gather.7.cloned.1.call-start = ((), (), s32[]{:S(2)}) async-start(), calls=%async_computation.4 | async-start | bytes 5242880 | tf_op jit(solution)/shard_map/all_gather | solution.py:78
  11.0 1.5 copy-start.33
  11.0 1.5 copy-start.35
  11.0 410.1 %copy-start.34 = (f32[256,16]{0,1:T(8,128)S(1)}, f32[256,16]{0,1:T(8,128)}, u32[]{:S(2)}) copy-start(f32[256,16]{0,1:T(8,128)} %param.9) | copy-start | bytes 49156
  11.0 421.3 %all-gather.11.cloned.1.call-start = ((), (), s32[]{:S(2)}) async-start(), calls=%async_computation.6 | async-start | bytes 5242880 | tf_op jit(solution)/shard_map/all_gather | solution.py:79
  12.4 885.5 %reduce-scatter.4.cloned.1.call-start = ((), (), s32[]{:S(2)}) async-start(), calls=%async_computation.7 | async-start | bytes 4259840 | tf_op jit(solution)/shard_map/reduce_scatter | solution.py:114
  423.8 6.9 copy-start.20
  430.7 1.0 copy-start.15
  432.3 2.5 copy-start.27
  434.8 1.2 copy-start.16
  436.0 1.2 copy-start.14
  436.0 1.4 copy-start.19
  436.5 1.4 copy-start.25
  437.9 1.3 copy-start
  439.2 2.2 copy-start.6
  439.2 1.6 copy-start.13
  439.2 1.7 copy-start.18
  439.7 1.8 copy-start.23
  441.4 1.3 copy-start.2
  442.7 2.2 copy-start.8
  442.7 1.6 copy-start.12
  442.7 1.7 copy-start.17
  443.2 1.8 copy-start.21
  445.0 1.4 copy-start.4
  446.4 1.0 copy-start.10
  449.6 533.9 %reduce-scatter.6.cloned.1.call-start = ((), (), s32[]{:S(2)}) async-start(), calls=%async_computation.8 | async-start | bytes 5242880 | tf_op jit(solution)/shard_map/reduce_scatter | solution.py:100
  452.1 2.4 copy-start.7
  456.9 2.4 copy-start.9
  461.8 2.4 copy-start.11
  466.6 2.4 copy-start.30
  472.5 1.0 copy-start.28
  472.5 5.0 copy-start.26
  472.6 596.8 %reduce-scatter.8.cloned.1.call-start = ((), (), s32[]{:S(2)}) async-start(), calls=%async_computation.9 | async-start | bytes 5242880 | tf_op jit(solution)/shard_map/reduce_scatter | solution.py:106
  475.1 2.4 copy-start.1
  477.6 4.0 copy-start.24
  479.2 2.4 copy-start.3
  481.6 4.0 copy-start.22
  483.2 2.4 copy-start.5
  487.2 1.6 copy-start.29
  487.2 1.9 copy-start.31
Sparse Core Ops, SparseCore 0:
  11.7 87.1 all-gather.4
  102.6 76.9 all-gather.8
  181.9 81.0 all-gather.6
  264.6 84.4 all-gather.10
  449.8 448.1 reduce-scatter.3
  901.1 82.4 reduce-scatter.5
  986.6 82.6 reduce-scatter.7
where the time goes:
time: 1080 us
  waiting for transfers between devices  576 us (53%)
  blocking collectives  408 us (38%)
  local copies, waits for them, and re-layouts  42.2 us (4%)
  matrix products  23.2 us (2%)
  between operations  14.5 us (1%)
  other arithmetic  11.9 us (1%)
    psum x1, blocking collectives, local(): row_sums = lax.psum(partial_sums, 'mem')  408 us
    reduce_scatter x1, waiting for transfers between devices, local(): lax.psum_scatter(query_local, 'mem', scatter_dimension=1, tiled=True)  404 us
    reduce_scatter x1, waiting for transfers between devices, local(): lax.psum_scatter(jnp.concatenate(value_parts, axis=1).astype(jnp.bfloat16...  85.9 us
    reduce_scatter x1, waiting for transfers between devices, local(): lax.psum_scatter(jnp.concatenate(key_parts, axis=1).astype(jnp.bfloat16),...  84.1 us
  transfers between devices with their start and end apart: 7, of which 3 were waited for; matrix products, arithmetic and copies ran while one was open for 5% of the time, Pallas kernels for 0%

commit v1 on v0

v1 whole, which is shorter than its diff:
```python
import jax
import jax.numpy as jnp
from jax import lax
from jax.experimental import pallas as pl
from jax.experimental.pallas import tpu as pltpu
from jax.sharding import Mesh, PartitionSpec as P

AXES = ("y", "zh", "x", "core", "zl")
SIZES = (4, 2, 4, 2, 4)
MEM = ("y", "zh", "x", "core")
PLANE_Z = ("zh", "zl")
HEADS = 16
DH = 256
ROWS = 256
PART = 64
KEYS = 128
STAT = 16
MESSAGE = 2 * PART + STAT
FACTOR = DH**-0.5
LOG2E = 1.4426950408889634
SLOTS = [(dy, dc) for dy in (0, 1, 2, 3) for dc in (0, 1)]
BF16, F32 = jnp.bfloat16, jnp.float32
ANY = pl.BlockSpec(memory_space=pl.ANY)
VMEM = pl.BlockSpec(memory_space=pltpu.VMEM)


def memory_pairs(dy, dc):
    return [
        (y * 2 + c, ((y + dy) % 4) * 2 + (c ^ dc)) for y in range(4) for c in range(2)
    ]


def plane_pairs(k):
    return [
        ((2 * xh + j // 2) * 2 + j % 2, (j ^ k) * 2 + xh)
        for xh in range(2)
        for j in range(4)
    ]


def inverse(pairs):
    return [(b, a) for a, b in pairs]


def pieces(value):
    high = value.astype(BF16)
    rest = value - high.astype(F32)
    middle = rest.astype(BF16)
    low = (rest - middle.astype(F32)).astype(BF16)
    return [high, middle, low]


def message_kernel(queries, outputs, cotangent, log_norms, message):
    sums = jnp.sum(
        cotangent[...].astype(F32) * outputs[...].astype(F32), axis=0, keepdims=True
    )
    zh, x, y = lax.axis_index("zh"), lax.axis_index("x"), lax.axis_index("y")
    head = 4 * y + 2 * zh + x // 2
    mine = lax.broadcasted_iota(jnp.int32, (HEADS, ROWS), 0) == head
    norms = jnp.sum(jnp.where(mine, log_norms[...], 0.0), axis=0, keepdims=True)
    rows = [r.astype(F32) for r in pieces(sums) + pieces(norms)]
    stat = jnp.concatenate(rows + [jnp.zeros((STAT - 6, ROWS), F32)], axis=0).astype(BF16)
    for z in range(8):
        message[z, :PART, :] = queries[...]
        message[z, PART : 2 * PART, :] = cotangent[...]
        message[z, 2 * PART :, :] = stat


def make_message(queries, outputs, cotangent, log_norms):
    return pl.pallas_call(
        message_kernel,
        out_shape=jax.ShapeDtypeStruct((8, MESSAGE, ROWS), BF16),
        in_specs=[VMEM] * 4,
        out_specs=VMEM,
        name="message",
    )(queries, outputs, cotangent, log_norms)


def slot_columns(dy, dc, zh):
    y, core = lax.axis_index("y"), lax.axis_index("core")
    owner = lax.rem(y + dy, 4)
    half = core if dc == 0 else 1 - core
    return pl.ds(pl.multiple_of((4 * owner + 2 * zh + half) * DH, DH), DH)


def split_kernel(keys, values, *refs):
    outs, sem = refs[:8], refs[8]
    copies = []
    for s, (dy, dc) in enumerate(SLOTS):
        for zh in range(2):
            for a, array in enumerate((keys, values)):
                copies.append(
                    pltpu.make_async_copy(
                        array.at[:, slot_columns(dy, dc, zh)],
                        outs[s].at[a, zh],
                        sem.at[len(copies)],
                    )
                )
    for copy in copies:
        copy.start()
    for copy in copies:
        copy.wait()


def split(keys, values):
    return pl.pallas_call(
        split_kernel,
        out_shape=[jax.ShapeDtypeStruct((2, 2, KEYS, DH), BF16)] * 8,
        in_specs=[ANY] * 2,
        out_specs=[ANY] * 8,
        scratch_shapes=[pltpu.SemaphoreType.DMA((32,))],
        name="split",
    )(keys, values)


def join_kernel(*refs):
    ins, (keys, values, sem) = refs[:8], refs[8:]
    copies = []
    for s, (dy, dc) in enumerate(SLOTS):
        for zh in range(2):
            for a, array in enumerate((keys, values)):
                copies.append(
                    pltpu.make_async_copy(
                        ins[s].at[a, zh],
                        array.at[:, slot_columns(dy, dc, zh)],
                        sem.at[len(copies)],
                    )
                )
    for copy in copies:
        copy.start()
    for copy in copies:
        copy.wait()


def join(chunks):
    return pl.pallas_call(
        join_kernel,
        out_shape=[jax.ShapeDtypeStruct((KEYS, HEADS * DH), BF16)] * 2,
        in_specs=[ANY] * 8,
        out_specs=[ANY] * 2,
        scratch_shapes=[pltpu.SemaphoreType.DMA((32,))],
        name="join",
    )(*chunks)


def dot(a, b, ca, cb):
    return lax.dot_general(a, b, (((ca,), (cb,)), ((), ())), preferred_element_type=F32)


def attention_kernel(*refs):
    messages, chunks = refs[:4], refs[4:12]
    grads, query_grads = refs[12:20], refs[20:24]
    kv, qt, dt, stat, dkv, dqt, ds, sem, out_sem = refs[24:]
    x = lax.axis_index("x")
    reads = []
    for k in range(4):
        j = lax.bitwise_xor(x, k)
        part = pl.ds(pl.multiple_of(j * PART, PART), PART)
        reads.append((messages[k].at[:, :PART, :], qt.at[:, part, :]))
        reads.append((messages[k].at[:, PART : 2 * PART, :], dt.at[:, part, :]))
        reads.append((messages[k].at[:, 2 * PART :, :], stat.at[k]))
    for s in range(8):
        reads.append((chunks[s], kv.at[s]))
    reads = [pltpu.make_async_copy(a, b, sem.at[i]) for i, (a, b) in enumerate(reads)]
    for copy in reads:
        copy.start()
    for copy in reads:
        copy.wait()

    writes = []

    def write(source, target):
        copy = pltpu.make_async_copy(source, target, out_sem.at[len(writes)])
        copy.start()
        writes.append(copy)

    for zh in range(2):
        sums, norms = [], []
        for zl in range(4):
            rows = [stat[k, 4 * zh + zl].astype(F32) for k in range(4)]
            total = rows[0] + rows[1] + rows[2] + rows[3]
            sums.append(total[0:1] + total[1:2] + total[2:3])
            norms.append((rows[0][3:4] + rows[0][4:5] + rows[0][5:6]) * LOG2E)

        for block in range(4):
            keys = kv[2 * block : 2 * block + 2, 0, zh].reshape(2 * KEYS, DH)
            values = kv[2 * block : 2 * block + 2, 1, zh].reshape(2 * KEYS, DH)
            weights, slopes = [], []
            for zl in range(4):
                z = 4 * zh + zl
                score = dot(keys, qt[z], 1, 0)
                weight = jnp.exp2(score * (FACTOR * LOG2E) - norms[zl])
                slope = dot(values, dt[z], 1, 0)
                grad = (weight * (slope - sums[zl])).astype(BF16)
                weights.append(weight.astype(BF16))
                slopes.append(grad)
                ds[zl, block * 2 * KEYS : (block + 1) * 2 * KEYS, :] = grad
            value_grad = sum(dot(weights[zl], dt[4 * zh + zl], 1, 1) for zl in range(4))
            key_grad = sum(dot(slopes[zl], qt[4 * zh + zl], 1, 1) for zl in range(4))
            for half in range(2):
                rows = slice(half * KEYS, (half + 1) * KEYS)
                dkv[2 * block + half, 0, zh] = (key_grad[rows] * FACTOR).astype(BF16)
                dkv[2 * block + half, 1, zh] = value_grad[rows].astype(BF16)
                if zh == 1:
                    write(dkv.at[2 * block + half], grads[2 * block + half])
        keys = kv[:, 0, zh].reshape(8 * KEYS, DH)
        for zl in range(4):
            dqt[4 * zh + zl] = (dot(keys, ds[zl], 0, 0) * FACTOR).astype(BF16)
    for k in range(4):
        j = lax.bitwise_xor(x, k)
        part = pl.ds(pl.multiple_of(j * PART, PART), PART)
        write(dqt.at[:, part, :], query_grads[k])
    for copy in writes:
        copy.wait()


def attention(messages, chunks):
    chunk = jax.ShapeDtypeStruct((2, 2, KEYS, DH), BF16)
    part = jax.ShapeDtypeStruct((8, PART, ROWS), BF16)
    outs = pl.pallas_call(
        attention_kernel,
        out_shape=[chunk] * 8 + [part] * 4,
        in_specs=[ANY] * 12,
        out_specs=[ANY] * 12,
        scratch_shapes=[
            pltpu.VMEM((8, 2, 2, KEYS, DH), BF16),
            pltpu.VMEM((8, DH, ROWS), BF16),
            pltpu.VMEM((8, DH, ROWS), BF16),
            pltpu.VMEM((4, 8, STAT, ROWS), BF16),
            pltpu.VMEM((8, 2, 2, KEYS, DH), BF16),
            pltpu.VMEM((8, DH, ROWS), BF16),
            pltpu.VMEM((4, 8 * KEYS, ROWS), BF16),
            pltpu.SemaphoreType.DMA((20,)),
            pltpu.SemaphoreType.DMA((12,)),
        ],
        compiler_params=pltpu.CompilerParams(vmem_limit_bytes=40 * 1024 * 1024),
        cost_estimate=pl.CostEstimate(
            flops=5 * 2 * 2 * 1024 * 1024 * 256,
            bytes_accessed=8 * 1024 * 1024,
            transcendentals=2 * 1024 * 1024,
        ),
        name="attention",
    )(*messages, *chunks)
    return outs[:8], outs[8:]


def local(queries, outputs, cotangent, log_norms, memory_keys, memory_values):
    chunks = split(memory_keys, memory_values)
    received = [chunks[0]] + [
        lax.ppermute(chunk, ("y", "core"), memory_pairs(*slot))
        for slot, chunk in list(zip(SLOTS, chunks))[1:]
    ]
    message = make_message(queries.T, outputs.T, cotangent.T, log_norms.T)
    gathered = lax.all_to_all(message, PLANE_Z, split_axis=0, concat_axis=0, tiled=True)
    messages = [lax.ppermute(gathered, ("x", "core"), plane_pairs(k)) for k in range(4)]
    grads, query_parts = attention(messages, received)
    query_parts = [
        lax.ppermute(part, ("x", "core"), inverse(plane_pairs(k)))
        for k, part in enumerate(query_parts)
    ]
    part = sum(p.astype(F32) for p in query_parts).astype(BF16)
    returned = [grads[0]] + [
        lax.ppermute(grad, ("y", "core"), inverse(memory_pairs(*slot)))
        for slot, grad in list(zip(SLOTS, grads))[1:]
    ]
    part = lax.all_to_all(part, PLANE_Z, split_axis=0, concat_axis=0, tiled=True)
    query_grads = jnp.sum(part.astype(F32), axis=0).astype(BF16).T
    key_grads, value_grads = join(returned)
    return query_grads, key_grads, value_grads


def solution(mesh):
    fine = Mesh(mesh.devices.reshape(SIZES), AXES)
    return jax.shard_map(
        local,
        mesh=fine,
        in_specs=(
            P("zl", MEM),
            P("zl", MEM),
            P("zl", MEM),
            P("zl", None),
            P(MEM + ("zl",), None),
            P(MEM + ("zl",), None),
        ),
        out_specs=(P("zl", MEM), P(MEM + ("zl",), None), P(MEM + ("zl",), None)),
        check_vma=False,
    )
```

time: 1080 us -> 255 us (0.24)
  waiting for transfers between devices: 576 us -> 52.2 us
  blocking collectives: 408 us -> 0 us
  Pallas kernels: 0 us -> 139 us
  starting transfers between devices: 0.46 us -> 59.3 us
  local copies, waits for them, and re-layouts: 42.2 us -> 2.31 us
  matrix products: 23.2 us -> 0 us
  between operations: 14.5 us -> 0.81 us
    reduce_scatter x3 -> x0, waiting for transfers between devices: 574 us -> none  [the longest x1 404 us: local(): lax.psum_scatter(query_local, 'mem', scatter_dimension=1, tiled=True)]
    psum x1 -> x0, blocking collectives: 408 us -> none  [local(): row_sums = lax.psum(partial_sums, 'mem')]
    pallas_call x0 -> x4, Pallas kernels: none -> 139 us  [the longest x1 64.9 us: split(): pl.pallas_call(split_kernel, out_shape=[jax.ShapeDtypeStruct((2, 2, KEYS,...]
    ppermute x0 -> x22, waiting for transfers between devices: none -> 52.2 us  [the longest x7 24.5 us: local(): lax.ppermute(chunk, ('y', 'core'), memory_pairs(*slot))]
    ppermute x0 -> x22, starting transfers between devices: none -> 43.4 us  [the longest x7 12.8 us: local(): lax.ppermute(grad, ('y', 'core'), inverse(memory_pairs(*slot)))]
    dot_general x21 -> x0, matrix products: 23.2 us -> none  [the longest x4 9.8 us: memory_terms(): jnp.einsum('gqk,qgd->kgd', score_grads, head_queries, preferred_element_t...]
    reshape x8 -> x0, local copies, waits for them, and re-layouts: 18.4 us -> none  [memory_terms(): return (key_part.reshape(row_count, -1), value_part.reshape(row_count, -1))]
    all_to_all x0 -> x2, starting transfers between devices: none -> 15.9 us  [the longest x1 9.01 us: local(): lax.all_to_all(message, PLANE_Z, split_axis=0, concat_axis=0, tiled=True)]
  transfers between devices with their start and end apart: 7 -> 24, of which waited for: 3 -> 12; matrix products, arithmetic and copies ran while one was open for 5% -> 0% of each run, Pallas kernels for 0% -> 51%
where the time goes in v1:
time: 255 us
  Pallas kernels  139 us (55%)
  starting transfers between devices  59.3 us (23%)
  waiting for transfers between devices  52.2 us (20%)
    pallas_call x1, Pallas kernels, split(): pl.pallas_call(split_kernel, out_shape=[jax.ShapeDtypeStruct((2, 2, KEYS,...  64.9 us
    pallas_call x1, Pallas kernels, join(): pl.pallas_call(join_kernel, out_shape=[jax.ShapeDtypeStruct((KEYS, HEADS...  64.9 us
    ppermute x7, waiting for transfers between devices, local(): lax.ppermute(chunk, ('y', 'core'), memory_pairs(*slot))  24.5 us
    ppermute x7, waiting for transfers between devices, local(): lax.ppermute(grad, ('y', 'core'), inverse(memory_pairs(*slot)))  21.8 us
    ppermute x7, starting transfers between devices, local(): lax.ppermute(grad, ('y', 'core'), inverse(memory_pairs(*slot)))  12.8 us
    ppermute x4, starting transfers between devices, local(): lax.ppermute(gathered, ('x', 'core'), plane_pairs(k))  11.4 us
    ppermute x4, starting transfers between devices, local(): lax.ppermute(part, ('x', 'core'), inverse(plane_pairs(k)))  9.83 us
    ppermute x7, starting transfers between devices, local(): lax.ppermute(chunk, ('y', 'core'), memory_pairs(*slot))  9.32 us
  transfers between devices with their start and end apart: 24, of which 12 were waited for; matrix products, arithmetic and copies ran while one was open for 0% of the time, Pallas kernels for 51%

profile of v1, /device:TPU:1, one launch (start us, length us, event | category | flops | bytes accessed | tf_op | source)
XLA Modules:
  0.0 254.9 jit_solution(2276554298214849355)
XLA Ops:
  0.6 1.7 message.1
  2.3 9.0 %all-to-all-start = ((bf16[8,144,256]{2,1,0:T(8,128)(2,1)}), bf16[8,144,256]{2,1,0:T(8,128)(2,1)S(1)}, u32[]{:S(2)}, u32[]{:S(2)}) async-start(bf16[8,144,256]{2,1,0:T(8,128)(2,1)} %message.1), calls=%async_computation | async-start | bytes 1179648 | tf_op jit(solution)/shard_map/all_to_all | solution.py:254
  11.3 64.9 %split.1 = (bf16[2,2,128,256]{3,2,1,0:T(8,128)(2,1)}, bf16[2,2,128,256]{3,2,1,0:T(8,128)(2,1)}, bf16[2,2,128,256]{3,2,1,0:T(8,128)(2,1)}, bf16[2,2,128,256]{3,2,...) custom-call(bf16[128,4096]{1,0:T(8,128)(2,1)} %keys.1, ...), custom_call_target="tpu_custom_call" | custom-call | tf_op jit(solution)/shard_map/split/pallas_call | solution.py:106
  76.2 1.0 collective-permute-start.4
  77.3 1.3 collective-permute-start.5
  78.6 1.5 collective-permute-start.6
  80.1 1.3 collective-permute-start.7
  81.4 2.0 collective-permute-start.8
  83.4 0.0 collective-permute-done.4.refs_5_
  83.4 0.0 all-to-all-done
  83.4 4.6 %collective-permute-start.3 = (bf16[8,144,256]{2,1,0:T(8,128)(2,1)S(1)}, bf16[8,144,256]{2,1,0:T(8,128)(2,1)S(1)}, u32[]{:S(2)}, u32[]{:S(2)}) collective-permute-start(bf16[8,144,256]{2,1,0:T(8,128)(2,1)S(1)} %all-to-all-done), channel_id=1, source_target_pairs={{0,24},{4,16},{8,8},{12,0},{16,28},{20,20},{24,12},{28,4},{1,25},{... | collective-permute-start | bytes 1769480 | tf_op jit(solution)/shard_map/ppermute | solution.py:255
  88.0 0.0 collective-permute-done.5.refs_6_
  88.0 2.2 collective-permute-start.2
  90.2 2.1 collective-permute-done.6.refs_7_
  92.4 0.3 collective-permute-start.1
  92.7 6.4 %collective-permute-done.7.refs_8_ = bf16[2,2,128,256]{3,2,1,0:T(8,128)(2,1)S(1)} collective-permute-done((bf16[2,2,128,256]{3,2,1,0:T(8,128)(2,1)}, bf16[2,2,128,256]{3,2,1,0:T(8,128)(2,1)S(1)}, u32[]{:S(2)}, u32[]{:S(2)}) %collective-permute-start.7) | collective-permute-done | bytes 262176 | tf_op jit(solution)/shard_map/ppermute | solution.py:250
  99.0 4.3 %collective-permute-start = (bf16[8,144,256]{2,1,0:T(8,128)(2,1)S(1)}, bf16[8,144,256]{2,1,0:T(8,128)(2,1)S(1)}, u32[]{:S(2)}, u32[]{:S(2)}) collective-permute-start(bf16[8,144,256]{2,1,0:T(8,128)(2,1)S(1)} %all-to-all-done), channel_id=1, source_target_pairs={{0,0},{4,8},{8,16},{12,24},{16,4},{20,12},{24,20},{28,28},{1,1},{5... | collective-permute-start | bytes 1769480 | tf_op jit(solution)/shard_map/ppermute | solution.py:255
  103.4 1.5 collective-permute-done.8.refs_9_
  104.8 7.9 %collective-permute-done.9.refs_10_ = bf16[2,2,128,256]{3,2,1,0:T(8,128)(2,1)S(1)} collective-permute-done((bf16[2,2,128,256]{3,2,1,0:T(8,128)(2,1)}, bf16[2,2,128,256]{3,2,1,0:T(8,128)(2,1)S(1)}, u32[]{:S(2)}, u32[]{:S(2)}) %collective-permute-start.9) | collective-permute-done | bytes 262176 | tf_op jit(solution)/shard_map/ppermute | solution.py:250
  112.7 2.1 collective-permute-start.10
  114.9 6.6 %collective-permute-done.10.refs_11_ = bf16[2,2,128,256]{3,2,1,0:T(8,128)(2,1)S(1)} collective-permute-done((bf16[2,2,128,256]{3,2,1,0:T(8,128)(2,1)}, bf16[2,2,128,256]{3,2,1,0:T(8,128)(2,1)S(1)}, u32[]{:S(2)}, u32[]{:S(2)}) %collective-permute-start.10) | collective-permute-done | bytes 262176 | tf_op jit(solution)/shard_map/ppermute | solution.py:250
  121.5 0.0 collective-permute-done.3.refs_3_
  121.5 0.0 collective-permute-done.2.refs_2_
  121.5 0.0 copy-start.1
  121.5 0.9 copy-done.1
  122.5 7.3 %attention.1 = (bf16[2,2,128,256]{3,2,1,0:T(8,128)(2,1)S(1)}, bf16[2,2,128,256]{3,2,1,0:T(8,128)(2,1)S(1)}, bf16[2,2,128,256]{3,2,1,0:T(8,128)(2,1)S(1)}, bf16[2...) custom-call(bf16[8,144,256]{2,1,0:T(8,128)(2,1)S(1)} %collective-per, ...), custom_call_target="tpu_custom_call" | custom-call | flops 5368709120 | bytes 8388608 | tf_op jit(solution)/shard_map/attention/pallas_call | solution.py:220
  129.8 0.7 copy-done
  130.5 5.5 %collective-permute-start.11 = (bf16[8,64,256]{2,1,0:T(8,128)(2,1)S(1)}, bf16[8,64,256]{2,1,0:T(8,128)(2,1)S(1)}, u32[]{:S(2)}, u32[]{:S(2)}) collective-permute-start(bf16[8,64,256]{2,1,0:T(8,128)(2,1)S(1)} %get-tuple-element.33), channel_id=1, source_target_pairs={{0,0},{8,4},{16,8},{24,12},{4,16},{12,20},{20,24},{28,28},{1,1},{9... | collective-permute-start | bytes 786440 | tf_op jit(solution)/shard_map/ppermute | solution.py:258
  136.1 1.4 collective-permute-start.12
  137.4 1.0 collective-permute-start.13
  138.4 1.9 collective-permute-start.14
  140.4 0.9 collective-permute-start.15
  141.2 0.2 collective-permute-done.11
  141.4 3.1 %collective-permute-start.16 = (bf16[2,2,128,256]{3,2,1,0:T(8,128)(2,1)S(1)}, bf16[2,2,128,256]{3,2,1,0:T(8,128)(2,1)S(1)}, u32[]{:S(2)}, u32[]{:S(2)}) collective-permute-start(bf16[2,2,128,256]{3,2,1,0:T(8,128)(2,1)S(1)} %get-tuple-element.39), channel_id=1, source_target_pairs={{64,0},{68,4},{128,64},{132,68},{192,128},{196,132},{0,192},{4,196... | collective-permute-start | bytes 786440 | tf_op jit(solution)/shard_map/ppermute | solution.py:263
  144.5 2.5 collective-permute-done.12
  147.0 2.8 %collective-permute-done.13 = bf16[8,64,256]{2,1,0:T(8,128)(2,1)S(1)} collective-permute-done((bf16[8,64,256]{2,1,0:T(8,128)(2,1)S(1)}, bf16[8,64,256]{2,1,0:T(8,128)(2,1)S(1)}, u32[]{:S(2)}, u32[]{:S(2)}) %collective-permute-start.13) | collective-permute-done | bytes 262176 | tf_op jit(solution)/shard_map/ppermute | solution.py:258
  149.8 0.4 collective-permute-done.14
  150.2 0.8 add_convert_fusion
  151.0 6.9 %all-to-all-start.1 = ((bf16[8,64,256]{2,1,0:T(8,128)(2,1)}), bf16[8,64,256]{2,1,0:T(8,128)(2,1)S(1)}, u32[]{:S(2)}, u32[]{:S(2)}) async-start(bf16[8,64,256]{2,1,0:T(8,128)(2,1)} %add_convert_fusion), calls=%async_computation.1 | async-start | bytes 524288 | tf_op jit(solution)/shard_map/all_to_all | solution.py:266
  157.9 5.6 %collective-permute-start.17 = (bf16[2,2,128,256]{3,2,1,0:T(8,128)(2,1)S(1)}, bf16[2,2,128,256]{3,2,1,0:T(8,128)(2,1)S(1)}, u32[]{:S(2)}, u32[]{:S(2)}) collective-permute-start(bf16[2,2,128,256]{3,2,1,0:T(8,128)(2,1)S(1)} %get-tuple-element.40), channel_id=1, source_target_pairs={{68,0},{64,4},{132,64},{128,68},{196,128},{192,132},{4,192},{0,196... | collective-permute-start | bytes 786440 | tf_op jit(solution)/shard_map/ppermute | solution.py:263
  163.6 1.2 collective-permute-start.19
  164.8 2.0 collective-permute-start.21
  166.8 12.4 %collective-permute-done.17.refs_3_ = bf16[2,2,128,256]{3,2,1,0:T(8,128)(2,1)S(1)} collective-permute-done((bf16[2,2,128,256]{3,2,1,0:T(8,128)(2,1)S(1)}, bf16[2,2,128,256]{3,2,1,0:T(8,128)(2,1)S(1)}, u32[]{:S(2)}, u32[]{:S(2)}) %collective-permute-start.17) | collective-permute-done | bytes 262176 | tf_op jit(solution)/shard_map/ppermute | solution.py:263
  179.2 3.9 %collective-permute-done.20.refs_6_ = bf16[2,2,128,256]{3,2,1,0:T(8,128)(2,1)S(1)} collective-permute-done((bf16[2,2,128,256]{3,2,1,0:T(8,128)(2,1)S(1)}, bf16[2,2,128,256]{3,2,1,0:T(8,128)(2,1)S(1)}, u32[]{:S(2)}, u32[]{:S(2)}) %collective-permute-start.20) | collective-permute-done | bytes 262176 | tf_op jit(solution)/shard_map/ppermute | solution.py:263
  183.0 5.6 %collective-permute-done.21.refs_7_ = bf16[2,2,128,256]{3,2,1,0:T(8,128)(2,1)S(1)} collective-permute-done((bf16[2,2,128,256]{3,2,1,0:T(8,128)(2,1)S(1)}, bf16[2,2,128,256]{3,2,1,0:T(8,128)(2,1)S(1)}, u32[]{:S(2)}, u32[]{:S(2)}) %collective-permute-start.21) | collective-permute-done | bytes 262176 | tf_op jit(solution)/shard_map/ppermute | solution.py:263
  188.7 0.7 copy-done.8
  189.4 64.9 %join.1 = (bf16[128,4096]{1,0:T(8,128)(2,1)}, bf16[128,4096]{1,0:T(8,128)(2,1)}) custom-call(bf16[2,2,128,256]{3,2,1,0:T(8,128)(2,1)} %copy-done, bf16[2,2,128,256]{3,2,1,0:T(8,128)(2,1)} %copy-done.2, bf16[2,2,128,256]{3,2,1,0:T(8,128)(2,1)} %copy-done.3, bf16[2,2,128,256]{3,2,1,0:T(8,128)(2,1)} %copy-done.4, bf16[2,2,128,256]{3,2,1,0:T(8,128)(2,1)} %copy-done.5, ...), custom_call_target="tpu_custom_call" | custom-call | tf_op jit(solution)/shard_map/join/pallas_call | solution.py:136
  254.3 0.7 reduce_sum.12
  (24 shorter events, 0.1 us)
Async XLA Ops:
  2.3 81.1 %all-to-all-start = ((bf16[8,144,256]{2,1,0:T(8,128)(2,1)}), bf16[8,144,256]{2,1,0:T(8,128)(2,1)S(1)}, u32[]{:S(2)}, u32[]{:S(2)}) async-start(bf16[8,144,256]{2,1,0:T(8,128)(2,1)} %message.1), calls=%async_computation | async-start | bytes 1179648 | tf_op jit(solution)/shard_map/all_to_all | solution.py:254
  76.2 7.2 %collective-permute-start.4 = (bf16[2,2,128,256]{3,2,1,0:T(8,128)(2,1)}, bf16[2,2,128,256]{3,2,1,0:T(8,128)(2,1)S(1)}, u32[]{:S(2)}, u32[]{:S(2)}) collective-permute-start(bf16[2,2,128,256]{3,2,1,0:T(8,128)(2,1)} %get-tuple-element.26), channel_id=1, source_target_pairs={{0,4},{4,0},{64,68},{68,64},{128,132},{132,128},{192,196},{196,192... | collective-permute-start | bytes 786440 | tf_op jit(solution)/shard_map/ppermute | solution.py:250
  77.3 10.8 %collective-permute-start.5 = (bf16[2,2,128,256]{3,2,1,0:T(8,128)(2,1)}, bf16[2,2,128,256]{3,2,1,0:T(8,128)(2,1)S(1)}, u32[]{:S(2)}, u32[]{:S(2)}) collective-permute-start(bf16[2,2,128,256]{3,2,1,0:T(8,128)(2,1)} %get-tuple-element.27), channel_id=1, source_target_pairs={{0,64},{4,68},{64,128},{68,132},{128,192},{132,196},{192,0},{196,4... | collective-permute-start | bytes 786440 | tf_op jit(solution)/shard_map/ppermute | solution.py:250
  78.6 13.8 %collective-permute-start.6 = (bf16[2,2,128,256]{3,2,1,0:T(8,128)(2,1)}, bf16[2,2,128,256]{3,2,1,0:T(8,128)(2,1)S(1)}, u32[]{:S(2)}, u32[]{:S(2)}) collective-permute-start(bf16[2,2,128,256]{3,2,1,0:T(8,128)(2,1)} %get-tuple-element.28), channel_id=1, source_target_pairs={{0,68},{4,64},{64,132},{68,128},{128,196},{132,192},{192,4},{196,0... | collective-permute-start | bytes 786440 | tf_op jit(solution)/shard_map/ppermute | solution.py:250
  80.1 18.9 %collective-permute-start.7 = (bf16[2,2,128,256]{3,2,1,0:T(8,128)(2,1)}, bf16[2,2,128,256]{3,2,1,0:T(8,128)(2,1)S(1)}, u32[]{:S(2)}, u32[]{:S(2)}) collective-permute-start(bf16[2,2,128,256]{3,2,1,0:T(8,128)(2,1)} %get-tuple-element.29), channel_id=1, source_target_pairs={{0,128},{4,132},{64,192},{68,196},{128,0},{132,4},{192,64},{196,68... | collective-permute-start | bytes 786440 | tf_op jit(solution)/shard_map/ppermute | solution.py:250
  81.4 23.4 %collective-permute-start.8 = (bf16[2,2,128,256]{3,2,1,0:T(8,128)(2,1)}, bf16[2,2,128,256]{3,2,1,0:T(8,128)(2,1)S(1)}, u32[]{:S(2)}, u32[]{:S(2)}) collective-permute-start(bf16[2,2,128,256]{3,2,1,0:T(8,128)(2,1)} %get-tuple-element.30), channel_id=1, source_target_pairs={{0,132},{4,128},{64,196},{68,192},{128,4},{132,0},{192,68},{196,64... | collective-permute-start | bytes 786440 | tf_op jit(solution)/shard_map/ppermute | solution.py:250
  83.4 38.1 %collective-permute-start.3 = (bf16[8,144,256]{2,1,0:T(8,128)(2,1)S(1)}, bf16[8,144,256]{2,1,0:T(8,128)(2,1)S(1)}, u32[]{:S(2)}, u32[]{:S(2)}) collective-permute-start(bf16[8,144,256]{2,1,0:T(8,128)(2,1)S(1)} %all-to-all-done), channel_id=1, source_target_pairs={{0,24},{4,16},{8,8},{12,0},{16,28},{20,20},{24,12},{28,4},{1,25},{... | collective-permute-start | bytes 1769480 | tf_op jit(solution)/shard_map/ppermute | solution.py:255
  88.0 33.5 %collective-permute-start.2 = (bf16[8,144,256]{2,1,0:T(8,128)(2,1)S(1)}, bf16[8,144,256]{2,1,0:T(8,128)(2,1)S(1)}, u32[]{:S(2)}, u32[]{:S(2)}) collective-permute-start(bf16[8,144,256]{2,1,0:T(8,128)(2,1)S(1)} %all-to-all-done), channel_id=1, source_target_pairs={{0,16},{4,24},{8,0},{12,8},{16,20},{20,28},{24,4},{28,12},{1,17},{... | collective-permute-start | bytes 1769480 | tf_op jit(solution)/shard_map/ppermute | solution.py:255
  92.4 29.1 %collective-permute-start.1 = (bf16[8,144,256]{2,1,0:T(8,128)(2,1)S(1)}, bf16[8,144,256]{2,1,0:T(8,128)(2,1)S(1)}, u32[]{:S(2)}, u32[]{:S(2)}) collective-permute-start(bf16[8,144,256]{2,1,0:T(8,128)(2,1)S(1)} %all-to-all-done), channel_id=1, source_target_pairs={{0,8},{4,0},{8,24},{12,16},{16,12},{20,4},{24,28},{28,20},{1,9},{5... | collective-permute-start | bytes 1769480 | tf_op jit(solution)/shard_map/ppermute | solution.py:255
  99.0 22.5 %collective-permute-start = (bf16[8,144,256]{2,1,0:T(8,128)(2,1)S(1)}, bf16[8,144,256]{2,1,0:T(8,128)(2,1)S(1)}, u32[]{:S(2)}, u32[]{:S(2)}) collective-permute-start(bf16[8,144,256]{2,1,0:T(8,128)(2,1)S(1)} %all-to-all-done), channel_id=1, source_target_pairs={{0,0},{4,8},{8,16},{12,24},{16,4},{20,12},{24,20},{28,28},{1,1},{5... | collective-permute-start | bytes 1769480 | tf_op jit(solution)/shard_map/ppermute | solution.py:255
  104.8 7.9 %collective-permute-start.9 = (bf16[2,2,128,256]{3,2,1,0:T(8,128)(2,1)}, bf16[2,2,128,256]{3,2,1,0:T(8,128)(2,1)S(1)}, u32[]{:S(2)}, u32[]{:S(2)}) collective-permute-start(bf16[2,2,128,256]{3,2,1,0:T(8,128)(2,1)} %get-tuple-element.31), channel_id=1, source_target_pairs={{0,192},{4,196},{64,0},{68,4},{128,64},{132,68},{192,128},{196,132... | collective-permute-start | bytes 786440 | tf_op jit(solution)/shard_map/ppermute | solution.py:250
  112.7 8.8 %collective-permute-start.10 = (bf16[2,2,128,256]{3,2,1,0:T(8,128)(2,1)}, bf16[2,2,128,256]{3,2,1,0:T(8,128)(2,1)S(1)}, u32[]{:S(2)}, u32[]{:S(2)}) collective-permute-start(bf16[2,2,128,256]{3,2,1,0:T(8,128)(2,1)} %get-tuple-element.32), channel_id=1, source_target_pairs={{0,196},{4,192},{64,4},{68,0},{128,68},{132,64},{192,132},{196,128... | collective-permute-start | bytes 786440 | tf_op jit(solution)/shard_map/ppermute | solution.py:250
  121.5 1.0 copy-start.1
  129.8 0.7 copy-start
  130.5 10.9 %collective-permute-start.11 = (bf16[8,64,256]{2,1,0:T(8,128)(2,1)S(1)}, bf16[8,64,256]{2,1,0:T(8,128)(2,1)S(1)}, u32[]{:S(2)}, u32[]{:S(2)}) collective-permute-start(bf16[8,64,256]{2,1,0:T(8,128)(2,1)S(1)} %get-tuple-element.33), channel_id=1, source_target_pairs={{0,0},{8,4},{16,8},{24,12},{4,16},{12,20},{20,24},{28,28},{1,1},{9... | collective-permute-start | bytes 786440 | tf_op jit(solution)/shard_map/ppermute | solution.py:258
  136.1 11.0 %collective-permute-start.12 = (bf16[8,64,256]{2,1,0:T(8,128)(2,1)S(1)}, bf16[8,64,256]{2,1,0:T(8,128)(2,1)S(1)}, u32[]{:S(2)}, u32[]{:S(2)}) collective-permute-start(bf16[8,64,256]{2,1,0:T(8,128)(2,1)S(1)} %get-tuple-element.34), channel_id=1, source_target_pairs={{8,0},{0,4},{24,8},{16,12},{12,16},{4,20},{28,24},{20,28},{9,1},{1... | collective-permute-start | bytes 786440 | tf_op jit(solution)/shard_map/ppermute | solution.py:258
  137.4 12.4 %collective-permute-start.13 = (bf16[8,64,256]{2,1,0:T(8,128)(2,1)S(1)}, bf16[8,64,256]{2,1,0:T(8,128)(2,1)S(1)}, u32[]{:S(2)}, u32[]{:S(2)}) collective-permute-start(bf16[8,64,256]{2,1,0:T(8,128)(2,1)S(1)} %get-tuple-element.35), channel_id=1, source_target_pairs={{16,0},{24,4},{0,8},{8,12},{20,16},{28,20},{4,24},{12,28},{17,1},{... | collective-permute-start | bytes 786440 | tf_op jit(solution)/shard_map/ppermute | solution.py:258
  138.4 11.7 %collective-permute-start.14 = (bf16[8,64,256]{2,1,0:T(8,128)(2,1)S(1)}, bf16[8,64,256]{2,1,0:T(8,128)(2,1)S(1)}, u32[]{:S(2)}, u32[]{:S(2)}) collective-permute-start(bf16[8,64,256]{2,1,0:T(8,128)(2,1)S(1)} %get-tuple-element.36), channel_id=1, source_target_pairs={{24,0},{16,4},{8,8},{0,12},{28,16},{20,20},{12,24},{4,28},{25,1},{... | collective-permute-start | bytes 786440 | tf_op jit(solution)/shard_map/ppermute | solution.py:258
  140.4 24.4 %collective-permute-start.15 = (bf16[2,2,128,256]{3,2,1,0:T(8,128)(2,1)S(1)}, bf16[2,2,128,256]{3,2,1,0:T(8,128)(2,1)S(1)}, u32[]{:S(2)}, u32[]{:S(2)}) collective-permute-start(bf16[2,2,128,256]{3,2,1,0:T(8,128)(2,1)S(1)} %get-tuple-element.38), channel_id=1, source_target_pairs={{4,0},{0,4},{68,64},{64,68},{132,128},{128,132},{196,192},{192,196... | collective-permute-start | bytes 786440 | tf_op jit(solution)/shard_map/ppermute | solution.py:263
  141.4 23.4 %collective-permute-start.16 = (bf16[2,2,128,256]{3,2,1,0:T(8,128)(2,1)S(1)}, bf16[2,2,128,256]{3,2,1,0:T(8,128)(2,1)S(1)}, u32[]{:S(2)}, u32[]{:S(2)}) collective-permute-start(bf16[2,2,128,256]{3,2,1,0:T(8,128)(2,1)S(1)} %get-tuple-element.39), channel_id=1, source_target_pairs={{64,0},{68,4},{128,64},{132,68},{192,128},{196,132},{0,192},{4,196... | collective-permute-start | bytes 786440 | tf_op jit(solution)/shard_map/ppermute | solution.py:263
  151.0 103.3 %all-to-all-start.1 = ((bf16[8,64,256]{2,1,0:T(8,128)(2,1)}), bf16[8,64,256]{2,1,0:T(8,128)(2,1)S(1)}, u32[]{:S(2)}, u32[]{:S(2)}) async-start(bf16[8,64,256]{2,1,0:T(8,128)(2,1)} %add_convert_fusion), calls=%async_computation.1 | async-start | bytes 524288 | tf_op jit(solution)/shard_map/all_to_all | solution.py:266
  157.9 21.2 %collective-permute-start.17 = (bf16[2,2,128,256]{3,2,1,0:T(8,128)(2,1)S(1)}, bf16[2,2,128,256]{3,2,1,0:T(8,128)(2,1)S(1)}, u32[]{:S(2)}, u32[]{:S(2)}) collective-permute-start(bf16[2,2,128,256]{3,2,1,0:T(8,128)(2,1)S(1)} %get-tuple-element.40), channel_id=1, source_target_pairs={{68,0},{64,4},{132,64},{128,68},{196,128},{192,132},{4,192},{0,196... | collective-permute-start | bytes 786440 | tf_op jit(solution)/shard_map/ppermute | solution.py:263
  163.5 15.6 %collective-permute-start.18 = (bf16[2,2,128,256]{3,2,1,0:T(8,128)(2,1)S(1)}, bf16[2,2,128,256]{3,2,1,0:T(8,128)(2,1)S(1)}, u32[]{:S(2)}, u32[]{:S(2)}) collective-permute-start(bf16[2,2,128,256]{3,2,1,0:T(8,128)(2,1)S(1)} %get-tuple-element.41), channel_id=1, source_target_pairs={{128,0},{132,4},{192,64},{196,68},{0,128},{4,132},{64,192},{68,196... | collective-permute-start | bytes 786440 | tf_op jit(solution)/shard_map/ppermute | solution.py:263
  163.6 15.6 %collective-permute-start.19 = (bf16[2,2,128,256]{3,2,1,0:T(8,128)(2,1)S(1)}, bf16[2,2,128,256]{3,2,1,0:T(8,128)(2,1)S(1)}, u32[]{:S(2)}, u32[]{:S(2)}) collective-permute-start(bf16[2,2,128,256]{3,2,1,0:T(8,128)(2,1)S(1)} %get-tuple-element.42), channel_id=1, source_target_pairs={{132,0},{128,4},{196,64},{192,68},{4,128},{0,132},{68,192},{64,196... | collective-permute-start | bytes 786440 | tf_op jit(solution)/shard_map/ppermute | solution.py:263
  164.8 23.9 %copy-start.2 = (bf16[2,2,128,256]{3,2,1,0:T(8,128)(2,1)}, bf16[2,2,128,256]{3,2,1,0:T(8,128)(2,1)S(1)}, u32[]{:S(2)}) copy-start(bf16[2,2,128,256]{3,2,1,0:T(8,128)(2,1)S(1)} %collective-permute-done.15.refs_1_) | copy-start | bytes 786436
  164.8 18.3 %collective-permute-start.20 = (bf16[2,2,128,256]{3,2,1,0:T(8,128)(2,1)S(1)}, bf16[2,2,128,256]{3,2,1,0:T(8,128)(2,1)S(1)}, u32[]{:S(2)}, u32[]{:S(2)}) collective-permute-start(bf16[2,2,128,256]{3,2,1,0:T(8,128)(2,1)S(1)} %get-tuple-element.43), channel_id=1, source_target_pairs={{192,0},{196,4},{0,64},{4,68},{64,128},{68,132},{128,192},{132,196... | collective-permute-start | bytes 786440 | tf_op jit(solution)/shard_map/ppermute | solution.py:263
  164.8 23.9 %copy-start.3 = (bf16[2,2,128,256]{3,2,1,0:T(8,128)(2,1)}, bf16[2,2,128,256]{3,2,1,0:T(8,128)(2,1)S(1)}, u32[]{:S(2)}) copy-start(bf16[2,2,128,256]{3,2,1,0:T(8,128)(2,1)S(1)} %collective-permute-done.16.refs_2_) | copy-start | bytes 786436
  164.8 23.9 %collective-permute-start.21 = (bf16[2,2,128,256]{3,2,1,0:T(8,128)(2,1)S(1)}, bf16[2,2,128,256]{3,2,1,0:T(8,128)(2,1)S(1)}, u32[]{:S(2)}, u32[]{:S(2)}) collective-permute-start(bf16[2,2,128,256]{3,2,1,0:T(8,128)(2,1)S(1)} %get-tuple-element.44), channel_id=1, source_target_pairs={{196,0},{192,4},{4,64},{0,68},{68,128},{64,132},{132,192},{128,196... | collective-permute-start | bytes 786440 | tf_op jit(solution)/shard_map/ppermute | solution.py:263
  179.2 9.5 %copy-start.4 = (bf16[2,2,128,256]{3,2,1,0:T(8,128)(2,1)}, bf16[2,2,128,256]{3,2,1,0:T(8,128)(2,1)S(1)}, u32[]{:S(2)}) copy-start(bf16[2,2,128,256]{3,2,1,0:T(8,128)(2,1)S(1)} %collective-permute-done.17.refs_3_) | copy-start | bytes 786436
  179.2 9.5 %copy-start.5 = (bf16[2,2,128,256]{3,2,1,0:T(8,128)(2,1)}, bf16[2,2,128,256]{3,2,1,0:T(8,128)(2,1)S(1)}, u32[]{:S(2)}) copy-start(bf16[2,2,128,256]{3,2,1,0:T(8,128)(2,1)S(1)} %collective-permute-done.18.refs_4_) | copy-start | bytes 786436
  179.2 9.5 %copy-start.6 = (bf16[2,2,128,256]{3,2,1,0:T(8,128)(2,1)}, bf16[2,2,128,256]{3,2,1,0:T(8,128)(2,1)S(1)}, u32[]{:S(2)}) copy-start(bf16[2,2,128,256]{3,2,1,0:T(8,128)(2,1)S(1)} %collective-permute-done.19.refs_5_) | copy-start | bytes 786436
  183.0 5.7 %copy-start.7 = (bf16[2,2,128,256]{3,2,1,0:T(8,128)(2,1)}, bf16[2,2,128,256]{3,2,1,0:T(8,128)(2,1)S(1)}, u32[]{:S(2)}) copy-start(bf16[2,2,128,256]{3,2,1,0:T(8,128)(2,1)S(1)} %collective-permute-done.20.refs_6_) | copy-start | bytes 786436
  188.7 0.7 copy-start.8

commit v2 on v1

--- a/solution.py
+++ b/solution.py
@@ -106,7 +106,7 @@
     return pl.pallas_call(
         split_kernel,
         out_shape=[jax.ShapeDtypeStruct((2, 2, KEYS, DH), BF16)] * 8,
-        in_specs=[ANY] * 2,
+        in_specs=[VMEM] * 2,
         out_specs=[ANY] * 8,
         scratch_shapes=[pltpu.SemaphoreType.DMA((32,))],
         name="split",
@@ -137,7 +137,7 @@
         join_kernel,
         out_shape=[jax.ShapeDtypeStruct((KEYS, HEADS * DH), BF16)] * 2,
         in_specs=[ANY] * 8,
-        out_specs=[ANY] * 2,
+        out_specs=[VMEM] * 2,
         scratch_shapes=[pltpu.SemaphoreType.DMA((32,))],
         name="join",
     )(*chunks)

time: 255 us -> 132 us (0.52)
  Pallas kernels: 139 us -> 15.2 us
  starting transfers between devices: 59.3 us -> 55.3 us
  waiting for transfers between devices: 52.2 us -> 56.1 us
    pallas_call x1, Pallas kernels: 64.9 us -> 3.09 us  [split(): pl.pallas_call(split_kernel, out_shape=[jax.ShapeDtypeStruct((2, 2, KEYS,...]
    pallas_call x1, Pallas kernels: 64.9 us -> 3.15 us  [join(): pl.pallas_call(join_kernel, out_shape=[jax.ShapeDtypeStruct((KEYS, HEADS...]
    ppermute x7, waiting for transfers between devices: 24.5 us -> 15.4 us  [local(): lax.ppermute(chunk, ('y', 'core'), memory_pairs(*slot))]
    all_to_all x1, waiting for transfers between devices: 0.01 us -> 9.06 us  [local(): lax.all_to_all(message, PLANE_Z, split_axis=0, concat_axis=0, tiled=True)]
    ppermute x4, waiting for transfers between devices: 0.01 us -> 3.06 us  [local(): lax.ppermute(gathered, ('x', 'core'), plane_pairs(k))]
  transfers between devices with their start and end apart: 24 -> 24, of which waited for: 12 -> 14; matrix products, arithmetic and copies ran while one was open for 0% -> 1% of each run, Pallas kernels for 51% -> 5%
where the time goes in v2:
time: 132 us; the launch traced here: 131 us
  waiting for transfers between devices  56.1 us (42%)
  starting transfers between devices  55.3 us (42%)
  Pallas kernels  15.2 us (12%)
  local copies, waits for them, and re-layouts  2.32 us (2%)
  other arithmetic  1.48 us (1%)
    ppermute x7, waiting for transfers between devices, local(): lax.ppermute(grad, ('y', 'core'), inverse(memory_pairs(*slot)))  21.6 us
    ppermute x7, waiting for transfers between devices, local(): lax.ppermute(chunk, ('y', 'core'), memory_pairs(*slot))  15.4 us
    ppermute x7, starting transfers between devices, local(): lax.ppermute(grad, ('y', 'core'), inverse(memory_pairs(*slot)))  11.7 us
    ppermute x4, starting transfers between devices, local(): lax.ppermute(gathered, ('x', 'core'), plane_pairs(k))  10.6 us
    ppermute x7, starting transfers between devices, local(): lax.ppermute(chunk, ('y', 'core'), memory_pairs(*slot))  10.1 us
    all_to_all x1, waiting for transfers between devices, local(): lax.all_to_all(message, PLANE_Z, split_axis=0, concat_axis=0, tiled=True)  9.06 us
    all_to_all x1, starting transfers between devices, local(): lax.all_to_all(message, PLANE_Z, split_axis=0, concat_axis=0, tiled=True)  9.01 us
    ppermute x4, starting transfers between devices, local(): lax.ppermute(part, ('x', 'core'), inverse(plane_pairs(k)))  8.31 us
  transfers between devices with their start and end apart: 24, of which 14 were waited for; matrix products, arithmetic and copies ran while one was open for 1% of the time, Pallas kernels for 5%

profile of v2, /device:TPU:1, one launch (start us, length us, event | category | flops | bytes accessed | tf_op | source)
XLA Modules:
  0.0 131.2 jit_solution(2075489699584157072)
XLA Ops:
  0.6 1.7 %message.1 = bf16[8,144,256]{2,1,0:T(8,128)(2,1)} custom-call(bf16[64,256]{1,0:T(8,128)(2,1)} %bitcast.5, bf16[64,256]{1,0:T(8,128)(2,1)} %bitcast.6, bf16[64,256]{1,0:T(8,128)(2,1)} %bitcast.7, f32[16,256]{1,0:T(8,128)} %bitcast.9), custom_call_target="tpu_custom_call" | custom-call | tf_op jit(solution)/shard_map/message/pallas_call | solution.py:70
  2.3 9.0 %all-to-all-start = ((bf16[8,144,256]{2,1,0:T(8,128)(2,1)}), bf16[8,144,256]{2,1,0:T(8,128)(2,1)S(1)}, u32[]{:S(2)}, u32[]{:S(2)}) async-start(bf16[8,144,256]{2,1,0:T(8,128)(2,1)} %message.1), calls=%async_computation | async-start | bytes 1179648 | tf_op jit(solution)/shard_map/all_to_all | solution.py:254
  11.3 3.1 %split.1 = (bf16[2,2,128,256]{3,2,1,0:T(8,128)(2,1)}, bf16[2,2,128,256]{3,2,1,0:T(8,128)(2,1)}, bf16[2,2,128,256]{3,2,1,0:T(8,128)(2,1)}, bf16[2,2,128,256]{3,2,...) custom-call(bf16[128,4096]{1,0:T(8,128)(2,1)} %keys.1, ...), custom_call_target="tpu_custom_call" | custom-call | tf_op jit(solution)/shard_map/split/pallas_call | solution.py:106
  14.4 1.0 collective-permute-start.4
  15.4 1.3 collective-permute-start.5
  16.8 1.5 %collective-permute-start.6 = (bf16[2,2,128,256]{3,2,1,0:T(8,128)(2,1)}, bf16[2,2,128,256]{3,2,1,0:T(8,128)(2,1)S(1)}, u32[]{:S(2)}, u32[]{:S(2)}) collective-permute-start(bf16[2,2,128,256]{3,2,1,0:T(8,128)(2,1)} %get-tuple-element.28), channel_id=1, source_target_pairs={{0,68},{4,64},{64,132},{68,128},{128,196},{132,192},{192,4},{196,0... | collective-permute-start | bytes 786440 | tf_op jit(solution)/shard_map/ppermute | solution.py:250
  18.3 1.3 collective-permute-start.7
  19.6 2.0 %collective-permute-start.8 = (bf16[2,2,128,256]{3,2,1,0:T(8,128)(2,1)}, bf16[2,2,128,256]{3,2,1,0:T(8,128)(2,1)S(1)}, u32[]{:S(2)}, u32[]{:S(2)}) collective-permute-start(bf16[2,2,128,256]{3,2,1,0:T(8,128)(2,1)} %get-tuple-element.30), channel_id=1, source_target_pairs={{0,132},{4,128},{64,196},{68,192},{128,4},{132,0},{192,68},{196,64... | collective-permute-start | bytes 786440 | tf_op jit(solution)/shard_map/ppermute | solution.py:250
  21.6 0.0 collective-permute-done.4.refs_5_
  21.6 9.1 %all-to-all-done = bf16[8,144,256]{2,1,0:T(8,128)(2,1)S(1)} async-done(((bf16[8,144,256]{2,1,0:T(8,128)(2,1)}), bf16[8,144,256]{2,1,0:T(8,128)(2,1)S(1)}, u32[]{:S(2)}, u32[]{:S(2)}) %all-to-all-start) | async-done | bytes 589856 | tf_op jit(solution)/shard_map/all_to_all | solution.py:254
  30.7 5.0 %collective-permute-start.3 = (bf16[8,144,256]{2,1,0:T(8,128)(2,1)S(1)}, bf16[8,144,256]{2,1,0:T(8,128)(2,1)S(1)}, u32[]{:S(2)}, u32[]{:S(2)}) collective-permute-start(bf16[8,144,256]{2,1,0:T(8,128)(2,1)S(1)} %all-to-all-done), channel_id=1, source_target_pairs={{0,24},{4,16},{8,8},{12,0},{16,28},{20,20},{24,12},{28,4},{1,25},{... | collective-permute-start | bytes 1769480 | tf_op jit(solution)/shard_map/ppermute | solution.py:255
  35.7 0.8 collective-permute-start.2
  36.5 0.5 collective-permute-start.1
  37.0 0.2 collective-permute-done.7.refs_8_
  37.2 4.3 %collective-permute-start = (bf16[8,144,256]{2,1,0:T(8,128)(2,1)S(1)}, bf16[8,144,256]{2,1,0:T(8,128)(2,1)S(1)}, u32[]{:S(2)}, u32[]{:S(2)}) collective-permute-start(bf16[8,144,256]{2,1,0:T(8,128)(2,1)S(1)} %all-to-all-done), channel_id=1, source_target_pairs={{0,0},{4,8},{8,16},{12,24},{16,4},{20,12},{24,20},{28,28},{1,1},{5... | collective-permute-start | bytes 1769480 | tf_op jit(solution)/shard_map/ppermute | solution.py:255
  41.5 1.5 %collective-permute-done.8.refs_9_ = bf16[2,2,128,256]{3,2,1,0:T(8,128)(2,1)S(1)} collective-permute-done((bf16[2,2,128,256]{3,2,1,0:T(8,128)(2,1)}, bf16[2,2,128,256]{3,2,1,0:T(8,128)(2,1)S(1)}, u32[]{:S(2)}, u32[]{:S(2)}) %collective-permute-start.8) | collective-permute-done | bytes 262176 | tf_op jit(solution)/shard_map/ppermute | solution.py:250
  43.0 1.3 %collective-permute-start.9 = (bf16[2,2,128,256]{3,2,1,0:T(8,128)(2,1)}, bf16[2,2,128,256]{3,2,1,0:T(8,128)(2,1)S(1)}, u32[]{:S(2)}, u32[]{:S(2)}) collective-permute-start(bf16[2,2,128,256]{3,2,1,0:T(8,128)(2,1)} %get-tuple-element.31), channel_id=1, source_target_pairs={{0,192},{4,196},{64,0},{68,4},{128,64},{132,68},{192,128},{196,132... | collective-permute-start | bytes 786440 | tf_op jit(solution)/shard_map/ppermute | solution.py:250
  44.3 6.6 %collective-permute-done.9.refs_10_ = bf16[2,2,128,256]{3,2,1,0:T(8,128)(2,1)S(1)} collective-permute-done((bf16[2,2,128,256]{3,2,1,0:T(8,128)(2,1)}, bf16[2,2,128,256]{3,2,1,0:T(8,128)(2,1)S(1)}, u32[]{:S(2)}, u32[]{:S(2)}) %collective-permute-start.9) | collective-permute-done | bytes 262176 | tf_op jit(solution)/shard_map/ppermute | solution.py:250
  50.9 1.6 %collective-permute-start.10 = (bf16[2,2,128,256]{3,2,1,0:T(8,128)(2,1)}, bf16[2,2,128,256]{3,2,1,0:T(8,128)(2,1)S(1)}, u32[]{:S(2)}, u32[]{:S(2)}) collective-permute-start(bf16[2,2,128,256]{3,2,1,0:T(8,128)(2,1)} %get-tuple-element.32), channel_id=1, source_target_pairs={{0,196},{4,192},{64,4},{68,0},{128,68},{132,64},{192,132},{196,128... | collective-permute-start | bytes 786440 | tf_op jit(solution)/shard_map/ppermute | solution.py:250
  52.5 7.2 %collective-permute-done.10.refs_11_ = bf16[2,2,128,256]{3,2,1,0:T(8,128)(2,1)S(1)} collective-permute-done((bf16[2,2,128,256]{3,2,1,0:T(8,128)(2,1)}, bf16[2,2,128,256]{3,2,1,0:T(8,128)(2,1)S(1)}, u32[]{:S(2)}, u32[]{:S(2)}) %collective-permute-start.10) | collective-permute-done | bytes 262176 | tf_op jit(solution)/shard_map/ppermute | solution.py:250
  59.7 2.1 %collective-permute-done.2.refs_2_ = bf16[8,144,256]{2,1,0:T(8,128)(2,1)S(1)} collective-permute-done((bf16[8,144,256]{2,1,0:T(8,128)(2,1)S(1)}, bf16[8,144,256]{2,1,0:T(8,128)(2,1)S(1)}, u32[]{:S(2)}, u32[]{:S(2)}) %collective-permute-start.2) | collective-permute-done | bytes 589856 | tf_op jit(solution)/shard_map/ppermute | solution.py:255
  61.8 0.7 collective-permute-done.1.refs_1_
  62.5 0.3 collective-permute-done.refs_0_
  62.7 0.9 copy-done.1
  63.7 7.3 %attention.1 = (bf16[2,2,128,256]{3,2,1,0:T(8,128)(2,1)S(1)}, bf16[2,2,128,256]{3,2,1,0:T(8,128)(2,1)S(1)}, bf16[2,2,128,256]{3,2,1,0:T(8,128)(2,1)S(1)}, bf16[2...) custom-call(bf16[8,144,256]{2,1,0:T(8,128)(2,1)S(1)} %collective-per, ...), custom_call_target="tpu_custom_call" | custom-call | flops 5368709120 | bytes 8388608 | tf_op jit(solution)/shard_map/attention/pallas_call | solution.py:220
  71.0 0.7 copy-done
  71.7 4.1 %collective-permute-start.11 = (bf16[8,64,256]{2,1,0:T(8,128)(2,1)S(1)}, bf16[8,64,256]{2,1,0:T(8,128)(2,1)S(1)}, u32[]{:S(2)}, u32[]{:S(2)}) collective-permute-start(bf16[8,64,256]{2,1,0:T(8,128)(2,1)S(1)} %get-tuple-element.33), channel_id=1, source_target_pairs={{0,0},{8,4},{16,8},{24,12},{4,16},{12,20},{20,24},{28,28},{1,1},{9... | collective-permute-start | bytes 786440 | tf_op jit(solution)/shard_map/ppermute | solution.py:258
  75.9 1.8 %collective-permute-start.12 = (bf16[8,64,256]{2,1,0:T(8,128)(2,1)S(1)}, bf16[8,64,256]{2,1,0:T(8,128)(2,1)S(1)}, u32[]{:S(2)}, u32[]{:S(2)}) collective-permute-start(bf16[8,64,256]{2,1,0:T(8,128)(2,1)S(1)} %get-tuple-element.34), channel_id=1, source_target_pairs={{8,0},{0,4},{24,8},{16,12},{12,16},{4,20},{28,24},{20,28},{9,1},{1... | collective-permute-start | bytes 786440 | tf_op jit(solution)/shard_map/ppermute | solution.py:258
  77.6 0.5 collective-permute-start.13
  78.1 1.9 %collective-permute-start.14 = (bf16[8,64,256]{2,1,0:T(8,128)(2,1)S(1)}, bf16[8,64,256]{2,1,0:T(8,128)(2,1)S(1)}, u32[]{:S(2)}, u32[]{:S(2)}) collective-permute-start(bf16[8,64,256]{2,1,0:T(8,128)(2,1)S(1)} %get-tuple-element.36), channel_id=1, source_target_pairs={{24,0},{16,4},{8,8},{0,12},{28,16},{20,20},{12,24},{4,28},{25,1},{... | collective-permute-start | bytes 786440 | tf_op jit(solution)/shard_map/ppermute | solution.py:258
  80.1 0.1 collective-permute-start.15
  80.2 1.0 collective-permute-done.11
  81.2 2.7 %collective-permute-start.16 = (bf16[2,2,128,256]{3,2,1,0:T(8,128)(2,1)S(1)}, bf16[2,2,128,256]{3,2,1,0:T(8,128)(2,1)S(1)}, u32[]{:S(2)}, u32[]{:S(2)}) collective-permute-start(bf16[2,2,128,256]{3,2,1,0:T(8,128)(2,1)S(1)} %get-tuple-element.39), channel_id=1, source_target_pairs={{64,0},{68,4},{128,64},{132,68},{192,128},{196,132},{0,192},{4,196... | collective-permute-start | bytes 786440 | tf_op jit(solution)/shard_map/ppermute | solution.py:263
  83.9 2.9 %collective-permute-done.12 = bf16[8,64,256]{2,1,0:T(8,128)(2,1)S(1)} collective-permute-done((bf16[8,64,256]{2,1,0:T(8,128)(2,1)S(1)}, bf16[8,64,256]{2,1,0:T(8,128)(2,1)S(1)}, u32[]{:S(2)}, u32[]{:S(2)}) %collective-permute-start.12) | collective-permute-done | bytes 262176 | tf_op jit(solution)/shard_map/ppermute | solution.py:258
  86.8 3.0 %collective-permute-done.13 = bf16[8,64,256]{2,1,0:T(8,128)(2,1)S(1)} collective-permute-done((bf16[8,64,256]{2,1,0:T(8,128)(2,1)S(1)}, bf16[8,64,256]{2,1,0:T(8,128)(2,1)S(1)}, u32[]{:S(2)}, u32[]{:S(2)}) %collective-permute-start.13) | collective-permute-done | bytes 262176 | tf_op jit(solution)/shard_map/ppermute | solution.py:258
  89.8 0.0 collective-permute-done.14
  89.8 0.8 add_convert_fusion
  90.6 5.5 %all-to-all-start.1 = ((bf16[8,64,256]{2,1,0:T(8,128)(2,1)}), bf16[8,64,256]{2,1,0:T(8,128)(2,1)S(1)}, u32[]{:S(2)}, u32[]{:S(2)}) async-start(bf16[8,64,256]{2,1,0:T(8,128)(2,1)} %add_convert_fusion), calls=%async_computation.1 | async-start | bytes 524288 | tf_op jit(solution)/shard_map/all_to_all | solution.py:266
  96.1 5.6 %collective-permute-start.17 = (bf16[2,2,128,256]{3,2,1,0:T(8,128)(2,1)S(1)}, bf16[2,2,128,256]{3,2,1,0:T(8,128)(2,1)S(1)}, u32[]{:S(2)}, u32[]{:S(2)}) collective-permute-start(bf16[2,2,128,256]{3,2,1,0:T(8,128)(2,1)S(1)} %get-tuple-element.40), channel_id=1, source_target_pairs={{68,0},{64,4},{132,64},{128,68},{196,128},{192,132},{4,192},{0,196... | collective-permute-start | bytes 786440 | tf_op jit(solution)/shard_map/ppermute | solution.py:263
  101.7 1.0 collective-permute-start.19
  102.7 0.1 collective-permute-start.20
  102.8 2.2 %collective-permute-start.21 = (bf16[2,2,128,256]{3,2,1,0:T(8,128)(2,1)S(1)}, bf16[2,2,128,256]{3,2,1,0:T(8,128)(2,1)S(1)}, u32[]{:S(2)}, u32[]{:S(2)}) collective-permute-start(bf16[2,2,128,256]{3,2,1,0:T(8,128)(2,1)S(1)} %get-tuple-element.44), channel_id=1, source_target_pairs={{196,0},{192,4},{4,64},{0,68},{68,128},{64,132},{132,192},{128,196... | collective-permute-start | bytes 786440 | tf_op jit(solution)/shard_map/ppermute | solution.py:263
  105.0 12.1 %collective-permute-done.17.refs_3_ = bf16[2,2,128,256]{3,2,1,0:T(8,128)(2,1)S(1)} collective-permute-done((bf16[2,2,128,256]{3,2,1,0:T(8,128)(2,1)S(1)}, bf16[2,2,128,256]{3,2,1,0:T(8,128)(2,1)S(1)}, u32[]{:S(2)}, u32[]{:S(2)}) %collective-permute-start.17) | collective-permute-done | bytes 262176 | tf_op jit(solution)/shard_map/ppermute | solution.py:263
  117.2 3.9 %collective-permute-done.20.refs_6_ = bf16[2,2,128,256]{3,2,1,0:T(8,128)(2,1)S(1)} collective-permute-done((bf16[2,2,128,256]{3,2,1,0:T(8,128)(2,1)S(1)}, bf16[2,2,128,256]{3,2,1,0:T(8,128)(2,1)S(1)}, u32[]{:S(2)}, u32[]{:S(2)}) %collective-permute-start.20) | collective-permute-done | bytes 262176 | tf_op jit(solution)/shard_map/ppermute | solution.py:263
  121.0 5.6 %collective-permute-done.21.refs_7_ = bf16[2,2,128,256]{3,2,1,0:T(8,128)(2,1)S(1)} collective-permute-done((bf16[2,2,128,256]{3,2,1,0:T(8,128)(2,1)S(1)}, bf16[2,2,128,256]{3,2,1,0:T(8,128)(2,1)S(1)}, u32[]{:S(2)}, u32[]{:S(2)}) %collective-permute-start.21) | collective-permute-done | bytes 262176 | tf_op jit(solution)/shard_map/ppermute | solution.py:263
  126.7 0.7 copy-done.8
  127.3 3.1 %join.1 = (bf16[128,4096]{1,0:T(8,128)(2,1)}, bf16[128,4096]{1,0:T(8,128)(2,1)}) custom-call(bf16[2,2,128,256]{3,2,1,0:T(8,128)(2,1)} %copy-done, bf16[2,2,128,256]{3,2,1,0:T(8,128)(2,1)} %copy-done.2, bf16[2,2,128,256]{3,2,1,0:T(8,128)(2,1)} %copy-done.3, bf16[2,2,128,256]{3,2,1,0:T(8,128)(2,1)} %copy-done.4, bf16[2,2,128,256]{3,2,1,0:T(8,128)(2,1)} %copy-done.5, ...), custom_call_target="tpu_custom_call" | custom-call | tf_op jit(solution)/shard_map/join/pallas_call | solution.py:136
  130.5 0.7 reduce_sum.12
  (24 shorter events, 0.1 us)
Async XLA Ops:
  2.3 28.4 %all-to-all-start = ((bf16[8,144,256]{2,1,0:T(8,128)(2,1)}), bf16[8,144,256]{2,1,0:T(8,128)(2,1)S(1)}, u32[]{:S(2)}, u32[]{:S(2)}) async-start(bf16[8,144,256]{2,1,0:T(8,128)(2,1)} %message.1), calls=%async_computation | async-start | bytes 1179648 | tf_op jit(solution)/shard_map/all_to_all | solution.py:254
  14.4 7.2 %collective-permute-start.4 = (bf16[2,2,128,256]{3,2,1,0:T(8,128)(2,1)}, bf16[2,2,128,256]{3,2,1,0:T(8,128)(2,1)S(1)}, u32[]{:S(2)}, u32[]{:S(2)}) collective-permute-start(bf16[2,2,128,256]{3,2,1,0:T(8,128)(2,1)} %get-tuple-element.26), channel_id=1, source_target_pairs={{0,4},{4,0},{64,68},{68,64},{128,132},{132,128},{192,196},{196,192... | collective-permute-start | bytes 786440 | tf_op jit(solution)/shard_map/ppermute | solution.py:250
  15.4 20.2 %collective-permute-start.5 = (bf16[2,2,128,256]{3,2,1,0:T(8,128)(2,1)}, bf16[2,2,128,256]{3,2,1,0:T(8,128)(2,1)S(1)}, u32[]{:S(2)}, u32[]{:S(2)}) collective-permute-start(bf16[2,2,128,256]{3,2,1,0:T(8,128)(2,1)} %get-tuple-element.27), channel_id=1, source_target_pairs={{0,64},{4,68},{64,128},{68,132},{128,192},{132,196},{192,0},{196,4... | collective-permute-start | bytes 786440 | tf_op jit(solution)/shard_map/ppermute | solution.py:250
  16.8 19.8 %collective-permute-start.6 = (bf16[2,2,128,256]{3,2,1,0:T(8,128)(2,1)}, bf16[2,2,128,256]{3,2,1,0:T(8,128)(2,1)S(1)}, u32[]{:S(2)}, u32[]{:S(2)}) collective-permute-start(bf16[2,2,128,256]{3,2,1,0:T(8,128)(2,1)} %get-tuple-element.28), channel_id=1, source_target_pairs={{0,68},{4,64},{64,132},{68,128},{128,196},{132,192},{192,4},{196,0... | collective-permute-start | bytes 786440 | tf_op jit(solution)/shard_map/ppermute | solution.py:250
  18.3 18.9 %collective-permute-start.7 = (bf16[2,2,128,256]{3,2,1,0:T(8,128)(2,1)}, bf16[2,2,128,256]{3,2,1,0:T(8,128)(2,1)S(1)}, u32[]{:S(2)}, u32[]{:S(2)}) collective-permute-start(bf16[2,2,128,256]{3,2,1,0:T(8,128)(2,1)} %get-tuple-element.29), channel_id=1, source_target_pairs={{0,128},{4,132},{64,192},{68,196},{128,0},{132,4},{192,64},{196,68... | collective-permute-start | bytes 786440 | tf_op jit(solution)/shard_map/ppermute | solution.py:250
  19.6 23.4 %collective-permute-start.8 = (bf16[2,2,128,256]{3,2,1,0:T(8,128)(2,1)}, bf16[2,2,128,256]{3,2,1,0:T(8,128)(2,1)S(1)}, u32[]{:S(2)}, u32[]{:S(2)}) collective-permute-start(bf16[2,2,128,256]{3,2,1,0:T(8,128)(2,1)} %get-tuple-element.30), channel_id=1, source_target_pairs={{0,132},{4,128},{64,196},{68,192},{128,4},{132,0},{192,68},{196,64... | collective-permute-start | bytes 786440 | tf_op jit(solution)/shard_map/ppermute | solution.py:250
  30.7 29.0 %collective-permute-start.3 = (bf16[8,144,256]{2,1,0:T(8,128)(2,1)S(1)}, bf16[8,144,256]{2,1,0:T(8,128)(2,1)S(1)}, u32[]{:S(2)}, u32[]{:S(2)}) collective-permute-start(bf16[8,144,256]{2,1,0:T(8,128)(2,1)S(1)} %all-to-all-done), channel_id=1, source_target_pairs={{0,24},{4,16},{8,8},{12,0},{16,28},{20,20},{24,12},{28,4},{1,25},{... | collective-permute-start | bytes 1769480 | tf_op jit(solution)/shard_map/ppermute | solution.py:255
  35.7 26.1 %collective-permute-start.2 = (bf16[8,144,256]{2,1,0:T(8,128)(2,1)S(1)}, bf16[8,144,256]{2,1,0:T(8,128)(2,1)S(1)}, u32[]{:S(2)}, u32[]{:S(2)}) collective-permute-start(bf16[8,144,256]{2,1,0:T(8,128)(2,1)S(1)} %all-to-all-done), channel_id=1, source_target_pairs={{0,16},{4,24},{8,0},{12,8},{16,20},{20,28},{24,4},{28,12},{1,17},{... | collective-permute-start | bytes 1769480 | tf_op jit(solution)/shard_map/ppermute | solution.py:255
  36.5 25.9 %collective-permute-start.1 = (bf16[8,144,256]{2,1,0:T(8,128)(2,1)S(1)}, bf16[8,144,256]{2,1,0:T(8,128)(2,1)S(1)}, u32[]{:S(2)}, u32[]{:S(2)}) collective-permute-start(bf16[8,144,256]{2,1,0:T(8,128)(2,1)S(1)} %all-to-all-done), channel_id=1, source_target_pairs={{0,8},{4,0},{8,24},{12,16},{16,12},{20,4},{24,28},{28,20},{1,9},{5... | collective-permute-start | bytes 1769480 | tf_op jit(solution)/shard_map/ppermute | solution.py:255
  37.2 25.5 %collective-permute-start = (bf16[8,144,256]{2,1,0:T(8,128)(2,1)S(1)}, bf16[8,144,256]{2,1,0:T(8,128)(2,1)S(1)}, u32[]{:S(2)}, u32[]{:S(2)}) collective-permute-start(bf16[8,144,256]{2,1,0:T(8,128)(2,1)S(1)} %all-to-all-done), channel_id=1, source_target_pairs={{0,0},{4,8},{8,16},{12,24},{16,4},{20,12},{24,20},{28,28},{1,1},{5... | collective-permute-start | bytes 1769480 | tf_op jit(solution)/shard_map/ppermute | solution.py:255
  43.0 7.9 %collective-permute-start.9 = (bf16[2,2,128,256]{3,2,1,0:T(8,128)(2,1)}, bf16[2,2,128,256]{3,2,1,0:T(8,128)(2,1)S(1)}, u32[]{:S(2)}, u32[]{:S(2)}) collective-permute-start(bf16[2,2,128,256]{3,2,1,0:T(8,128)(2,1)} %get-tuple-element.31), channel_id=1, source_target_pairs={{0,192},{4,196},{64,0},{68,4},{128,64},{132,68},{192,128},{196,132... | collective-permute-start | bytes 786440 | tf_op jit(solution)/shard_map/ppermute | solution.py:250
  50.9 8.8 %collective-permute-start.10 = (bf16[2,2,128,256]{3,2,1,0:T(8,128)(2,1)}, bf16[2,2,128,256]{3,2,1,0:T(8,128)(2,1)S(1)}, u32[]{:S(2)}, u32[]{:S(2)}) collective-permute-start(bf16[2,2,128,256]{3,2,1,0:T(8,128)(2,1)} %get-tuple-element.32), channel_id=1, source_target_pairs={{0,196},{4,192},{64,4},{68,0},{128,68},{132,64},{192,132},{196,128... | collective-permute-start | bytes 786440 | tf_op jit(solution)/shard_map/ppermute | solution.py:250
  62.7 1.0 copy-start.1
  71.0 0.7 copy-start
  71.7 9.5 %collective-permute-start.11 = (bf16[8,64,256]{2,1,0:T(8,128)(2,1)S(1)}, bf16[8,64,256]{2,1,0:T(8,128)(2,1)S(1)}, u32[]{:S(2)}, u32[]{:S(2)}) collective-permute-start(bf16[8,64,256]{2,1,0:T(8,128)(2,1)S(1)} %get-tuple-element.33), channel_id=1, source_target_pairs={{0,0},{8,4},{16,8},{24,12},{4,16},{12,20},{20,24},{28,28},{1,1},{9... | collective-permute-start | bytes 786440 | tf_op jit(solution)/shard_map/ppermute | solution.py:258
  75.9 11.0 %collective-permute-start.12 = (bf16[8,64,256]{2,1,0:T(8,128)(2,1)S(1)}, bf16[8,64,256]{2,1,0:T(8,128)(2,1)S(1)}, u32[]{:S(2)}, u32[]{:S(2)}) collective-permute-start(bf16[8,64,256]{2,1,0:T(8,128)(2,1)S(1)} %get-tuple-element.34), channel_id=1, source_target_pairs={{8,0},{0,4},{24,8},{16,12},{12,16},{4,20},{28,24},{20,28},{9,1},{1... | collective-permute-start | bytes 786440 | tf_op jit(solution)/shard_map/ppermute | solution.py:258
  77.6 12.2 %collective-permute-start.13 = (bf16[8,64,256]{2,1,0:T(8,128)(2,1)S(1)}, bf16[8,64,256]{2,1,0:T(8,128)(2,1)S(1)}, u32[]{:S(2)}, u32[]{:S(2)}) collective-permute-start(bf16[8,64,256]{2,1,0:T(8,128)(2,1)S(1)} %get-tuple-element.35), channel_id=1, source_target_pairs={{16,0},{24,4},{0,8},{8,12},{20,16},{28,20},{4,24},{12,28},{17,1},{... | collective-permute-start | bytes 786440 | tf_op jit(solution)/shard_map/ppermute | solution.py:258
  78.1 11.7 %collective-permute-start.14 = (bf16[8,64,256]{2,1,0:T(8,128)(2,1)S(1)}, bf16[8,64,256]{2,1,0:T(8,128)(2,1)S(1)}, u32[]{:S(2)}, u32[]{:S(2)}) collective-permute-start(bf16[8,64,256]{2,1,0:T(8,128)(2,1)S(1)} %get-tuple-element.36), channel_id=1, source_target_pairs={{24,0},{16,4},{8,8},{0,12},{28,16},{20,20},{12,24},{4,28},{25,1},{... | collective-permute-start | bytes 786440 | tf_op jit(solution)/shard_map/ppermute | solution.py:258
  80.1 22.7 %collective-permute-start.15 = (bf16[2,2,128,256]{3,2,1,0:T(8,128)(2,1)S(1)}, bf16[2,2,128,256]{3,2,1,0:T(8,128)(2,1)S(1)}, u32[]{:S(2)}, u32[]{:S(2)}) collective-permute-start(bf16[2,2,128,256]{3,2,1,0:T(8,128)(2,1)S(1)} %get-tuple-element.38), channel_id=1, source_target_pairs={{4,0},{0,4},{68,64},{64,68},{132,128},{128,132},{196,192},{192,196... | collective-permute-start | bytes 786440 | tf_op jit(solution)/shard_map/ppermute | solution.py:263
  81.2 21.6 %collective-permute-start.16 = (bf16[2,2,128,256]{3,2,1,0:T(8,128)(2,1)S(1)}, bf16[2,2,128,256]{3,2,1,0:T(8,128)(2,1)S(1)}, u32[]{:S(2)}, u32[]{:S(2)}) collective-permute-start(bf16[2,2,128,256]{3,2,1,0:T(8,128)(2,1)S(1)} %get-tuple-element.39), channel_id=1, source_target_pairs={{64,0},{68,4},{128,64},{132,68},{192,128},{196,132},{0,192},{4,196... | collective-permute-start | bytes 786440 | tf_op jit(solution)/shard_map/ppermute | solution.py:263
  90.6 39.9 %all-to-all-start.1 = ((bf16[8,64,256]{2,1,0:T(8,128)(2,1)}), bf16[8,64,256]{2,1,0:T(8,128)(2,1)S(1)}, u32[]{:S(2)}, u32[]{:S(2)}) async-start(bf16[8,64,256]{2,1,0:T(8,128)(2,1)} %add_convert_fusion), calls=%async_computation.1 | async-start | bytes 524288 | tf_op jit(solution)/shard_map/all_to_all | solution.py:266
  96.1 21.0 %collective-permute-start.17 = (bf16[2,2,128,256]{3,2,1,0:T(8,128)(2,1)S(1)}, bf16[2,2,128,256]{3,2,1,0:T(8,128)(2,1)S(1)}, u32[]{:S(2)}, u32[]{:S(2)}) collective-permute-start(bf16[2,2,128,256]{3,2,1,0:T(8,128)(2,1)S(1)} %get-tuple-element.40), channel_id=1, source_target_pairs={{68,0},{64,4},{132,64},{128,68},{196,128},{192,132},{4,192},{0,196... | collective-permute-start | bytes 786440 | tf_op jit(solution)/shard_map/ppermute | solution.py:263
  101.7 15.4 %collective-permute-start.18 = (bf16[2,2,128,256]{3,2,1,0:T(8,128)(2,1)S(1)}, bf16[2,2,128,256]{3,2,1,0:T(8,128)(2,1)S(1)}, u32[]{:S(2)}, u32[]{:S(2)}) collective-permute-start(bf16[2,2,128,256]{3,2,1,0:T(8,128)(2,1)S(1)} %get-tuple-element.41), channel_id=1, source_target_pairs={{128,0},{132,4},{192,64},{196,68},{0,128},{4,132},{64,192},{68,196... | collective-permute-start | bytes 786440 | tf_op jit(solution)/shard_map/ppermute | solution.py:263
  101.7 15.4 %collective-permute-start.19 = (bf16[2,2,128,256]{3,2,1,0:T(8,128)(2,1)S(1)}, bf16[2,2,128,256]{3,2,1,0:T(8,128)(2,1)S(1)}, u32[]{:S(2)}, u32[]{:S(2)}) collective-permute-start(bf16[2,2,128,256]{3,2,1,0:T(8,128)(2,1)S(1)} %get-tuple-element.42), channel_id=1, source_target_pairs={{132,0},{128,4},{196,64},{192,68},{4,128},{0,132},{68,192},{64,196... | collective-permute-start | bytes 786440 | tf_op jit(solution)/shard_map/ppermute | solution.py:263
  102.7 23.9 %copy-start.2 = (bf16[2,2,128,256]{3,2,1,0:T(8,128)(2,1)}, bf16[2,2,128,256]{3,2,1,0:T(8,128)(2,1)S(1)}, u32[]{:S(2)}) copy-start(bf16[2,2,128,256]{3,2,1,0:T(8,128)(2,1)S(1)} %collective-permute-done.15.refs_1_) | copy-start | bytes 786436
  102.7 18.3 %collective-permute-start.20 = (bf16[2,2,128,256]{3,2,1,0:T(8,128)(2,1)S(1)}, bf16[2,2,128,256]{3,2,1,0:T(8,128)(2,1)S(1)}, u32[]{:S(2)}, u32[]{:S(2)}) collective-permute-start(bf16[2,2,128,256]{3,2,1,0:T(8,128)(2,1)S(1)} %get-tuple-element.43), channel_id=1, source_target_pairs={{192,0},{196,4},{0,64},{4,68},{64,128},{68,132},{128,192},{132,196... | collective-permute-start | bytes 786440 | tf_op jit(solution)/shard_map/ppermute | solution.py:263
  102.8 23.9 %copy-start.3 = (bf16[2,2,128,256]{3,2,1,0:T(8,128)(2,1)}, bf16[2,2,128,256]{3,2,1,0:T(8,128)(2,1)S(1)}, u32[]{:S(2)}) copy-start(bf16[2,2,128,256]{3,2,1,0:T(8,128)(2,1)S(1)} %collective-permute-done.16.refs_2_) | copy-start | bytes 786436
  102.8 23.8 %collective-permute-start.21 = (bf16[2,2,128,256]{3,2,1,0:T(8,128)(2,1)S(1)}, bf16[2,2,128,256]{3,2,1,0:T(8,128)(2,1)S(1)}, u32[]{:S(2)}, u32[]{:S(2)}) collective-permute-start(bf16[2,2,128,256]{3,2,1,0:T(8,128)(2,1)S(1)} %get-tuple-element.44), channel_id=1, source_target_pairs={{196,0},{192,4},{4,64},{0,68},{68,128},{64,132},{132,192},{128,196... | collective-permute-start | bytes 786440 | tf_op jit(solution)/shard_map/ppermute | solution.py:263
  117.1 9.5 %copy-start.4 = (bf16[2,2,128,256]{3,2,1,0:T(8,128)(2,1)}, bf16[2,2,128,256]{3,2,1,0:T(8,128)(2,1)S(1)}, u32[]{:S(2)}) copy-start(bf16[2,2,128,256]{3,2,1,0:T(8,128)(2,1)S(1)} %collective-permute-done.17.refs_3_) | copy-start | bytes 786436
  117.1 9.5 %copy-start.5 = (bf16[2,2,128,256]{3,2,1,0:T(8,128)(2,1)}, bf16[2,2,128,256]{3,2,1,0:T(8,128)(2,1)S(1)}, u32[]{:S(2)}) copy-start(bf16[2,2,128,256]{3,2,1,0:T(8,128)(2,1)S(1)} %collective-permute-done.18.refs_4_) | copy-start | bytes 786436
  117.2 9.5 %copy-start.6 = (bf16[2,2,128,256]{3,2,1,0:T(8,128)(2,1)}, bf16[2,2,128,256]{3,2,1,0:T(8,128)(2,1)S(1)}, u32[]{:S(2)}) copy-start(bf16[2,2,128,256]{3,2,1,0:T(8,128)(2,1)S(1)} %collective-permute-done.19.refs_5_) | copy-start | bytes 786436
  121.0 5.7 %copy-start.7 = (bf16[2,2,128,256]{3,2,1,0:T(8,128)(2,1)}, bf16[2,2,128,256]{3,2,1,0:T(8,128)(2,1)S(1)}, u32[]{:S(2)}) copy-start(bf16[2,2,128,256]{3,2,1,0:T(8,128)(2,1)S(1)} %collective-permute-done.20.refs_6_) | copy-start | bytes 786436
  126.6 0.7 copy-start.8

commit v3 on v0

v3 whole, which is shorter than its diff:
```python
import jax
import jax.numpy as jnp
from jax import lax
from jax.experimental import pallas as pl
from jax.experimental.pallas import tpu as pltpu
from jax.sharding import Mesh, PartitionSpec as P

AXES = ("y", "zh", "x", "core", "zl")
SIZES = (4, 2, 4, 2, 4)
MEM = ("y", "zh", "x", "core")
OWNERS = ("y", "x")
HEADS = 16
DH = 256
ROWS = 256
PART = 64
KEYS = 128
STAT = 16
FACTOR = DH**-0.5
LOG2E = 1.4426950408889634
MIB = 1024 * 1024
BF16, F32 = jnp.bfloat16, jnp.float32
HBM = pl.BlockSpec(memory_space=pltpu.HBM)
VMEM = pl.BlockSpec(memory_space=pltpu.VMEM)


def call(kernel, outs, ins, out_specs, limit, name, scratch=(), cost=None):
    return pl.pallas_call(
        kernel,
        out_shape=outs,
        in_specs=ins,
        out_specs=out_specs,
        scratch_shapes=list(scratch),
        compiler_params=pltpu.CompilerParams(vmem_limit_bytes=limit * MIB),
        cost_estimate=cost,
        name=name,
    )


def shape(*dims, dtype=BF16):
    return jax.ShapeDtypeStruct(dims, dtype)


def pair_of(zh, x):
    return zh * 4 + x


CROSS = [
    (pair_of(zh, x), pair_of(zh, x - 1) if x % 2 else pair_of(1 - zh, x + 1))
    for zh in range(2)
    for x in range(4)
]
STRAIGHT = [
    (pair_of(zh, x), pair_of(1 - zh, x) if x % 2 else pair_of(zh, x))
    for zh in range(2)
    for x in range(4)
]
SWAP = [(0, 1), (1, 0)]


def inverse(pairs):
    return [(b, a) for a, b in pairs]


def turn(step):
    return [(i, (i + step) % 4) for i in range(4)]


def pieces(value):
    high = value.astype(BF16)
    rest = value - high.astype(F32)
    middle = rest.astype(BF16)
    low = (rest - middle.astype(F32)).astype(BF16)
    return [high.astype(F32), middle.astype(F32), low.astype(F32)]


def in_hbm(array):
    return pltpu.with_memory_space_constraint(array, pltpu.HBM)


def stat_rows(rows):
    pad = jnp.zeros((STAT - 6, ROWS), F32)
    return jnp.concatenate(rows + [pad], axis=0).astype(BF16)


def message_kernel(*refs):
    message, scratch, sem = refs[4], refs[5:9], refs[9]
    copies = [
        pltpu.make_async_copy(refs[i], scratch[i], sem.at[i]) for i in range(4)
    ]
    for copy in copies:
        copy.start()
    for copy in copies:
        copy.wait()
    queries, outputs, cotangent, log_norms = scratch
    sums = jnp.sum(
        cotangent[...].astype(F32) * outputs[...].astype(F32), axis=0, keepdims=True
    )
    zh, x, y = lax.axis_index("zh"), lax.axis_index("x"), lax.axis_index("y")
    head = 4 * y + 2 * zh + x // 2
    mine = lax.broadcasted_iota(jnp.int32, (HEADS, ROWS), 0) == head
    norms = jnp.sum(jnp.where(mine, log_norms[...], 0.0), axis=0, keepdims=True)
    message[:PART, :] = queries[...]
    message[PART : 2 * PART, :] = cotangent[...]
    message[2 * PART :, :] = stat_rows(pieces(sums) + pieces(norms))


def make_message(*args):
    return call(
        message_kernel,
        shape(2 * PART + STAT, ROWS),
        [HBM] * 4,
        VMEM,
        4,
        "message",
        [pltpu.VMEM(a.shape, a.dtype) for a in args] + [pltpu.SemaphoreType.DMA((4,))],
    )(*map(in_hbm, args))


def bundle_kernel(cross, straight, out):
    odd = lax.rem(lax.axis_index("x"), 2)
    for ref, place in ((cross, 1 - odd), (straight, odd)):
        start = pl.multiple_of(place * PART, PART)
        out[pl.ds(start, PART), :] = ref[:PART, :]
        out[pl.ds(start + 2 * PART, PART), :] = ref[PART : 2 * PART, :]
    one, two = cross[2 * PART :, :].astype(F32), straight[2 * PART :, :].astype(F32)
    both = one + two
    rows = pieces(both[0:1] + both[1:2] + both[2:3])
    out[4 * PART :, :] = stat_rows(rows + [one[3:6]])


def bundle(*args):
    return call(
        bundle_kernel, shape(4 * PART + STAT, ROWS), [VMEM] * 2, VMEM, 4, "bundle"
    )(*args)


def stack_kernel(*refs):
    for i, ref in enumerate(refs[:-1]):
        refs[-1][i] = ref[...]


def stack(parts):
    out = shape(len(parts), *parts[0].shape)
    return call(stack_kernel, out, [VMEM] * len(parts), VMEM, 8, "stack")(*parts)


def slot_columns(s):
    y, x = s // 4, s % 4
    zh = lax.axis_index("zh")
    if x % 2:
        zh = 1 - zh
    return pl.ds(pl.multiple_of((4 * y + 2 * zh + x // 2) * DH, DH), DH)


def split_kernel(keys, values, out, held, in_sem, out_sem):
    pieces = [(s, a) for s in range(16) for a in range(2)]
    reads, writes = [], []
    for s, a in pieces:
        array = (keys, values)[a]
        at = held.at[s, a]
        number = 2 * s + a
        reads.append(
            pltpu.make_async_copy(array.at[:, slot_columns(s)], at, in_sem.at[number])
        )
        writes.append(pltpu.make_async_copy(at, out.at[s, a], out_sem.at[number]))
    for copy in reads:
        copy.start()
    for read, write in zip(reads, writes):
        read.wait()
        write.start()
    for copy in writes:
        copy.wait()


def split(keys, values):
    return call(
        split_kernel,
        pltpu.HBM((16, 2, KEYS, DH), BF16),
        [HBM] * 2,
        HBM,
        8,
        "split",
        [
            pltpu.VMEM((16, 2, KEYS, DH), BF16),
            pltpu.SemaphoreType.DMA((32,)),
            pltpu.SemaphoreType.DMA((32,)),
        ],
        pl.CostEstimate(flops=0, bytes_accessed=8 * MIB, transcendentals=0),
    )(in_hbm(keys), in_hbm(values))


def join_kernel(chunks, keys, values):
    for s in range(16):
        columns = slot_columns(s)
        keys[:, columns] = chunks[s, 0]
        values[:, columns] = chunks[s, 1]


def join(chunks):
    out = shape(KEYS, HEADS * DH)
    return call(join_kernel, [out] * 2, [VMEM], [VMEM] * 2, 8, "join")(chunks)


def dot(a, b, ca, cb):
    return lax.dot_general(a, b, (((ca,), (cb,)), ((), ())), preferred_element_type=F32)


def attention_kernel(
    mine, there, kv, grads, own, other, theirs, qt, dt, stat, dkv, dq, ds, sem
):
    core, here = lax.axis_index("core"), lax.axis_index("zl")
    copy = pltpu.make_async_copy(there, theirs, sem.at[0])
    copy.start()
    copy.wait()
    for d in range(4):
        zl = lax.rem(here + 4 - d, 4)
        for ref, c in ((mine, core), (theirs, 1 - core)):
            for xl in range(2):
                to = pl.ds(pl.multiple_of((2 * xl + c) * PART, PART), PART)
                qt[zl, to, :] = ref[d, xl * PART : (xl + 1) * PART, :]
                dt[zl, to, :] = ref[d, (2 + xl) * PART : (3 + xl) * PART, :]
        one = mine[d, 4 * PART :, :].astype(F32)
        both = one + theirs[d, 4 * PART :, :].astype(F32)
        stat[zl, 0:1, :] = both[0:1] + both[1:2] + both[2:3]
        stat[zl, 1:2, :] = (one[3:4] + one[4:5] + one[5:6]) * LOG2E

    writes = []
    for block in range(8):
        rows = slice(block * 2 * KEYS, (block + 1) * 2 * KEYS)
        keys = kv[2 * block : 2 * block + 2, 0].reshape(2 * KEYS, DH)
        values = kv[2 * block : 2 * block + 2, 1].reshape(2 * KEYS, DH)
        weights, slopes = [], []
        for zl in range(4):
            score = dot(keys, qt[zl], 1, 0)
            weight = jnp.exp2(score * (FACTOR * LOG2E) - stat[zl, 1:2, :])
            slope = dot(values, dt[zl], 1, 0)
            grad = (weight * (slope - stat[zl, 0:1, :])).astype(BF16)
            weights.append(weight.astype(BF16))
            slopes.append(grad)
            ds[zl, rows, :] = grad
        value_grad = sum(dot(weights[zl], dt[zl], 1, 1) for zl in range(4))
        key_grad = sum(dot(slopes[zl], qt[zl], 1, 1) for zl in range(4)) * FACTOR
        for half in range(2):
            part = slice(half * KEYS, (half + 1) * KEYS)
            dkv[2 * block + half, 0] = key_grad[part].astype(BF16)
            dkv[2 * block + half, 1] = value_grad[part].astype(BF16)
        pair = slice(2 * block, 2 * block + 2)
        copy = pltpu.make_async_copy(dkv.at[pair], grads.at[pair], sem.at[block])
        copy.start()
        writes.append(copy)
    keys = kv[:, 0].reshape(16 * KEYS, DH)
    for zl in range(4):
        dq[zl] = dot(keys, ds[zl], 0, 0) * FACTOR
    for d in range(4):
        zl = lax.rem(here + d, 4)
        for xl in range(2):
            at = pl.ds(pl.multiple_of((2 * xl + core) * PART, PART), PART)
            own[d, xl] = dq[zl, at, :]
            at = pl.ds(pl.multiple_of((2 * xl + 1 - core) * PART, PART), PART)
            other[d, xl] = dq[zl, at, :].astype(BF16)
    for copy in writes:
        copy.wait()


def attention(mine, theirs, kv):
    part = (4, 2, PART, ROWS)
    return call(
        attention_kernel,
        [pltpu.HBM((16, 2, KEYS, DH), BF16), shape(*part, dtype=F32), shape(*part)],
        [VMEM, HBM, VMEM],
        [HBM, VMEM, VMEM],
        32,
        "attention",
        [
            pltpu.VMEM((4, 4 * PART + STAT, ROWS), BF16),
            pltpu.VMEM((4, DH, ROWS), BF16),
            pltpu.VMEM((4, DH, ROWS), BF16),
            pltpu.VMEM((4, 8, ROWS), F32),
            pltpu.VMEM((16, 2, KEYS, DH), BF16),
            pltpu.VMEM((4, DH, ROWS), F32),
            pltpu.VMEM((4, 16 * KEYS, ROWS), BF16),
            pltpu.SemaphoreType.DMA((8,)),
        ],
        pl.CostEstimate(
            flops=5 * 2 * 2048 * 1024 * 256,
            bytes_accessed=8 * MIB,
            transcendentals=2048 * 1024,
        ),
    )(mine, in_hbm(theirs), kv)


def core_sum_kernel(own, other, *outs):
    for d, out in enumerate(outs):
        out[...] = (own[d] + other[d].astype(F32)).astype(BF16)


def core_sum(own, other):
    return call(
        core_sum_kernel,
        [shape(2, PART, ROWS)] * 4,
        [VMEM] * 2,
        [VMEM] * 4,
        4,
        "core_sum",
    )(own, other)


def line_sum_kernel(*refs):
    parts, cross, straight = refs[:4], refs[4], refs[5]
    odd = lax.rem(lax.axis_index("x"), 2)
    for out, place in ((cross, 1 - odd), (straight, odd)):
        total = parts[0][place].astype(F32)
        for part in parts[1:]:
            total = total + part[place].astype(F32)
        out[...] = total.astype(BF16)


def line_sum(parts):
    return call(
        line_sum_kernel, [shape(PART, ROWS)] * 2, [VMEM] * 4, [VMEM] * 2, 4, "line_sum"
    )(*parts)


def local(queries, outputs, cotangent, log_norms, memory_keys, memory_values):
    message = make_message(queries.T, outputs.T, cotangent.T, log_norms.T)
    cross = lax.ppermute(message, ("zh", "x"), CROSS)
    straight = lax.ppermute(message, ("zh", "x"), STRAIGHT)
    chunks = split(memory_keys, memory_values)
    chunks, cross, straight = lax.optimization_barrier((chunks, cross, straight))
    received = lax.all_to_all(chunks, OWNERS, split_axis=0, concat_axis=0, tiled=True)
    first = bundle(cross, straight)
    mine = stack([first] + [lax.ppermute(first, "zl", turn(d)) for d in (1, 2, 3)])
    theirs = lax.ppermute(mine, "core", SWAP)
    grads, own, other = attention(mine, theirs, received)
    returned = lax.all_to_all(grads, OWNERS, split_axis=0, concat_axis=0, tiled=True)
    sums = core_sum(own, lax.ppermute(other, "core", SWAP))
    parts = [sums[0]] + [lax.ppermute(sums[d], "zl", turn(d)) for d in (1, 2, 3)]
    cross, straight = line_sum(parts)
    cross = lax.ppermute(cross, ("zh", "x"), inverse(CROSS))
    straight = lax.ppermute(straight, ("zh", "x"), inverse(STRAIGHT))
    query_grads = (cross.astype(F32) + straight.astype(F32)).astype(BF16).T
    key_grads, value_grads = join(returned)
    return query_grads, key_grads, value_grads


def solution(mesh):
    fine = Mesh(mesh.devices.reshape(SIZES), AXES)
    return jax.shard_map(
        local,
        mesh=fine,
        in_specs=(
            P("zl", MEM),
            P("zl", MEM),
            P("zl", MEM),
            P("zl", None),
            P(MEM + ("zl",), None),
            P(MEM + ("zl",), None),
        ),
        out_specs=(P("zl", MEM), P(MEM + ("zl",), None), P(MEM + ("zl",), None)),
        check_vma=False,
    )
```

time: 1080 us -> 98.2 us (0.09)
  the two profiles are of different devices: /device:TPU:1 before, /device:TPU:96 now
where the time goes in v3:
time: 98.2 us; the launch traced here: 97.8 us
  waiting for transfers between devices  49.2 us (50%)
  starting transfers between devices  34.1 us (35%)
  Pallas kernels  12.4 us (13%)
    all_to_all x1, waiting for transfers between devices, local(): lax.all_to_all(chunks, OWNERS, split_axis=0, concat_axis=0, tiled=True)  14.8 us
    ppermute x1, waiting for transfers between devices, local(): cross = lax.ppermute(cross, ('zh', 'x'), inverse(CROSS))  13.1 us
    all_to_all x1, starting transfers between devices, local(): lax.all_to_all(chunks, OWNERS, split_axis=0, concat_axis=0, tiled=True)  10.9 us
    ppermute x1, starting transfers between devices, local(): cross = lax.ppermute(message, ('zh', 'x'), CROSS)  8.18 us
    pallas_call x1, Pallas kernels, attention(): call(attention_kernel, [pltpu.HBM((16, 2, KEYS, DH), BF16), shape(*part,...  6.92 us
    ppermute x3, waiting for transfers between devices, local(): lax.ppermute(first, 'zl', turn(d))  6.82 us
    ppermute x3, waiting for transfers between devices, local(): lax.ppermute(sums[d], 'zl', turn(d))  6.21 us
    ppermute x3, starting transfers between devices, local(): lax.ppermute(first, 'zl', turn(d))  5.76 us
  transfers between devices with their start and end apart: 14, of which 9 were waited for; matrix products, arithmetic and copies ran while one was open for 1% of the time, Pallas kernels for 3%

profile of v3, /device:TPU:96, one launch (start us, length us, event | category | flops | bytes accessed | tf_op | source)
XLA Modules:
  0.0 97.8 jit_solution(1624926008605344658)
XLA Ops:
  0.6 0.9 message.1
  1.5 0.7 collective-permute-start.1
  2.2 8.2 %collective-permute-start = (bf16[144,256]{1,0:T(8,128)(2,1)S(1)}, bf16[144,256]{1,0:T(8,128)(2,1)S(1)}, u32[]{:S(2)}, u32[]{:S(2)}) collective-permute-start(bf16[144,256]{1,0:T(8,128)(2,1)S(1)} %message.1), channel_id=1, source_target_pairs={{0,40},{8,0},{16,56},{24,16},{32,8},{40,32},{48,24},{56,48},{1,41}... | collective-permute-start | bytes 221192 | tf_op jit(solution)/shard_map/ppermute | solution.py:326
  10.4 2.8 %split.1 = bf16[16,2,128,256]{3,2,1,0:T(8,128)(2,1)} custom-call(bf16[128,4096]{1,0:T(8,128)(2,1)} %keys.1, bf16[128,4096]{1,0:T(8,128)(2,1)} %values.1), custom_call_target="tpu_custom_call" | custom-call | bytes 8388608 | tf_op jit(solution)/shard_map/split/pallas_call | solution.py:176
  13.2 0.0 collective-permute-done.1.straight
  13.2 0.0 collective-permute-done.cross
  13.2 10.9 %all-to-all-start = ((bf16[16,2,128,256]{3,2,1,0:T(8,128)(2,1)}), bf16[16,2,128,256]{3,2,1,0:T(8,128)(2,1)S(1)}, u32[]{:S(2)}, u32[]{:S(2)}) async-start(bf16[16,2,128,256]{3,2,1,0:T(8,128)(2,1)} %split.1), calls=%async_computation | async-start | bytes 4194304 | tf_op jit(solution)/shard_map/all_to_all | solution.py:330
  24.2 1.5 %collective-permute-start.4 = (bf16[272,256]{1,0:T(8,128)(2,1)S(1)}, bf16[272,256]{1,0:T(8,128)(2,1)S(1)}, u32[]{:S(2)}, u32[]{:S(2)}) collective-permute-start(bf16[272,256]{1,0:T(8,128)(2,1)S(1)} %bundle.1.refs_0_), channel_id=1, source_target_pairs={{0,3},{1,0},{2,1},{3,2},{4,7},{5,4},{6,5},{7,6},{8,11},{9,8},{10,9... | collective-permute-start | bytes 417800 | tf_op jit(solution)/shard_map/ppermute | solution.py:332
  25.7 1.5 %collective-permute-start.3 = (bf16[272,256]{1,0:T(8,128)(2,1)S(1)}, bf16[272,256]{1,0:T(8,128)(2,1)S(1)}, u32[]{:S(2)}, u32[]{:S(2)}) collective-permute-start(bf16[272,256]{1,0:T(8,128)(2,1)S(1)} %bundle.1.refs_0_), channel_id=1, source_target_pairs={{0,2},{1,3},{2,0},{3,1},{4,6},{5,7},{6,4},{7,5},{8,10},{9,11},{10,... | collective-permute-start | bytes 417800 | tf_op jit(solution)/shard_map/ppermute | solution.py:332
  27.1 2.8 %collective-permute-start.2 = (bf16[272,256]{1,0:T(8,128)(2,1)S(1)}, bf16[272,256]{1,0:T(8,128)(2,1)S(1)}, u32[]{:S(2)}, u32[]{:S(2)}) collective-permute-start(bf16[272,256]{1,0:T(8,128)(2,1)S(1)} %bundle.1.refs_0_), channel_id=1, source_target_pairs={{0,1},{1,2},{2,3},{3,0},{4,5},{5,6},{6,7},{7,4},{8,9},{9,10},{10,1... | collective-permute-start | bytes 417800 | tf_op jit(solution)/shard_map/ppermute | solution.py:332
  29.9 2.8 %collective-permute-done.4.refs_3_ = bf16[272,256]{1,0:T(8,128)(2,1)S(1)} collective-permute-done((bf16[272,256]{1,0:T(8,128)(2,1)S(1)}, bf16[272,256]{1,0:T(8,128)(2,1)S(1)}, u32[]{:S(2)}, u32[]{:S(2)}) %collective-permute-start.4) | collective-permute-done | bytes 139296 | tf_op jit(solution)/shard_map/ppermute | solution.py:332
  32.7 4.0 %collective-permute-done.3.refs_2_ = bf16[272,256]{1,0:T(8,128)(2,1)S(1)} collective-permute-done((bf16[272,256]{1,0:T(8,128)(2,1)S(1)}, bf16[272,256]{1,0:T(8,128)(2,1)S(1)}, u32[]{:S(2)}, u32[]{:S(2)}) %collective-permute-start.3) | collective-permute-done | bytes 139296 | tf_op jit(solution)/shard_map/ppermute | solution.py:332
  36.8 0.0 collective-permute-done.2.refs_1_
  36.8 0.1 collective-permute-start.5
  36.9 1.9 %collective-permute-done.5.there = bf16[4,272,256]{2,1,0:T(8,128)(2,1)S(1)} collective-permute-done((bf16[4,272,256]{2,1,0:T(8,128)(2,1)S(1)}, bf16[4,272,256]{2,1,0:T(8,128)(2,1)S(1)}, u32[]{:S(2)}, u32[]{:S(2)}) %collective-permute-start.5) | collective-permute-done | bytes 557088 | tf_op jit(solution)/shard_map/ppermute | solution.py:333
  38.9 0.0 copy-start
  38.9 0.8 copy-done
  39.7 14.8 %all-to-all-done.kv = bf16[16,2,128,256]{3,2,1,0:T(8,128)(2,1)S(1)} async-done(((bf16[16,2,128,256]{3,2,1,0:T(8,128)(2,1)}), bf16[16,2,128,256]{3,2,1,0:T(8,128)(2,1)S(1)}, u32[]{:S(2)}, u32[]{:S(2)}) %all-to-all-start) | async-done | bytes 2097184 | tf_op jit(solution)/shard_map/all_to_all | solution.py:330
  54.5 6.9 %attention.1 = (bf16[16,2,128,256]{3,2,1,0:T(8,128)(2,1)}, f32[4,2,64,256]{3,2,1,0:T(8,128)S(1)}, bf16[4,2,64,256]{3,2,1,0:T(8,128)(2,1)S(1)}) custom-call(bf16[4,272,256]{2,1,0:T(8,128)(2,1)S(1)} %stack.1.mine, bf16[4,272,256]{2,1,0:T(8,128)(2,1)} %copy-done, bf16[16,2,128,256]{3,2,1,0:T(8,128)(2,1)S(1)} %all-to-all-done.kv), custom_call_target="tpu_custom_call" | custom-call | flops 5368709120 | bytes 8388608 | tf_op jit(solution)/shard_map/attention/pallas_call | solution.py:267
  61.4 3.7 %all-to-all-start.1 = ((bf16[16,2,128,256]{3,2,1,0:T(8,128)(2,1)}), bf16[16,2,128,256]{3,2,1,0:T(8,128)(2,1)S(1)}, u32[]{:S(2)}, u32[]{:S(2)}) async-start(bf16[16,2,128,256]{3,2,1,0:T(8,128)(2,1)} %get-tuple-element.28), calls=%async_computation.1 | async-start | bytes 4194304 | tf_op jit(solution)/shard_map/all_to_all | solution.py:335
  65.1 0.1 collective-permute-start.6
  65.2 1.5 %collective-permute-done.6.other = bf16[4,2,64,256]{3,2,1,0:T(8,128)(2,1)S(1)} collective-permute-done((bf16[4,2,64,256]{3,2,1,0:T(8,128)(2,1)S(1)}, bf16[4,2,64,256]{3,2,1,0:T(8,128)(2,1)S(1)}, u32[]{:S(2)}, u32[]{:S(2)}) %collective-permute-start.6) | collective-permute-done | bytes 262176 | tf_op jit(solution)/shard_map/ppermute | solution.py:336
  66.8 0.5 collective-permute-start.7
  67.3 0.0 collective-permute-start.8
  67.3 1.7 %collective-permute-start.9 = (bf16[2,64,256]{2,1,0:T(8,128)(2,1)S(1)}, bf16[2,64,256]{2,1,0:T(8,128)(2,1)S(1)}, u32[]{:S(2)}, u32[]{:S(2)}) collective-permute-start(bf16[2,64,256]{2,1,0:T(8,128)(2,1)S(1)} %get-tuple-element.25), channel_id=1, source_target_pairs={{0,3},{1,0},{2,1},{3,2},{4,7},{5,4},{6,5},{7,6},{8,11},{9,8},{10,9... | collective-permute-start | bytes 196616 | tf_op jit(solution)/shard_map/ppermute | solution.py:337
  69.0 2.9 %collective-permute-done.7.refs_1_ = bf16[2,64,256]{2,1,0:T(8,128)(2,1)S(1)} collective-permute-done((bf16[2,64,256]{2,1,0:T(8,128)(2,1)S(1)}, bf16[2,64,256]{2,1,0:T(8,128)(2,1)S(1)}, u32[]{:S(2)}, u32[]{:S(2)}) %collective-permute-start.7) | collective-permute-done | bytes 65568 | tf_op jit(solution)/shard_map/ppermute | solution.py:337
  71.8 3.3 %collective-permute-done.8.refs_2_ = bf16[2,64,256]{2,1,0:T(8,128)(2,1)S(1)} collective-permute-done((bf16[2,64,256]{2,1,0:T(8,128)(2,1)S(1)}, bf16[2,64,256]{2,1,0:T(8,128)(2,1)S(1)}, u32[]{:S(2)}, u32[]{:S(2)}) %collective-permute-start.8) | collective-permute-done | bytes 65568 | tf_op jit(solution)/shard_map/ppermute | solution.py:337
  75.2 0.0 collective-permute-done.9.refs_3_
  75.2 1.8 %collective-permute-start.10 = (bf16[64,256]{1,0:T(8,128)(2,1)S(1)}, bf16[64,256]{1,0:T(8,128)(2,1)S(1)}, u32[]{:S(2)}, u32[]{:S(2)}) collective-permute-start(bf16[64,256]{1,0:T(8,128)(2,1)S(1)} %get-tuple-element.26), channel_id=1, source_target_pairs={{40,0},{0,8},{56,16},{16,24},{8,32},{32,40},{24,48},{48,56},{41,1}... | collective-permute-start | bytes 98312 | tf_op jit(solution)/shard_map/ppermute | solution.py:339
  77.0 0.7 collective-permute-start.11
  77.7 13.1 %collective-permute-done.10 = bf16[64,256]{1,0:T(8,128)(2,1)S(1)} collective-permute-done((bf16[64,256]{1,0:T(8,128)(2,1)S(1)}, bf16[64,256]{1,0:T(8,128)(2,1)S(1)}, u32[]{:S(2)}, u32[]{:S(2)}) %collective-permute-start.10) | collective-permute-done | bytes 32800 | tf_op jit(solution)/shard_map/ppermute | solution.py:339
  90.8 0.0 collective-permute-done.11
  90.8 0.6 fusion
  91.4 4.8 %all-to-all-done.1.chunks = bf16[16,2,128,256]{3,2,1,0:T(8,128)(2,1)S(1)} async-done(((bf16[16,2,128,256]{3,2,1,0:T(8,128)(2,1)}), bf16[16,2,128,256]{3,2,1,0:T(8,128)(2,1)S(1)}, u32[]{:S(2)}, u32[]{:S(2)}) %all-to-all-start.1) | async-done | bytes 2097184 | tf_op jit(solution)/shard_map/all_to_all | solution.py:335
  96.2 1.6 %join.1 = (bf16[128,4096]{1,0:T(8,128)(2,1)}, bf16[128,4096]{1,0:T(8,128)(2,1)}) custom-call(bf16[16,2,128,256]{3,2,1,0:T(8,128)(2,1)S(1)} %all-to-all-done.1.chunks), custom_call_target="tpu_custom_call" | custom-call | tf_op jit(solution)/shard_map/join/pallas_call | solution.py:201
  (4 shorter events, 0.1 us)
Async XLA Ops:
  1.5 11.7 %collective-permute-start.1 = (bf16[144,256]{1,0:T(8,128)(2,1)S(1)}, bf16[144,256]{1,0:T(8,128)(2,1)S(1)}, u32[]{:S(2)}, u32[]{:S(2)}) collective-permute-start(bf16[144,256]{1,0:T(8,128)(2,1)S(1)} %message.1), channel_id=1, source_target_pairs={{0,0},{8,40},{16,16},{24,56},{32,32},{40,8},{48,48},{56,24},{1,1},... | collective-permute-start | bytes 221192 | tf_op jit(solution)/shard_map/ppermute | solution.py:327
  2.2 11.0 %collective-permute-start = (bf16[144,256]{1,0:T(8,128)(2,1)S(1)}, bf16[144,256]{1,0:T(8,128)(2,1)S(1)}, u32[]{:S(2)}, u32[]{:S(2)}) collective-permute-start(bf16[144,256]{1,0:T(8,128)(2,1)S(1)} %message.1), channel_id=1, source_target_pairs={{0,40},{8,0},{16,56},{24,16},{32,8},{40,32},{48,24},{56,48},{1,41}... | collective-permute-start | bytes 221192 | tf_op jit(solution)/shard_map/ppermute | solution.py:326
  13.2 41.2 %all-to-all-start = ((bf16[16,2,128,256]{3,2,1,0:T(8,128)(2,1)}), bf16[16,2,128,256]{3,2,1,0:T(8,128)(2,1)S(1)}, u32[]{:S(2)}, u32[]{:S(2)}) async-start(bf16[16,2,128,256]{3,2,1,0:T(8,128)(2,1)} %split.1), calls=%async_computation | async-start | bytes 4194304 | tf_op jit(solution)/shard_map/all_to_all | solution.py:330
  24.2 8.5 %collective-permute-start.4 = (bf16[272,256]{1,0:T(8,128)(2,1)S(1)}, bf16[272,256]{1,0:T(8,128)(2,1)S(1)}, u32[]{:S(2)}, u32[]{:S(2)}) collective-permute-start(bf16[272,256]{1,0:T(8,128)(2,1)S(1)} %bundle.1.refs_0_), channel_id=1, source_target_pairs={{0,3},{1,0},{2,1},{3,2},{4,7},{5,4},{6,5},{7,6},{8,11},{9,8},{10,9... | collective-permute-start | bytes 417800 | tf_op jit(solution)/shard_map/ppermute | solution.py:332
  25.7 11.1 %collective-permute-start.3 = (bf16[272,256]{1,0:T(8,128)(2,1)S(1)}, bf16[272,256]{1,0:T(8,128)(2,1)S(1)}, u32[]{:S(2)}, u32[]{:S(2)}) collective-permute-start(bf16[272,256]{1,0:T(8,128)(2,1)S(1)} %bundle.1.refs_0_), channel_id=1, source_target_pairs={{0,2},{1,3},{2,0},{3,1},{4,6},{5,7},{6,4},{7,5},{8,10},{9,11},{10,... | collective-permute-start | bytes 417800 | tf_op jit(solution)/shard_map/ppermute | solution.py:332
  27.1 9.7 %collective-permute-start.2 = (bf16[272,256]{1,0:T(8,128)(2,1)S(1)}, bf16[272,256]{1,0:T(8,128)(2,1)S(1)}, u32[]{:S(2)}, u32[]{:S(2)}) collective-permute-start(bf16[272,256]{1,0:T(8,128)(2,1)S(1)} %bundle.1.refs_0_), channel_id=1, source_target_pairs={{0,1},{1,2},{2,3},{3,0},{4,5},{5,6},{6,7},{7,4},{8,9},{9,10},{10,1... | collective-permute-start | bytes 417800 | tf_op jit(solution)/shard_map/ppermute | solution.py:332
  36.8 2.0 %collective-permute-start.5 = (bf16[4,272,256]{2,1,0:T(8,128)(2,1)S(1)}, bf16[4,272,256]{2,1,0:T(8,128)(2,1)S(1)}, u32[]{:S(2)}, u32[]{:S(2)}) collective-permute-start(bf16[4,272,256]{2,1,0:T(8,128)(2,1)S(1)} %stack.1.mine), channel_id=1, source_target_pairs={{0,4},{4,0},{1,5},{5,1},{2,6},{6,2},{3,7},{7,3},{8,12},{12,8},{9,1... | collective-permute-start | bytes 1671176 | tf_op jit(solution)/shard_map/ppermute | solution.py:333
  38.9 0.8 copy-start
  61.4 34.8 %all-to-all-start.1 = ((bf16[16,2,128,256]{3,2,1,0:T(8,128)(2,1)}), bf16[16,2,128,256]{3,2,1,0:T(8,128)(2,1)S(1)}, u32[]{:S(2)}, u32[]{:S(2)}) async-start(bf16[16,2,128,256]{3,2,1,0:T(8,128)(2,1)} %get-tuple-element.28), calls=%async_computation.1 | async-start | bytes 4194304 | tf_op jit(solution)/shard_map/all_to_all | solution.py:335
  65.1 1.6 %collective-permute-start.6 = (bf16[4,2,64,256]{3,2,1,0:T(8,128)(2,1)S(1)}, bf16[4,2,64,256]{3,2,1,0:T(8,128)(2,1)S(1)}, u32[]{:S(2)}, u32[]{:S(2)}) collective-permute-start(bf16[4,2,64,256]{3,2,1,0:T(8,128)(2,1)S(1)} %get-tuple-element.21), channel_id=1, source_target_pairs={{0,4},{4,0},{1,5},{5,1},{2,6},{6,2},{3,7},{7,3},{8,12},{12,8},{9,1... | collective-permute-start | bytes 786440 | tf_op jit(solution)/shard_map/ppermute | solution.py:336
  66.8 5.0 %collective-permute-start.7 = (bf16[2,64,256]{2,1,0:T(8,128)(2,1)S(1)}, bf16[2,64,256]{2,1,0:T(8,128)(2,1)S(1)}, u32[]{:S(2)}, u32[]{:S(2)}) collective-permute-start(bf16[2,64,256]{2,1,0:T(8,128)(2,1)S(1)} %get-tuple-element.23), channel_id=1, source_target_pairs={{0,1},{1,2},{2,3},{3,0},{4,5},{5,6},{6,7},{7,4},{8,9},{9,10},{10,1... | collective-permute-start | bytes 196616 | tf_op jit(solution)/shard_map/ppermute | solution.py:337
  67.3 7.9 %collective-permute-start.8 = (bf16[2,64,256]{2,1,0:T(8,128)(2,1)S(1)}, bf16[2,64,256]{2,1,0:T(8,128)(2,1)S(1)}, u32[]{:S(2)}, u32[]{:S(2)}) collective-permute-start(bf16[2,64,256]{2,1,0:T(8,128)(2,1)S(1)} %get-tuple-element.24), channel_id=1, source_target_pairs={{0,2},{1,3},{2,0},{3,1},{4,6},{5,7},{6,4},{7,5},{8,10},{9,11},{10,... | collective-permute-start | bytes 196616 | tf_op jit(solution)/shard_map/ppermute | solution.py:337
  67.3 7.9 %collective-permute-start.9 = (bf16[2,64,256]{2,1,0:T(8,128)(2,1)S(1)}, bf16[2,64,256]{2,1,0:T(8,128)(2,1)S(1)}, u32[]{:S(2)}, u32[]{:S(2)}) collective-permute-start(bf16[2,64,256]{2,1,0:T(8,128)(2,1)S(1)} %get-tuple-element.25), channel_id=1, source_target_pairs={{0,3},{1,0},{2,1},{3,2},{4,7},{5,4},{6,5},{7,6},{8,11},{9,8},{10,9... | collective-permute-start | bytes 196616 | tf_op jit(solution)/shard_map/ppermute | solution.py:337
  75.2 15.5 %collective-permute-start.10 = (bf16[64,256]{1,0:T(8,128)(2,1)S(1)}, bf16[64,256]{1,0:T(8,128)(2,1)S(1)}, u32[]{:S(2)}, u32[]{:S(2)}) collective-permute-start(bf16[64,256]{1,0:T(8,128)(2,1)S(1)} %get-tuple-element.26), channel_id=1, source_target_pairs={{40,0},{0,8},{56,16},{16,24},{8,32},{32,40},{24,48},{48,56},{41,1}... | collective-permute-start | bytes 98312 | tf_op jit(solution)/shard_map/ppermute | solution.py:339
  77.0 13.8 %collective-permute-start.11 = (bf16[64,256]{1,0:T(8,128)(2,1)S(1)}, bf16[64,256]{1,0:T(8,128)(2,1)S(1)}, u32[]{:S(2)}, u32[]{:S(2)}) collective-permute-start(bf16[64,256]{1,0:T(8,128)(2,1)S(1)} %get-tuple-element.27), channel_id=1, source_target_pairs={{0,0},{40,8},{16,16},{56,24},{32,32},{8,40},{48,48},{24,56},{1,1},... | collective-permute-start | bytes 98312 | tf_op jit(solution)/shard_map/ppermute | solution.py:340

commit v4 on v3

--- a/solution.py
+++ b/solution.py
@@ -8,7 +8,6 @@
 AXES = ("y", "zh", "x", "core", "zl")
 SIZES = (4, 2, 4, 2, 4)
 MEM = ("y", "zh", "x", "core")
-OWNERS = ("y", "x")
 HEADS = 16
 DH = 256
 ROWS = 256
@@ -40,29 +39,49 @@
     return jax.ShapeDtypeStruct(dims, dtype)
 
 
-def pair_of(zh, x):
-    return zh * 4 + x
-
-
-CROSS = [
-    (pair_of(zh, x), pair_of(zh, x - 1) if x % 2 else pair_of(1 - zh, x + 1))
-    for zh in range(2)
-    for x in range(4)
-]
-STRAIGHT = [
-    (pair_of(zh, x), pair_of(1 - zh, x) if x % 2 else pair_of(zh, x))
-    for zh in range(2)
-    for x in range(4)
-]
+LINE = ("zh", "x", "zl")
+
+
+def line_pairs(k):
+    pairs = []
+    for zh in range(2):
+        for x in range(4):
+            for zl in range(4):
+                z = 2 * ((zl + k) % 4) + (zh + x) % 2
+                to = (z // 4 * 4 + x) * 4 + z % 4
+                pairs.append(((zh * 4 + x) * 4 + zl, to))
+    return pairs
+
+
+def row_block(k):
+    step = 2 * lax.axis_index("zh") + lax.axis_index("zl") // 2
+    return lax.rem(step + 4 - k, 4)
+
+
+NEXT = [(0, 1), (1, 0), (2, 3), (3, 2)]
 SWAP = [(0, 1), (1, 0)]
+
+
+def peer(slot, core):
+    return (slot // 4 + 2 * core) % 4, (slot + 2 * core) % 4
+
+
+def exchange(chunks):
+    groups = []
+    for zh in range(2):
+        for core in range(2):
+            for zl in range(4):
+                peers = [peer(slot, core) for slot in range(16)]
+                groups.append(
+                    [(((y * 2 + zh) * 4 + x) * 2 + core) * 4 + zl for y, x in peers]
+                )
+    return lax.all_to_all(
+        chunks, AXES, split_axis=0, concat_axis=0, tiled=True, axis_index_groups=groups
+    )
 
 
 def inverse(pairs):
     return [(b, a) for a, b in pairs]
-
-
-def turn(step):
-    return [(i, (i + step) % 4) for i in range(4)]
 
 
 def pieces(value):
@@ -116,13 +135,13 @@
     )(*map(in_hbm, args))
 
 
-def bundle_kernel(cross, straight, out):
+def bundle_kernel(own, other, out):
     odd = lax.rem(lax.axis_index("x"), 2)
-    for ref, place in ((cross, 1 - odd), (straight, odd)):
+    for ref, place in ((own, odd), (other, 1 - odd)):
         start = pl.multiple_of(place * PART, PART)
         out[pl.ds(start, PART), :] = ref[:PART, :]
         out[pl.ds(start + 2 * PART, PART), :] = ref[PART : 2 * PART, :]
-    one, two = cross[2 * PART :, :].astype(F32), straight[2 * PART :, :].astype(F32)
+    one, two = own[2 * PART :, :].astype(F32), other[2 * PART :, :].astype(F32)
     both = one + two
     rows = pieces(both[0:1] + both[1:2] + both[2:3])
     out[4 * PART :, :] = stat_rows(rows + [one[3:6]])
@@ -134,21 +153,9 @@
     )(*args)
 
 
-def stack_kernel(*refs):
-    for i, ref in enumerate(refs[:-1]):
-        refs[-1][i] = ref[...]
-
-
-def stack(parts):
-    out = shape(len(parts), *parts[0].shape)
-    return call(stack_kernel, out, [VMEM] * len(parts), VMEM, 8, "stack")(*parts)
-
-
 def slot_columns(s):
-    y, x = s // 4, s % 4
-    zh = lax.axis_index("zh")
-    if x % 2:
-        zh = 1 - zh
+    y, x = peer(s, lax.axis_index("core"))
+    zh = (lax.axis_index("zl") + x) % 2
     return pl.ds(pl.multiple_of((4 * y + 2 * zh + x // 2) * DH, DH), DH)
 
 
@@ -205,25 +212,36 @@
     return lax.dot_general(a, b, (((ca,), (cb,)), ((), ())), preferred_element_type=F32)
 
 
-def attention_kernel(
-    mine, there, kv, grads, own, other, theirs, qt, dt, stat, dkv, dq, ds, sem
-):
-    core, here = lax.axis_index("core"), lax.axis_index("zl")
-    copy = pltpu.make_async_copy(there, theirs, sem.at[0])
-    copy.start()
-    copy.wait()
-    for d in range(4):
-        zl = lax.rem(here + 4 - d, 4)
-        for ref, c in ((mine, core), (theirs, 1 - core)):
+def assemble_kernel(*refs):
+    mine, theirs, (qt, dt, stat) = refs[:4], refs[4:8], refs[8:]
+    core = lax.axis_index("core")
+    for k in range(4):
+        zl = row_block(k)
+        for ref, c in ((mine[k], core), (theirs[k], 1 - core)):
             for xl in range(2):
                 to = pl.ds(pl.multiple_of((2 * xl + c) * PART, PART), PART)
-                qt[zl, to, :] = ref[d, xl * PART : (xl + 1) * PART, :]
-                dt[zl, to, :] = ref[d, (2 + xl) * PART : (3 + xl) * PART, :]
-        one = mine[d, 4 * PART :, :].astype(F32)
-        both = one + theirs[d, 4 * PART :, :].astype(F32)
+                qt[zl, to, :] = ref[xl * PART : (xl + 1) * PART, :]
+                dt[zl, to, :] = ref[(2 + xl) * PART : (3 + xl) * PART, :]
+        one = mine[k][4 * PART :, :].astype(F32)
+        both = one + theirs[k][4 * PART :, :].astype(F32)
         stat[zl, 0:1, :] = both[0:1] + both[1:2] + both[2:3]
         stat[zl, 1:2, :] = (one[3:4] + one[4:5] + one[5:6]) * LOG2E
 
+
+def assemble(mine, theirs):
+    block = shape(4, DH, ROWS)
+    return call(
+        assemble_kernel,
+        [block, block, shape(4, 8, ROWS, dtype=F32)],
+        [VMEM] * 8,
+        [VMEM] * 3,
+        8,
+        "assemble",
+    )(*mine, *theirs)
+
+
+def attention_kernel(qt, dt, stat, kv, grads, own, other, dkv, dq, ds, sem):
+    core = lax.axis_index("core")
     writes = []
     for block in range(8):
         rows = slice(block * 2 * KEYS, (block + 1) * 2 * KEYS)
@@ -251,31 +269,27 @@
     keys = kv[:, 0].reshape(16 * KEYS, DH)
     for zl in range(4):
         dq[zl] = dot(keys, ds[zl], 0, 0) * FACTOR
-    for d in range(4):
-        zl = lax.rem(here + d, 4)
+    for k in range(4):
+        zl = row_block(k)
         for xl in range(2):
             at = pl.ds(pl.multiple_of((2 * xl + core) * PART, PART), PART)
-            own[d, xl] = dq[zl, at, :]
+            own[k, xl] = dq[zl, at, :]
             at = pl.ds(pl.multiple_of((2 * xl + 1 - core) * PART, PART), PART)
-            other[d, xl] = dq[zl, at, :].astype(BF16)
+            other[k, xl] = dq[zl, at, :].astype(BF16)
     for copy in writes:
         copy.wait()
 
 
-def attention(mine, theirs, kv):
+def attention(qt, dt, stat, kv):
     part = (4, 2, PART, ROWS)
     return call(
         attention_kernel,
         [pltpu.HBM((16, 2, KEYS, DH), BF16), shape(*part, dtype=F32), shape(*part)],
-        [VMEM, HBM, VMEM],
+        [VMEM] * 4,
         [HBM, VMEM, VMEM],
         32,
         "attention",
         [
-            pltpu.VMEM((4, 4 * PART + STAT, ROWS), BF16),
-            pltpu.VMEM((4, DH, ROWS), BF16),
-            pltpu.VMEM((4, DH, ROWS), BF16),
-            pltpu.VMEM((4, 8, ROWS), F32),
             pltpu.VMEM((16, 2, KEYS, DH), BF16),
             pltpu.VMEM((4, DH, ROWS), F32),
             pltpu.VMEM((4, 16 * KEYS, ROWS), BF16),
@@ -286,7 +300,7 @@
             bytes_accessed=8 * MIB,
             transcendentals=2048 * 1024,
         ),
-    )(mine, in_hbm(theirs), kv)
+    )(qt, dt, stat, kv)
 
 
 def core_sum_kernel(own, other, *outs):
@@ -306,40 +320,40 @@
 
 
 def line_sum_kernel(*refs):
-    parts, cross, straight = refs[:4], refs[4], refs[5]
+    parts, own, other = refs[:4], refs[4], refs[5]
     odd = lax.rem(lax.axis_index("x"), 2)
-    for out, place in ((cross, 1 - odd), (straight, odd)):
+    for out, place in ((own, odd), (other, 1 - odd)):
         total = parts[0][place].astype(F32)
         for part in parts[1:]:
             total = total + part[place].astype(F32)
-        out[...] = total.astype(BF16)
+        out[...] = total.astype(out.dtype)
 
 
 def line_sum(parts):
-    return call(
-        line_sum_kernel, [shape(PART, ROWS)] * 2, [VMEM] * 4, [VMEM] * 2, 4, "line_sum"
-    )(*parts)
+    outs = [shape(PART, ROWS, dtype=F32), shape(PART, ROWS)]
+    return call(line_sum_kernel, outs, [VMEM] * 4, [VMEM] * 2, 4, "line_sum")(*parts)
 
 
 def local(queries, outputs, cotangent, log_norms, memory_keys, memory_values):
     message = make_message(queries.T, outputs.T, cotangent.T, log_norms.T)
-    cross = lax.ppermute(message, ("zh", "x"), CROSS)
-    straight = lax.ppermute(message, ("zh", "x"), STRAIGHT)
+    other = lax.ppermute(message, "x", NEXT)
     chunks = split(memory_keys, memory_values)
-    chunks, cross, straight = lax.optimization_barrier((chunks, cross, straight))
-    received = lax.all_to_all(chunks, OWNERS, split_axis=0, concat_axis=0, tiled=True)
-    first = bundle(cross, straight)
-    mine = stack([first] + [lax.ppermute(first, "zl", turn(d)) for d in (1, 2, 3)])
-    theirs = lax.ppermute(mine, "core", SWAP)
-    grads, own, other = attention(mine, theirs, received)
-    returned = lax.all_to_all(grads, OWNERS, split_axis=0, concat_axis=0, tiled=True)
+    chunks, other = lax.optimization_barrier((chunks, other))
+    received = exchange(chunks)
+    part = bundle(message, other)
+    mine = [lax.ppermute(part, LINE, line_pairs(k)) for k in range(4)]
+    theirs = [lax.ppermute(part, "core", SWAP) for part in mine]
+    grads, own, other = attention(*assemble(mine, theirs), received)
+    returned = exchange(grads)
     sums = core_sum(own, lax.ppermute(other, "core", SWAP))
-    parts = [sums[0]] + [lax.ppermute(sums[d], "zl", turn(d)) for d in (1, 2, 3)]
-    cross, straight = line_sum(parts)
-    cross = lax.ppermute(cross, ("zh", "x"), inverse(CROSS))
-    straight = lax.ppermute(straight, ("zh", "x"), inverse(STRAIGHT))
-    query_grads = (cross.astype(F32) + straight.astype(F32)).astype(BF16).T
+    sums = [lax.ppermute(sums[k], LINE, inverse(line_pairs(k))) for k in range(4)]
+    own, other = line_sum(sums)
+    other = lax.ppermute(other, "x", NEXT)
     key_grads, value_grads = join(returned)
+    other, key_grads, value_grads = lax.optimization_barrier(
+        (other, key_grads, value_grads)
+    )
+    query_grads = (own + other.astype(F32)).astype(BF16).T
     return query_grads, key_grads, value_grads
 
 

time: 98.2 us -> 89.5 us (0.911)
  the two profiles are of different devices: /device:TPU:96 before, /device:TPU:200 now
where the time goes in v4:
time: 89.5 us; the launch traced here: 88.9 us
  starting transfers between devices  41.1 us (46%)
  waiting for transfers between devices  33.2 us (37%)
  Pallas kernels  11.4 us (13%)
  local copies, waits for them, and re-layouts  1.83 us (2%)
    ppermute x4, waiting for transfers between devices, local(): mine = [lax.ppermute(part, LINE, line_pairs(k)) for k in range(4)]  13.6 us
    ppermute x4, starting transfers between devices, local(): mine = [lax.ppermute(part, LINE, line_pairs(k)) for k in range(4)]  13.2 us
    all_to_all x2, starting transfers between devices, exchange(): lax.all_to_all(chunks, AXES, split_axis=0, concat_axis=0, tiled=True, axi...  13 us
    all_to_all x2, waiting for transfers between devices, exchange(): lax.all_to_all(chunks, AXES, split_axis=0, concat_axis=0, tiled=True, axi...  10.9 us
    ppermute x4, starting transfers between devices, local(): lax.ppermute(sums[k], LINE, inverse(line_pairs(k)))  10.3 us
    ppermute x4, waiting for transfers between devices, local(): lax.ppermute(sums[k], LINE, inverse(line_pairs(k)))  6.22 us
    pallas_call x1, Pallas kernels, attention(): call(attention_kernel, [pltpu.HBM((16, 2, KEYS, DH), BF16), shape(*part,...  5.78 us
    pallas_call x1, Pallas kernels, split(): call(split_kernel, pltpu.HBM((16, 2, KEYS, DH), BF16), [HBM] * 2, HBM, 8,...  2.85 us
  transfers between devices with their start and end apart: 17, of which 8 were waited for; matrix products, arithmetic and copies ran while one was open for 0% of the time, Pallas kernels for 5%

profile of v4, /device:TPU:200, one launch (start us, length us, event | category | flops | bytes accessed | tf_op | source)
XLA Modules:
  0.0 88.9 jit_solution(10105593727296104562)
XLA Ops:
  0.6 0.9 message.1.own
  1.5 1.6 %collective-permute-start = (bf16[144,256]{1,0:T(8,128)(2,1)S(1)}, bf16[144,256]{1,0:T(8,128)(2,1)S(1)}, u32[]{:S(2)}, u32[]{:S(2)}) collective-permute-start(bf16[144,256]{1,0:T(8,128)(2,1)S(1)} %message.1.own), channel_id=1, source_target_pairs={{0,8},{8,0},{16,24},{24,16},{1,9},{9,1},{17,25},{25,17},{2,10},{10... | collective-permute-start | bytes 221192 | tf_op jit(solution)/shard_map/ppermute | solution.py:339
  3.1 2.8 %split.1 = bf16[16,2,128,256]{3,2,1,0:T(8,128)(2,1)} custom-call(bf16[128,4096]{1,0:T(8,128)(2,1)} %keys.1, bf16[128,4096]{1,0:T(8,128)(2,1)} %values.1), custom_call_target="tpu_custom_call" | custom-call | bytes 8388608 | tf_op jit(solution)/shard_map/split/pallas_call | solution.py:183
  5.9 0.0 collective-permute-done.other
  5.9 7.4 %all-to-all-start = ((bf16[16,2,128,256]{3,2,1,0:T(8,128)(2,1)}), bf16[16,2,128,256]{3,2,1,0:T(8,128)(2,1)S(1)}, u32[]{:S(2)}, u32[]{:S(2)}) async-start(bf16[16,2,128,256]{3,2,1,0:T(8,128)(2,1)} %split.1), calls=%async_computation | async-start | bytes 4194304 | tf_op jit(solution)/shard_map/all_to_all | solution.py:78
  13.4 2.9 %collective-permute-start.4 = (bf16[272,256]{1,0:T(8,128)(2,1)S(1)}, bf16[272,256]{1,0:T(8,128)(2,1)S(1)}, u32[]{:S(2)}, u32[]{:S(2)}) collective-permute-start(bf16[272,256]{1,0:T(8,128)(2,1)S(1)} %bundle.1), channel_id=1, source_target_pairs={{0,34},{1,0},{2,2},{3,32},{8,43},{9,9},{10,11},{11,41},{16,50},{17... | collective-permute-start | bytes 417800 | tf_op jit(solution)/shard_map/ppermute | solution.py:344
  16.3 1.9 %collective-permute-start.3 = (bf16[272,256]{1,0:T(8,128)(2,1)S(1)}, bf16[272,256]{1,0:T(8,128)(2,1)S(1)}, u32[]{:S(2)}, u32[]{:S(2)}) collective-permute-start(bf16[272,256]{1,0:T(8,128)(2,1)S(1)} %bundle.1), channel_id=1, source_target_pairs={{0,32},{1,34},{2,0},{3,2},{8,41},{9,43},{10,9},{11,11},{16,48},{17... | collective-permute-start | bytes 417800 | tf_op jit(solution)/shard_map/ppermute | solution.py:344
  18.2 6.5 %collective-permute-start.2 = (bf16[272,256]{1,0:T(8,128)(2,1)S(1)}, bf16[272,256]{1,0:T(8,128)(2,1)S(1)}, u32[]{:S(2)}, u32[]{:S(2)}) collective-permute-start(bf16[272,256]{1,0:T(8,128)(2,1)S(1)} %bundle.1), channel_id=1, source_target_pairs={{0,2},{1,32},{2,34},{3,0},{8,11},{9,41},{10,43},{11,9},{16,18},{17... | collective-permute-start | bytes 417800 | tf_op jit(solution)/shard_map/ppermute | solution.py:344
  24.7 1.9 %collective-permute-start.1 = (bf16[272,256]{1,0:T(8,128)(2,1)S(1)}, bf16[272,256]{1,0:T(8,128)(2,1)S(1)}, u32[]{:S(2)}, u32[]{:S(2)}) collective-permute-start(bf16[272,256]{1,0:T(8,128)(2,1)S(1)} %bundle.1), channel_id=1, source_target_pairs={{0,0},{1,2},{2,32},{3,34},{8,9},{9,11},{10,41},{11,43},{16,16},{17... | collective-permute-start | bytes 417800 | tf_op jit(solution)/shard_map/ppermute | solution.py:344
  26.6 0.0 collective-permute-done.4.refs_3_
  26.6 0.1 collective-permute-start.8
  26.7 3.4 %collective-permute-done.3.refs_2_ = bf16[272,256]{1,0:T(8,128)(2,1)S(1)} collective-permute-done((bf16[272,256]{1,0:T(8,128)(2,1)S(1)}, bf16[272,256]{1,0:T(8,128)(2,1)S(1)}, u32[]{:S(2)}, u32[]{:S(2)}) %collective-permute-start.3) | collective-permute-done | bytes 139296 | tf_op jit(solution)/shard_map/ppermute | solution.py:344
  30.2 0.0 collective-permute-start.7
  30.2 3.7 %collective-permute-done.2.refs_1_ = bf16[272,256]{1,0:T(8,128)(2,1)S(1)} collective-permute-done((bf16[272,256]{1,0:T(8,128)(2,1)S(1)}, bf16[272,256]{1,0:T(8,128)(2,1)S(1)}, u32[]{:S(2)}, u32[]{:S(2)}) %collective-permute-start.2) | collective-permute-done | bytes 139296 | tf_op jit(solution)/shard_map/ppermute | solution.py:344
  33.9 0.0 collective-permute-start.6
  33.9 6.5 %collective-permute-done.1.refs_0_ = bf16[272,256]{1,0:T(8,128)(2,1)S(1)} collective-permute-done((bf16[272,256]{1,0:T(8,128)(2,1)S(1)}, bf16[272,256]{1,0:T(8,128)(2,1)S(1)}, u32[]{:S(2)}, u32[]{:S(2)}) %collective-permute-start.1) | collective-permute-done | bytes 139296 | tf_op jit(solution)/shard_map/ppermute | solution.py:344
  40.4 0.0 collective-permute-start.5
  40.4 0.0 collective-permute-done.8.refs_7_
  40.4 0.0 collective-permute-done.7.refs_6_
  40.4 0.0 collective-permute-done.6.refs_5_
  40.4 1.3 %collective-permute-done.5.refs_4_ = bf16[272,256]{1,0:T(8,128)(2,1)S(1)} collective-permute-done((bf16[272,256]{1,0:T(8,128)(2,1)S(1)}, bf16[272,256]{1,0:T(8,128)(2,1)S(1)}, u32[]{:S(2)}, u32[]{:S(2)}) %collective-permute-start.5) | collective-permute-done | bytes 139296 | tf_op jit(solution)/shard_map/ppermute | solution.py:345
  41.7 0.1 assemble.1
  41.9 0.0 copy-start
  41.9 0.8 copy-done
  42.7 0.0 all-to-all-done.kv
  42.7 0.0 copy-start.1
  42.7 1.0 %copy-done.1 = bf16[4,256,256]{2,1,0:T(8,128)(2,1)S(1)} copy-done((bf16[4,256,256]{2,1,0:T(8,128)(2,1)S(1)}, bf16[4,256,256]{2,1,0:T(8,128)(2,1)}, u32[]{:S(2)}) %copy-start.1) | copy-done | bytes 524312
  43.7 5.8 %attention.1 = (bf16[16,2,128,256]{3,2,1,0:T(8,128)(2,1)}, f32[4,2,64,256]{3,2,1,0:T(8,128)S(1)}, bf16[4,2,64,256]{3,2,1,0:T(8,128)(2,1)S(1)}) custom-call(bf16[4,256,256]{2,1,0:T(8,128)(2,1)S(1)} %get-tuple-element.23.qt, bf16[4,256,256]{2,1,0:T(8,128)(2,1)S(1)} %copy-done.1, f32[4,8,256]{2,1,0:T(8,128)S(1)} %get-tuple-element.25.stat, ...), custom_call_target="tpu_custom_call" | custom-call | flops 5368709120 | bytes 8388608 | tf_op jit(solution)/shard_map/attention/pallas_call | solution.py:285
  49.5 5.6 %all-to-all-start.1 = ((bf16[16,2,128,256]{3,2,1,0:T(8,128)(2,1)}), bf16[16,2,128,256]{3,2,1,0:T(8,128)(2,1)S(1)}, u32[]{:S(2)}, u32[]{:S(2)}) async-start(bf16[16,2,128,256]{3,2,1,0:T(8,128)(2,1)} %get-tuple-element.35), calls=%async_computation.1 | async-start | bytes 4194304 | tf_op jit(solution)/shard_map/all_to_all | solution.py:78
  55.1 1.2 %collective-permute-start.9 = (bf16[4,2,64,256]{3,2,1,0:T(8,128)(2,1)S(1)}, bf16[4,2,64,256]{3,2,1,0:T(8,128)(2,1)S(1)}, u32[]{:S(2)}, u32[]{:S(2)}) collective-permute-start(bf16[4,2,64,256]{3,2,1,0:T(8,128)(2,1)S(1)} %get-tuple-element.28), channel_id=1, source_target_pairs={{0,4},{4,0},{1,5},{5,1},{2,6},{6,2},{3,7},{7,3},{8,12},{12,8},{9,1... | collective-permute-start | bytes 786440 | tf_op jit(solution)/shard_map/ppermute | solution.py:348
  56.3 1.2 %collective-permute-done.9.other = bf16[4,2,64,256]{3,2,1,0:T(8,128)(2,1)S(1)} collective-permute-done((bf16[4,2,64,256]{3,2,1,0:T(8,128)(2,1)S(1)}, bf16[4,2,64,256]{3,2,1,0:T(8,128)(2,1)S(1)}, u32[]{:S(2)}, u32[]{:S(2)}) %collective-permute-start.9) | collective-permute-done | bytes 262176 | tf_op jit(solution)/shard_map/ppermute | solution.py:348
  57.5 1.9 %collective-permute-start.10 = (bf16[2,64,256]{2,1,0:T(8,128)(2,1)S(1)}, bf16[2,64,256]{2,1,0:T(8,128)(2,1)S(1)}, u32[]{:S(2)}, u32[]{:S(2)}) collective-permute-start(bf16[2,64,256]{2,1,0:T(8,128)(2,1)S(1)} %get-tuple-element.29), channel_id=1, source_target_pairs={{0,0},{2,1},{32,2},{34,3},{9,8},{11,9},{41,10},{43,11},{16,16},{18... | collective-permute-start | bytes 196616 | tf_op jit(solution)/shard_map/ppermute | solution.py:349
  59.4 2.2 %collective-permute-start.11 = (bf16[2,64,256]{2,1,0:T(8,128)(2,1)S(1)}, bf16[2,64,256]{2,1,0:T(8,128)(2,1)S(1)}, u32[]{:S(2)}, u32[]{:S(2)}) collective-permute-start(bf16[2,64,256]{2,1,0:T(8,128)(2,1)S(1)} %get-tuple-element.30), channel_id=1, source_target_pairs={{2,0},{32,1},{34,2},{0,3},{11,8},{41,9},{43,10},{9,11},{18,16},{48... | collective-permute-start | bytes 196616 | tf_op jit(solution)/shard_map/ppermute | solution.py:349
  61.6 3.3 %collective-permute-start.12 = (bf16[2,64,256]{2,1,0:T(8,128)(2,1)S(1)}, bf16[2,64,256]{2,1,0:T(8,128)(2,1)S(1)}, u32[]{:S(2)}, u32[]{:S(2)}) collective-permute-start(bf16[2,64,256]{2,1,0:T(8,128)(2,1)S(1)} %get-tuple-element.31), channel_id=1, source_target_pairs={{32,0},{34,1},{0,2},{2,3},{41,8},{43,9},{9,10},{11,11},{48,16},{50... | collective-permute-start | bytes 196616 | tf_op jit(solution)/shard_map/ppermute | solution.py:349
  64.9 2.9 %collective-permute-start.13 = (bf16[2,64,256]{2,1,0:T(8,128)(2,1)S(1)}, bf16[2,64,256]{2,1,0:T(8,128)(2,1)S(1)}, u32[]{:S(2)}, u32[]{:S(2)}) collective-permute-start(bf16[2,64,256]{2,1,0:T(8,128)(2,1)S(1)} %get-tuple-element.32), channel_id=1, source_target_pairs={{34,0},{0,1},{2,2},{32,3},{43,8},{9,9},{11,10},{41,11},{50,16},{16... | collective-permute-start | bytes 196616 | tf_op jit(solution)/shard_map/ppermute | solution.py:349
  67.8 0.0 collective-permute-done.10.refs_0_
  67.8 0.0 collective-permute-done.11.refs_1_
  67.8 3.0 %collective-permute-done.12.refs_2_ = bf16[2,64,256]{2,1,0:T(8,128)(2,1)S(1)} collective-permute-done((bf16[2,64,256]{2,1,0:T(8,128)(2,1)S(1)}, bf16[2,64,256]{2,1,0:T(8,128)(2,1)S(1)}, u32[]{:S(2)}, u32[]{:S(2)}) %collective-permute-start.12) | collective-permute-done | bytes 65568 | tf_op jit(solution)/shard_map/ppermute | solution.py:349
  70.8 3.3 %collective-permute-done.13.refs_3_ = bf16[2,64,256]{2,1,0:T(8,128)(2,1)S(1)} collective-permute-done((bf16[2,64,256]{2,1,0:T(8,128)(2,1)S(1)}, bf16[2,64,256]{2,1,0:T(8,128)(2,1)S(1)}, u32[]{:S(2)}, u32[]{:S(2)}) %collective-permute-start.13) | collective-permute-done | bytes 65568 | tf_op jit(solution)/shard_map/ppermute | solution.py:349
  74.1 1.7 %collective-permute-start.14 = (bf16[64,256]{1,0:T(8,128)(2,1)S(1)}, bf16[64,256]{1,0:T(8,128)(2,1)S(1)}, u32[]{:S(2)}, u32[]{:S(2)}) collective-permute-start(bf16[64,256]{1,0:T(8,128)(2,1)S(1)} %get-tuple-element.34), channel_id=1, source_target_pairs={{0,8},{8,0},{16,24},{24,16},{1,9},{9,1},{17,25},{25,17},{2,10},{10... | collective-permute-start | bytes 98312 | tf_op jit(solution)/shard_map/ppermute | solution.py:351
  75.8 10.8 %all-to-all-done.1.chunks = bf16[16,2,128,256]{3,2,1,0:T(8,128)(2,1)S(1)} async-done(((bf16[16,2,128,256]{3,2,1,0:T(8,128)(2,1)}), bf16[16,2,128,256]{3,2,1,0:T(8,128)(2,1)S(1)}, u32[]{:S(2)}, u32[]{:S(2)}) %all-to-all-start.1) | async-done | bytes 2097184 | tf_op jit(solution)/shard_map/all_to_all | solution.py:78
  86.6 1.7 %join.1 = (bf16[128,4096]{1,0:T(8,128)(2,1)}, bf16[128,4096]{1,0:T(8,128)(2,1)}) custom-call(bf16[16,2,128,256]{3,2,1,0:T(8,128)(2,1)S(1)} %all-to-all-done.1.chunks), custom_call_target="tpu_custom_call" | custom-call | tf_op jit(solution)/shard_map/join/pallas_call | solution.py:208
  88.3 0.0 collective-permute-done.14
  88.3 0.6 fusion
  (3 shorter events, 0.1 us)
Async XLA Ops:
  1.5 4.4 %collective-permute-start = (bf16[144,256]{1,0:T(8,128)(2,1)S(1)}, bf16[144,256]{1,0:T(8,128)(2,1)S(1)}, u32[]{:S(2)}, u32[]{:S(2)}) collective-permute-start(bf16[144,256]{1,0:T(8,128)(2,1)S(1)} %message.1.own), channel_id=1, source_target_pairs={{0,8},{8,0},{16,24},{24,16},{1,9},{9,1},{17,25},{25,17},{2,10},{10... | collective-permute-start | bytes 221192 | tf_op jit(solution)/shard_map/ppermute | solution.py:339
  5.9 36.7 %all-to-all-start = ((bf16[16,2,128,256]{3,2,1,0:T(8,128)(2,1)}), bf16[16,2,128,256]{3,2,1,0:T(8,128)(2,1)S(1)}, u32[]{:S(2)}, u32[]{:S(2)}) async-start(bf16[16,2,128,256]{3,2,1,0:T(8,128)(2,1)} %split.1), calls=%async_computation | async-start | bytes 4194304 | tf_op jit(solution)/shard_map/all_to_all | solution.py:78
  13.4 13.3 %collective-permute-start.4 = (bf16[272,256]{1,0:T(8,128)(2,1)S(1)}, bf16[272,256]{1,0:T(8,128)(2,1)S(1)}, u32[]{:S(2)}, u32[]{:S(2)}) collective-permute-start(bf16[272,256]{1,0:T(8,128)(2,1)S(1)} %bundle.1), channel_id=1, source_target_pairs={{0,34},{1,0},{2,2},{3,32},{8,43},{9,9},{10,11},{11,41},{16,50},{17... | collective-permute-start | bytes 417800 | tf_op jit(solution)/shard_map/ppermute | solution.py:344
  16.3 13.9 %collective-permute-start.3 = (bf16[272,256]{1,0:T(8,128)(2,1)S(1)}, bf16[272,256]{1,0:T(8,128)(2,1)S(1)}, u32[]{:S(2)}, u32[]{:S(2)}) collective-permute-start(bf16[272,256]{1,0:T(8,128)(2,1)S(1)} %bundle.1), channel_id=1, source_target_pairs={{0,32},{1,34},{2,0},{3,2},{8,41},{9,43},{10,9},{11,11},{16,48},{17... | collective-permute-start | bytes 417800 | tf_op jit(solution)/shard_map/ppermute | solution.py:344
  18.2 15.7 %collective-permute-start.2 = (bf16[272,256]{1,0:T(8,128)(2,1)S(1)}, bf16[272,256]{1,0:T(8,128)(2,1)S(1)}, u32[]{:S(2)}, u32[]{:S(2)}) collective-permute-start(bf16[272,256]{1,0:T(8,128)(2,1)S(1)} %bundle.1), channel_id=1, source_target_pairs={{0,2},{1,32},{2,34},{3,0},{8,11},{9,41},{10,43},{11,9},{16,18},{17... | collective-permute-start | bytes 417800 | tf_op jit(solution)/shard_map/ppermute | solution.py:344
  24.7 15.7 %collective-permute-start.1 = (bf16[272,256]{1,0:T(8,128)(2,1)S(1)}, bf16[272,256]{1,0:T(8,128)(2,1)S(1)}, u32[]{:S(2)}, u32[]{:S(2)}) collective-permute-start(bf16[272,256]{1,0:T(8,128)(2,1)S(1)} %bundle.1), channel_id=1, source_target_pairs={{0,0},{1,2},{2,32},{3,34},{8,9},{9,11},{10,41},{11,43},{16,16},{17... | collective-permute-start | bytes 417800 | tf_op jit(solution)/shard_map/ppermute | solution.py:344
  26.6 13.7 %collective-permute-start.8 = (bf16[272,256]{1,0:T(8,128)(2,1)S(1)}, bf16[272,256]{1,0:T(8,128)(2,1)S(1)}, u32[]{:S(2)}, u32[]{:S(2)}) collective-permute-start(bf16[272,256]{1,0:T(8,128)(2,1)S(1)} %collective-permute-done.4.refs_3_), channel_id=1, source_target_pairs={{0,4},{4,0},{1,5},{5,1},{2,6},{6,2},{3,7},{7,3},{8,12},{12,8},{9,1... | collective-permute-start | bytes 417800 | tf_op jit(solution)/shard_map/ppermute | solution.py:345
  30.2 10.2 %collective-permute-start.7 = (bf16[272,256]{1,0:T(8,128)(2,1)S(1)}, bf16[272,256]{1,0:T(8,128)(2,1)S(1)}, u32[]{:S(2)}, u32[]{:S(2)}) collective-permute-start(bf16[272,256]{1,0:T(8,128)(2,1)S(1)} %collective-permute-done.3.refs_2_), channel_id=1, source_target_pairs={{0,4},{4,0},{1,5},{5,1},{2,6},{6,2},{3,7},{7,3},{8,12},{12,8},{9,1... | collective-permute-start | bytes 417800 | tf_op jit(solution)/shard_map/ppermute | solution.py:345
  33.9 6.5 %collective-permute-start.6 = (bf16[272,256]{1,0:T(8,128)(2,1)S(1)}, bf16[272,256]{1,0:T(8,128)(2,1)S(1)}, u32[]{:S(2)}, u32[]{:S(2)}) collective-permute-start(bf16[272,256]{1,0:T(8,128)(2,1)S(1)} %collective-permute-done.2.refs_1_), channel_id=1, source_target_pairs={{0,4},{4,0},{1,5},{5,1},{2,6},{6,2},{3,7},{7,3},{8,12},{12,8},{9,1... | collective-permute-start | bytes 417800 | tf_op jit(solution)/shard_map/ppermute | solution.py:345
  40.4 1.4 %collective-permute-start.5 = (bf16[272,256]{1,0:T(8,128)(2,1)S(1)}, bf16[272,256]{1,0:T(8,128)(2,1)S(1)}, u32[]{:S(2)}, u32[]{:S(2)}) collective-permute-start(bf16[272,256]{1,0:T(8,128)(2,1)S(1)} %collective-permute-done.1.refs_0_), channel_id=1, source_target_pairs={{0,4},{4,0},{1,5},{5,1},{2,6},{6,2},{3,7},{7,3},{8,12},{12,8},{9,1... | collective-permute-start | bytes 417800 | tf_op jit(solution)/shard_map/ppermute | solution.py:345
  41.9 0.8 copy-start
  42.7 1.0 %copy-start.1 = (bf16[4,256,256]{2,1,0:T(8,128)(2,1)S(1)}, bf16[4,256,256]{2,1,0:T(8,128)(2,1)}, u32[]{:S(2)}) copy-start(bf16[4,256,256]{2,1,0:T(8,128)(2,1)} %copy-done) | copy-start | bytes 1572868
  49.5 37.1 %all-to-all-start.1 = ((bf16[16,2,128,256]{3,2,1,0:T(8,128)(2,1)}), bf16[16,2,128,256]{3,2,1,0:T(8,128)(2,1)S(1)}, u32[]{:S(2)}, u32[]{:S(2)}) async-start(bf16[16,2,128,256]{3,2,1,0:T(8,128)(2,1)} %get-tuple-element.35), calls=%async_computation.1 | async-start | bytes 4194304 | tf_op jit(solution)/shard_map/all_to_all | solution.py:78
  55.1 2.4 %collective-permute-start.9 = (bf16[4,2,64,256]{3,2,1,0:T(8,128)(2,1)S(1)}, bf16[4,2,64,256]{3,2,1,0:T(8,128)(2,1)S(1)}, u32[]{:S(2)}, u32[]{:S(2)}) collective-permute-start(bf16[4,2,64,256]{3,2,1,0:T(8,128)(2,1)S(1)} %get-tuple-element.28), channel_id=1, source_target_pairs={{0,4},{4,0},{1,5},{5,1},{2,6},{6,2},{3,7},{7,3},{8,12},{12,8},{9,1... | collective-permute-start | bytes 786440 | tf_op jit(solution)/shard_map/ppermute | solution.py:348
  57.5 10.3 %collective-permute-start.10 = (bf16[2,64,256]{2,1,0:T(8,128)(2,1)S(1)}, bf16[2,64,256]{2,1,0:T(8,128)(2,1)S(1)}, u32[]{:S(2)}, u32[]{:S(2)}) collective-permute-start(bf16[2,64,256]{2,1,0:T(8,128)(2,1)S(1)} %get-tuple-element.29), channel_id=1, source_target_pairs={{0,0},{2,1},{32,2},{34,3},{9,8},{11,9},{41,10},{43,11},{16,16},{18... | collective-permute-start | bytes 196616 | tf_op jit(solution)/shard_map/ppermute | solution.py:349
  59.4 8.4 %collective-permute-start.11 = (bf16[2,64,256]{2,1,0:T(8,128)(2,1)S(1)}, bf16[2,64,256]{2,1,0:T(8,128)(2,1)S(1)}, u32[]{:S(2)}, u32[]{:S(2)}) collective-permute-start(bf16[2,64,256]{2,1,0:T(8,128)(2,1)S(1)} %get-tuple-element.30), channel_id=1, source_target_pairs={{2,0},{32,1},{34,2},{0,3},{11,8},{41,9},{43,10},{9,11},{18,16},{48... | collective-permute-start | bytes 196616 | tf_op jit(solution)/shard_map/ppermute | solution.py:349
  61.6 9.2 %collective-permute-start.12 = (bf16[2,64,256]{2,1,0:T(8,128)(2,1)S(1)}, bf16[2,64,256]{2,1,0:T(8,128)(2,1)S(1)}, u32[]{:S(2)}, u32[]{:S(2)}) collective-permute-start(bf16[2,64,256]{2,1,0:T(8,128)(2,1)S(1)} %get-tuple-element.31), channel_id=1, source_target_pairs={{32,0},{34,1},{0,2},{2,3},{41,8},{43,9},{9,10},{11,11},{48,16},{50... | collective-permute-start | bytes 196616 | tf_op jit(solution)/shard_map/ppermute | solution.py:349
  64.9 9.2 %collective-permute-start.13 = (bf16[2,64,256]{2,1,0:T(8,128)(2,1)S(1)}, bf16[2,64,256]{2,1,0:T(8,128)(2,1)S(1)}, u32[]{:S(2)}, u32[]{:S(2)}) collective-permute-start(bf16[2,64,256]{2,1,0:T(8,128)(2,1)S(1)} %get-tuple-element.32), channel_id=1, source_target_pairs={{34,0},{0,1},{2,2},{32,3},{43,8},{9,9},{11,10},{41,11},{50,16},{16... | collective-permute-start | bytes 196616 | tf_op jit(solution)/shard_map/ppermute | solution.py:349
  74.1 14.2 %collective-permute-start.14 = (bf16[64,256]{1,0:T(8,128)(2,1)S(1)}, bf16[64,256]{1,0:T(8,128)(2,1)S(1)}, u32[]{:S(2)}, u32[]{:S(2)}) collective-permute-start(bf16[64,256]{1,0:T(8,128)(2,1)S(1)} %get-tuple-element.34), channel_id=1, source_target_pairs={{0,8},{8,0},{16,24},{24,16},{1,9},{9,1},{17,25},{25,17},{2,10},{10... | collective-permute-start | bytes 98312 | tf_op jit(solution)/shard_map/ppermute | solution.py:351

commit v5 on v4

--- a/solution.py
+++ b/solution.py
@@ -39,23 +39,24 @@
     return jax.ShapeDtypeStruct(dims, dtype)
 
 
-LINE = ("zh", "x", "zl")
+LINE = ("zh", "x", "core", "zl")
 
 
 def line_pairs(k):
     pairs = []
     for zh in range(2):
         for x in range(4):
-            for zl in range(4):
-                z = 2 * ((zl + k) % 4) + (zh + x) % 2
-                to = (z // 4 * 4 + x) * 4 + z % 4
-                pairs.append(((zh * 4 + x) * 4 + zl, to))
+            for core in range(2):
+                for zl in range(4):
+                    z = 2 * ((zl + k + 2 * core) % 4) + (zh + x) % 2
+                    to = ((z // 4 * 4 + x) * 2 + core) * 4 + z % 4
+                    pairs.append((((zh * 4 + x) * 2 + core) * 4 + zl, to))
     return pairs
 
 
-def row_block(k):
+def row_block(k, core):
     step = 2 * lax.axis_index("zh") + lax.axis_index("zl") // 2
-    return lax.rem(step + 4 - k, 4)
+    return (step + 4 - k + 2 * core) % 4
 
 
 NEXT = [(0, 1), (1, 0), (2, 3), (3, 2)]
@@ -196,16 +197,20 @@
     )(in_hbm(keys), in_hbm(values))
 
 
-def join_kernel(chunks, keys, values):
+def join_kernel(chunks, own, other, keys, values, queries):
+    queries[...] = (own[...] + other[...].astype(F32)).astype(BF16)
     for s in range(16):
         columns = slot_columns(s)
         keys[:, columns] = chunks[s, 0]
         values[:, columns] = chunks[s, 1]
 
 
-def join(chunks):
+def join(chunks, own, other):
     out = shape(KEYS, HEADS * DH)
-    return call(join_kernel, [out] * 2, [VMEM], [VMEM] * 2, 8, "join")(chunks)
+    outs = [out, out, shape(PART, ROWS)]
+    return call(join_kernel, outs, [VMEM] * 3, [VMEM] * 3, 8, "join")(
+        chunks, own, other
+    )
 
 
 def dot(a, b, ca, cb):
@@ -213,35 +218,44 @@
 
 
 def assemble_kernel(*refs):
-    mine, theirs, (qt, dt, stat) = refs[:4], refs[4:8], refs[8:]
+    mine, theirs, (qt, out, stat, dt, sem) = refs[:4], refs[4:8], refs[8:]
     core = lax.axis_index("core")
     for k in range(4):
-        zl = row_block(k)
-        for ref, c in ((mine[k], core), (theirs[k], 1 - core)):
+        for ref, c in ((mine[k], core), (theirs[(k + 2) % 4], 1 - core)):
+            zl = row_block(k, core)
             for xl in range(2):
                 to = pl.ds(pl.multiple_of((2 * xl + c) * PART, PART), PART)
                 qt[zl, to, :] = ref[xl * PART : (xl + 1) * PART, :]
                 dt[zl, to, :] = ref[(2 + xl) * PART : (3 + xl) * PART, :]
         one = mine[k][4 * PART :, :].astype(F32)
-        both = one + theirs[k][4 * PART :, :].astype(F32)
+        both = one + theirs[(k + 2) % 4][4 * PART :, :].astype(F32)
         stat[zl, 0:1, :] = both[0:1] + both[1:2] + both[2:3]
         stat[zl, 1:2, :] = (one[3:4] + one[4:5] + one[5:6]) * LOG2E
+    copy = pltpu.make_async_copy(dt, out, sem)
+    copy.start()
+    copy.wait()
 
 
 def assemble(mine, theirs):
-    block = shape(4, DH, ROWS)
+    block = (4, DH, ROWS)
     return call(
         assemble_kernel,
-        [block, block, shape(4, 8, ROWS, dtype=F32)],
+        [shape(*block), pltpu.HBM(block, BF16), shape(4, 8, ROWS, dtype=F32)],
         [VMEM] * 8,
-        [VMEM] * 3,
+        [VMEM, HBM, VMEM],
         8,
         "assemble",
+        [pltpu.VMEM(block, BF16), pltpu.SemaphoreType.DMA],
     )(*mine, *theirs)
 
 
-def attention_kernel(qt, dt, stat, kv, grads, own, other, dkv, dq, ds, sem):
+def attention_kernel(
+    qt, cotangent, stat, kv, grads, own, other, dt, dkv, dq, ds, sem, in_sem
+):
     core = lax.axis_index("core")
+    read = pltpu.make_async_copy(cotangent, dt, in_sem)
+    read.start()
+    read.wait()
     writes = []
     for block in range(8):
         rows = slice(block * 2 * KEYS, (block + 1) * 2 * KEYS)
@@ -270,12 +284,12 @@
     for zl in range(4):
         dq[zl] = dot(keys, ds[zl], 0, 0) * FACTOR
     for k in range(4):
-        zl = row_block(k)
+        zl = row_block(k, core)
         for xl in range(2):
             at = pl.ds(pl.multiple_of((2 * xl + core) * PART, PART), PART)
             own[k, xl] = dq[zl, at, :]
             at = pl.ds(pl.multiple_of((2 * xl + 1 - core) * PART, PART), PART)
-            other[k, xl] = dq[zl, at, :].astype(BF16)
+            other[(k + 2) % 4, xl] = dq[zl, at, :].astype(BF16)
     for copy in writes:
         copy.wait()
 
@@ -285,22 +299,24 @@
     return call(
         attention_kernel,
         [pltpu.HBM((16, 2, KEYS, DH), BF16), shape(*part, dtype=F32), shape(*part)],
-        [VMEM] * 4,
+        [VMEM, HBM, VMEM, VMEM],
         [HBM, VMEM, VMEM],
         32,
         "attention",
         [
+            pltpu.VMEM((4, DH, ROWS), BF16),
             pltpu.VMEM((16, 2, KEYS, DH), BF16),
             pltpu.VMEM((4, DH, ROWS), F32),
             pltpu.VMEM((4, 16 * KEYS, ROWS), BF16),
             pltpu.SemaphoreType.DMA((8,)),
+            pltpu.SemaphoreType.DMA,
         ],
         pl.CostEstimate(
             flops=5 * 2 * 2048 * 1024 * 256,
             bytes_accessed=8 * MIB,
             transcendentals=2048 * 1024,
         ),
-    )(qt, dt, stat, kv)
+    )(qt, in_hbm(dt), stat, kv)
 
 
 def core_sum_kernel(own, other, *outs):
@@ -349,12 +365,8 @@
     sums = [lax.ppermute(sums[k], LINE, inverse(line_pairs(k))) for k in range(4)]
     own, other = line_sum(sums)
     other = lax.ppermute(other, "x", NEXT)
-    key_grads, value_grads = join(returned)
-    other, key_grads, value_grads = lax.optimization_barrier(
-        (other, key_grads, value_grads)
-    )
-    query_grads = (own + other.astype(F32)).astype(BF16).T
-    return query_grads, key_grads, value_grads
+    key_grads, value_grads, query_grads = join(returned, own, other)
+    return query_grads.T, key_grads, value_grads
 
 
 def solution(mesh):

time: 89.5 us -> 88 us (0.983)
  the two profiles are of different devices: /device:TPU:200 before, /device:TPU:1 now
where the time goes in v5:
time: 88 us; the launch traced here: 87.4 us
  starting transfers between devices  59.9 us (68%)
  waiting for transfers between devices  13.6 us (15%)
  Pallas kernels  13.2 us (15%)
    all_to_all x2, starting transfers between devices, exchange(): lax.all_to_all(chunks, AXES, split_axis=0, concat_axis=0, tiled=True, axi...  19.1 us
    ppermute x4, starting transfers between devices, local(): mine = [lax.ppermute(part, LINE, line_pairs(k)) for k in range(4)]  19 us
    ppermute x4, starting transfers between devices, local(): lax.ppermute(sums[k], LINE, inverse(line_pairs(k)))  15.4 us
    pallas_call x1, Pallas kernels, attention(): call(attention_kernel, [pltpu.HBM((16, 2, KEYS, DH), BF16), shape(*part,...  6.82 us
    ppermute x1, waiting for transfers between devices, local(): other = lax.ppermute(other, 'x', NEXT)  6.75 us
    pallas_call x1, Pallas kernels, split(): call(split_kernel, pltpu.HBM((16, 2, KEYS, DH), BF16), [HBM] * 2, HBM, 8,...  2.84 us
    ppermute x4, starting transfers between devices, local(): theirs = [lax.ppermute(part, 'core', SWAP) for part in mine]  2.66 us
    ppermute x1, starting transfers between devices, local(): other = lax.ppermute(message, 'x', NEXT)  2.13 us
  transfers between devices with their start and end apart: 17, of which 7 were waited for; matrix products, arithmetic and copies ran while one was open for 0% of the time, Pallas kernels for 4%

profile of v5, /device:TPU:1, one launch (start us, length us, event | category | flops | bytes accessed | tf_op | source)
XLA Modules:
  0.0 87.4 jit_solution(235513073689456935)
XLA Ops:
  0.6 0.9 message.1.own
  1.5 2.1 %collective-permute-start = (bf16[144,256]{1,0:T(8,128)(2,1)S(1)}, bf16[144,256]{1,0:T(8,128)(2,1)S(1)}, u32[]{:S(2)}, u32[]{:S(2)}) collective-permute-start(bf16[144,256]{1,0:T(8,128)(2,1)S(1)} %message.1.own), channel_id=1, source_target_pairs={{0,8},{8,0},{16,24},{24,16},{1,9},{9,1},{17,25},{25,17},{2,10},{10... | collective-permute-start | bytes 221192 | tf_op jit(solution)/shard_map/ppermute | solution.py:355
  3.6 2.8 %split.1 = bf16[16,2,128,256]{3,2,1,0:T(8,128)(2,1)} custom-call(bf16[128,4096]{1,0:T(8,128)(2,1)} %keys.1, bf16[128,4096]{1,0:T(8,128)(2,1)} %values.1), custom_call_target="tpu_custom_call" | custom-call | bytes 8388608 | tf_op jit(solution)/shard_map/split/pallas_call | solution.py:184
  6.5 0.0 collective-permute-done.other
  6.5 8.7 %all-to-all-start = ((bf16[16,2,128,256]{3,2,1,0:T(8,128)(2,1)}), bf16[16,2,128,256]{3,2,1,0:T(8,128)(2,1)S(1)}, u32[]{:S(2)}, u32[]{:S(2)}) async-start(bf16[16,2,128,256]{3,2,1,0:T(8,128)(2,1)} %split.1), calls=%async_computation | async-start | bytes 4194304 | tf_op jit(solution)/shard_map/all_to_all | solution.py:79
  15.2 4.9 %collective-permute-start.4 = (bf16[272,256]{1,0:T(8,128)(2,1)S(1)}, bf16[272,256]{1,0:T(8,128)(2,1)S(1)}, u32[]{:S(2)}, u32[]{:S(2)}) collective-permute-start(bf16[272,256]{1,0:T(8,128)(2,1)S(1)} %bundle.1), channel_id=1, source_target_pairs={{0,34},{1,0},{2,2},{3,32},{4,6},{5,36},{6,38},{7,4},{8,43},{9,9},{... | collective-permute-start | bytes 417800 | tf_op jit(solution)/shard_map/ppermute | solution.py:360
  20.1 0.7 collective-permute-start.3
  20.8 6.9 %collective-permute-start.2 = (bf16[272,256]{1,0:T(8,128)(2,1)S(1)}, bf16[272,256]{1,0:T(8,128)(2,1)S(1)}, u32[]{:S(2)}, u32[]{:S(2)}) collective-permute-start(bf16[272,256]{1,0:T(8,128)(2,1)S(1)} %bundle.1), channel_id=1, source_target_pairs={{0,2},{1,32},{2,34},{3,0},{4,38},{5,4},{6,6},{7,36},{8,11},{9,41},... | collective-permute-start | bytes 417800 | tf_op jit(solution)/shard_map/ppermute | solution.py:360
  27.7 6.5 %collective-permute-start.1 = (bf16[272,256]{1,0:T(8,128)(2,1)S(1)}, bf16[272,256]{1,0:T(8,128)(2,1)S(1)}, u32[]{:S(2)}, u32[]{:S(2)}) collective-permute-start(bf16[272,256]{1,0:T(8,128)(2,1)S(1)} %bundle.1), channel_id=1, source_target_pairs={{0,0},{1,2},{2,32},{3,34},{4,36},{5,38},{6,4},{7,6},{8,9},{9,11},{... | collective-permute-start | bytes 417800 | tf_op jit(solution)/shard_map/ppermute | solution.py:360
  34.2 0.0 collective-permute-done.4.refs_3_
  34.2 0.1 collective-permute-start.8
  34.3 0.0 collective-permute-done.3.refs_2_
  34.4 0.5 collective-permute-start.7
  34.8 0.0 collective-permute-done.2.refs_1_
  34.8 2.1 %collective-permute-start.6 = (bf16[272,256]{1,0:T(8,128)(2,1)S(1)}, bf16[272,256]{1,0:T(8,128)(2,1)S(1)}, u32[]{:S(2)}, u32[]{:S(2)}) collective-permute-start(bf16[272,256]{1,0:T(8,128)(2,1)S(1)} %collective-permute-done.2.refs_1_), channel_id=1, source_target_pairs={{0,4},{4,0},{1,5},{5,1},{2,6},{6,2},{3,7},{7,3},{8,12},{12,8},{9,1... | collective-permute-start | bytes 417800 | tf_op jit(solution)/shard_map/ppermute | solution.py:361
  36.9 0.6 collective-permute-done.1.refs_0_
  37.5 0.0 collective-permute-start.5
  37.5 0.0 collective-permute-done.8.refs_7_
  37.5 0.0 collective-permute-done.7.refs_6_
  37.5 0.4 collective-permute-done.6.refs_5_
  37.9 0.9 %collective-permute-done.5.refs_4_ = bf16[272,256]{1,0:T(8,128)(2,1)S(1)} collective-permute-done((bf16[272,256]{1,0:T(8,128)(2,1)S(1)}, bf16[272,256]{1,0:T(8,128)(2,1)S(1)}, u32[]{:S(2)}, u32[]{:S(2)}) %collective-permute-start.5) | collective-permute-done | bytes 139296 | tf_op jit(solution)/shard_map/ppermute | solution.py:361
  38.8 0.9 %assemble.1 = (bf16[4,256,256]{2,1,0:T(8,128)(2,1)S(1)}, bf16[4,256,256]{2,1,0:T(8,128)(2,1)}, f32[4,8,256]{2,1,0:T(8,128)S(1)}) custom-call(bf16[272,256]{1,0:T(8,128)(2,1)S(1)} %collective-permute-done.1.refs_0_, bf16[272,256]{1,0:T(8,128)(2,1)S(1)} %collective-permute-done.2.refs_1_, bf16[272,256]{1,0:T(8,128)(2,1)S(1)} %collective-permute-done.3.refs_2_, ...), custom_call_target="tpu_custom_call" | custom-call | tf_op jit(solution)/shard_map/assemble/pallas_call | solution.py:241
  39.8 1.6 %all-to-all-done.kv = bf16[16,2,128,256]{3,2,1,0:T(8,128)(2,1)S(1)} async-done(((bf16[16,2,128,256]{3,2,1,0:T(8,128)(2,1)}), bf16[16,2,128,256]{3,2,1,0:T(8,128)(2,1)S(1)}, u32[]{:S(2)}, u32[]{:S(2)}) %all-to-all-start) | async-done | bytes 2097184 | tf_op jit(solution)/shard_map/all_to_all | solution.py:79
  41.4 6.8 %attention.1 = (bf16[16,2,128,256]{3,2,1,0:T(8,128)(2,1)}, f32[4,2,64,256]{3,2,1,0:T(8,128)S(1)}, bf16[4,2,64,256]{3,2,1,0:T(8,128)(2,1)S(1)}) custom-call(bf16[4,256,256]{2,1,0:T(8,128)(2,1)S(1)} %get-tuple-element.21.qt, bf16[4,256,256]{2,1,0:T(8,128)(2,1)} %get-tuple-element.22.cotangent, f32[4,8,256]{2,1,0:T(8,128)S(1)} %get-tuple-element.23.stat, ...), custom_call_target="tpu_custom_call" | custom-call | flops 5368709120 | bytes 8388608 | tf_op jit(solution)/shard_map/attention/pallas_call | solution.py:299
  48.2 10.4 %all-to-all-start.1 = ((bf16[16,2,128,256]{3,2,1,0:T(8,128)(2,1)}), bf16[16,2,128,256]{3,2,1,0:T(8,128)(2,1)S(1)}, u32[]{:S(2)}, u32[]{:S(2)}) async-start(bf16[16,2,128,256]{3,2,1,0:T(8,128)(2,1)} %get-tuple-element.25), calls=%async_computation.1 | async-start | bytes 4194304 | tf_op jit(solution)/shard_map/all_to_all | solution.py:79
  58.6 0.0 collective-permute-start.9
  58.6 1.5 %collective-permute-done.9.other = bf16[4,2,64,256]{3,2,1,0:T(8,128)(2,1)S(1)} collective-permute-done((bf16[4,2,64,256]{3,2,1,0:T(8,128)(2,1)S(1)}, bf16[4,2,64,256]{3,2,1,0:T(8,128)(2,1)S(1)}, u32[]{:S(2)}, u32[]{:S(2)}) %collective-permute-start.9) | collective-permute-done | bytes 262176 | tf_op jit(solution)/shard_map/ppermute | solution.py:364
  60.2 3.1 %collective-permute-start.10 = (bf16[2,64,256]{2,1,0:T(8,128)(2,1)S(1)}, bf16[2,64,256]{2,1,0:T(8,128)(2,1)S(1)}, u32[]{:S(2)}, u32[]{:S(2)}) collective-permute-start(bf16[2,64,256]{2,1,0:T(8,128)(2,1)S(1)} %get-tuple-element.28), channel_id=1, source_target_pairs={{0,0},{2,1},{32,2},{34,3},{36,4},{38,5},{4,6},{6,7},{9,8},{11,9},{... | collective-permute-start | bytes 196616 | tf_op jit(solution)/shard_map/ppermute | solution.py:365
  63.3 5.2 %collective-permute-start.11 = (bf16[2,64,256]{2,1,0:T(8,128)(2,1)S(1)}, bf16[2,64,256]{2,1,0:T(8,128)(2,1)S(1)}, u32[]{:S(2)}, u32[]{:S(2)}) collective-permute-start(bf16[2,64,256]{2,1,0:T(8,128)(2,1)S(1)} %get-tuple-element.29), channel_id=1, source_target_pairs={{2,0},{32,1},{34,2},{0,3},{38,4},{4,5},{6,6},{36,7},{11,8},{41,9},... | collective-permute-start | bytes 196616 | tf_op jit(solution)/shard_map/ppermute | solution.py:365
  68.5 0.7 collective-permute-start.12
  69.2 6.5 %collective-permute-start.13 = (bf16[2,64,256]{2,1,0:T(8,128)(2,1)S(1)}, bf16[2,64,256]{2,1,0:T(8,128)(2,1)S(1)}, u32[]{:S(2)}, u32[]{:S(2)}) collective-permute-start(bf16[2,64,256]{2,1,0:T(8,128)(2,1)S(1)} %get-tuple-element.31), channel_id=1, source_target_pairs={{34,0},{0,1},{2,2},{32,3},{6,4},{36,5},{38,6},{4,7},{43,8},{9,9},{... | collective-permute-start | bytes 196616 | tf_op jit(solution)/shard_map/ppermute | solution.py:365
  75.6 0.0 collective-permute-done.10.refs_0_
  75.6 0.0 collective-permute-done.11.refs_1_
  75.7 0.0 collective-permute-done.12.refs_2_
  75.7 1.8 %collective-permute-done.13.refs_3_ = bf16[2,64,256]{2,1,0:T(8,128)(2,1)S(1)} collective-permute-done((bf16[2,64,256]{2,1,0:T(8,128)(2,1)S(1)}, bf16[2,64,256]{2,1,0:T(8,128)(2,1)S(1)}, u32[]{:S(2)}, u32[]{:S(2)}) %collective-permute-start.13) | collective-permute-done | bytes 65568 | tf_op jit(solution)/shard_map/ppermute | solution.py:365
  77.5 1.5 %collective-permute-start.14 = (bf16[64,256]{1,0:T(8,128)(2,1)S(1)}, bf16[64,256]{1,0:T(8,128)(2,1)S(1)}, u32[]{:S(2)}, u32[]{:S(2)}) collective-permute-start(bf16[64,256]{1,0:T(8,128)(2,1)S(1)} %get-tuple-element.33), channel_id=1, source_target_pairs={{0,8},{8,0},{16,24},{24,16},{1,9},{9,1},{17,25},{25,17},{2,10},{10... | collective-permute-start | bytes 98312 | tf_op jit(solution)/shard_map/ppermute | solution.py:367
  79.0 6.8 %collective-permute-done.14.other = bf16[64,256]{1,0:T(8,128)(2,1)S(1)} collective-permute-done((bf16[64,256]{1,0:T(8,128)(2,1)S(1)}, bf16[64,256]{1,0:T(8,128)(2,1)S(1)}, u32[]{:S(2)}, u32[]{:S(2)}) %collective-permute-start.14) | collective-permute-done | bytes 32800 | tf_op jit(solution)/shard_map/ppermute | solution.py:367
  85.8 0.0 all-to-all-done.1.chunks
  85.8 1.7 %join.1 = (bf16[128,4096]{1,0:T(8,128)(2,1)}, bf16[128,4096]{1,0:T(8,128)(2,1)}, bf16[64,256]{1,0:T(8,128)(2,1)}) custom-call(bf16[16,2,128,256]{3,2,1,0:T(8,128)(2,1)S(1)} %all-to-all-done.1.chunks, f32[64,256]{1,0:T(8,128)S(1)} %get-tuple-element.32.own, bf16[64,256]{1,0:T(8,128)(2,1)S(1)} %collective-permute-done.14.other), custom_call_target="tpu_custom_call" | custom-call | tf_op jit(solution)/shard_map/join/pallas_call | solution.py:211
  (3 shorter events, 0.1 us)
Async XLA Ops:
  1.5 5.0 %collective-permute-start = (bf16[144,256]{1,0:T(8,128)(2,1)S(1)}, bf16[144,256]{1,0:T(8,128)(2,1)S(1)}, u32[]{:S(2)}, u32[]{:S(2)}) collective-permute-start(bf16[144,256]{1,0:T(8,128)(2,1)S(1)} %message.1.own), channel_id=1, source_target_pairs={{0,8},{8,0},{16,24},{24,16},{1,9},{9,1},{17,25},{25,17},{2,10},{10... | collective-permute-start | bytes 221192 | tf_op jit(solution)/shard_map/ppermute | solution.py:355
  6.5 34.9 %all-to-all-start = ((bf16[16,2,128,256]{3,2,1,0:T(8,128)(2,1)}), bf16[16,2,128,256]{3,2,1,0:T(8,128)(2,1)S(1)}, u32[]{:S(2)}, u32[]{:S(2)}) async-start(bf16[16,2,128,256]{3,2,1,0:T(8,128)(2,1)} %split.1), calls=%async_computation | async-start | bytes 4194304 | tf_op jit(solution)/shard_map/all_to_all | solution.py:79
  15.2 19.1 %collective-permute-start.4 = (bf16[272,256]{1,0:T(8,128)(2,1)S(1)}, bf16[272,256]{1,0:T(8,128)(2,1)S(1)}, u32[]{:S(2)}, u32[]{:S(2)}) collective-permute-start(bf16[272,256]{1,0:T(8,128)(2,1)S(1)} %bundle.1), channel_id=1, source_target_pairs={{0,34},{1,0},{2,2},{3,32},{4,6},{5,36},{6,38},{7,4},{8,43},{9,9},{... | collective-permute-start | bytes 417800 | tf_op jit(solution)/shard_map/ppermute | solution.py:360
  20.1 14.3 %collective-permute-start.3 = (bf16[272,256]{1,0:T(8,128)(2,1)S(1)}, bf16[272,256]{1,0:T(8,128)(2,1)S(1)}, u32[]{:S(2)}, u32[]{:S(2)}) collective-permute-start(bf16[272,256]{1,0:T(8,128)(2,1)S(1)} %bundle.1), channel_id=1, source_target_pairs={{0,32},{1,34},{2,0},{3,2},{4,4},{5,6},{6,36},{7,38},{8,41},{9,43},... | collective-permute-start | bytes 417800 | tf_op jit(solution)/shard_map/ppermute | solution.py:360
  20.8 14.1 %collective-permute-start.2 = (bf16[272,256]{1,0:T(8,128)(2,1)S(1)}, bf16[272,256]{1,0:T(8,128)(2,1)S(1)}, u32[]{:S(2)}, u32[]{:S(2)}) collective-permute-start(bf16[272,256]{1,0:T(8,128)(2,1)S(1)} %bundle.1), channel_id=1, source_target_pairs={{0,2},{1,32},{2,34},{3,0},{4,38},{5,4},{6,6},{7,36},{8,11},{9,41},... | collective-permute-start | bytes 417800 | tf_op jit(solution)/shard_map/ppermute | solution.py:360
  27.7 9.8 %collective-permute-start.1 = (bf16[272,256]{1,0:T(8,128)(2,1)S(1)}, bf16[272,256]{1,0:T(8,128)(2,1)S(1)}, u32[]{:S(2)}, u32[]{:S(2)}) collective-permute-start(bf16[272,256]{1,0:T(8,128)(2,1)S(1)} %bundle.1), channel_id=1, source_target_pairs={{0,0},{1,2},{2,32},{3,34},{4,36},{5,38},{6,4},{7,6},{8,9},{9,11},{... | collective-permute-start | bytes 417800 | tf_op jit(solution)/shard_map/ppermute | solution.py:360
  34.2 3.2 %collective-permute-start.8 = (bf16[272,256]{1,0:T(8,128)(2,1)S(1)}, bf16[272,256]{1,0:T(8,128)(2,1)S(1)}, u32[]{:S(2)}, u32[]{:S(2)}) collective-permute-start(bf16[272,256]{1,0:T(8,128)(2,1)S(1)} %collective-permute-done.4.refs_3_), channel_id=1, source_target_pairs={{0,4},{4,0},{1,5},{5,1},{2,6},{6,2},{3,7},{7,3},{8,12},{12,8},{9,1... | collective-permute-start | bytes 417800 | tf_op jit(solution)/shard_map/ppermute | solution.py:361
  34.4 3.1 %collective-permute-start.7 = (bf16[272,256]{1,0:T(8,128)(2,1)S(1)}, bf16[272,256]{1,0:T(8,128)(2,1)S(1)}, u32[]{:S(2)}, u32[]{:S(2)}) collective-permute-start(bf16[272,256]{1,0:T(8,128)(2,1)S(1)} %collective-permute-done.3.refs_2_), channel_id=1, source_target_pairs={{0,4},{4,0},{1,5},{5,1},{2,6},{6,2},{3,7},{7,3},{8,12},{12,8},{9,1... | collective-permute-start | bytes 417800 | tf_op jit(solution)/shard_map/ppermute | solution.py:361
  34.8 3.1 %collective-permute-start.6 = (bf16[272,256]{1,0:T(8,128)(2,1)S(1)}, bf16[272,256]{1,0:T(8,128)(2,1)S(1)}, u32[]{:S(2)}, u32[]{:S(2)}) collective-permute-start(bf16[272,256]{1,0:T(8,128)(2,1)S(1)} %collective-permute-done.2.refs_1_), channel_id=1, source_target_pairs={{0,4},{4,0},{1,5},{5,1},{2,6},{6,2},{3,7},{7,3},{8,12},{12,8},{9,1... | collective-permute-start | bytes 417800 | tf_op jit(solution)/shard_map/ppermute | solution.py:361
  37.5 1.4 %collective-permute-start.5 = (bf16[272,256]{1,0:T(8,128)(2,1)S(1)}, bf16[272,256]{1,0:T(8,128)(2,1)S(1)}, u32[]{:S(2)}, u32[]{:S(2)}) collective-permute-start(bf16[272,256]{1,0:T(8,128)(2,1)S(1)} %collective-permute-done.1.refs_0_), channel_id=1, source_target_pairs={{0,4},{4,0},{1,5},{5,1},{2,6},{6,2},{3,7},{7,3},{8,12},{12,8},{9,1... | collective-permute-start | bytes 417800 | tf_op jit(solution)/shard_map/ppermute | solution.py:361
  48.2 37.6 %all-to-all-start.1 = ((bf16[16,2,128,256]{3,2,1,0:T(8,128)(2,1)}), bf16[16,2,128,256]{3,2,1,0:T(8,128)(2,1)S(1)}, u32[]{:S(2)}, u32[]{:S(2)}) async-start(bf16[16,2,128,256]{3,2,1,0:T(8,128)(2,1)} %get-tuple-element.25), calls=%async_computation.1 | async-start | bytes 4194304 | tf_op jit(solution)/shard_map/all_to_all | solution.py:79
  58.6 1.5 %collective-permute-start.9 = (bf16[4,2,64,256]{3,2,1,0:T(8,128)(2,1)S(1)}, bf16[4,2,64,256]{3,2,1,0:T(8,128)(2,1)S(1)}, u32[]{:S(2)}, u32[]{:S(2)}) collective-permute-start(bf16[4,2,64,256]{3,2,1,0:T(8,128)(2,1)S(1)} %get-tuple-element.27), channel_id=1, source_target_pairs={{0,4},{4,0},{1,5},{5,1},{2,6},{6,2},{3,7},{7,3},{8,12},{12,8},{9,1... | collective-permute-start | bytes 786440 | tf_op jit(solution)/shard_map/ppermute | solution.py:364
  60.2 15.5 %collective-permute-start.10 = (bf16[2,64,256]{2,1,0:T(8,128)(2,1)S(1)}, bf16[2,64,256]{2,1,0:T(8,128)(2,1)S(1)}, u32[]{:S(2)}, u32[]{:S(2)}) collective-permute-start(bf16[2,64,256]{2,1,0:T(8,128)(2,1)S(1)} %get-tuple-element.28), channel_id=1, source_target_pairs={{0,0},{2,1},{32,2},{34,3},{36,4},{38,5},{4,6},{6,7},{9,8},{11,9},{... | collective-permute-start | bytes 196616 | tf_op jit(solution)/shard_map/ppermute | solution.py:365
  63.3 12.4 %collective-permute-start.11 = (bf16[2,64,256]{2,1,0:T(8,128)(2,1)S(1)}, bf16[2,64,256]{2,1,0:T(8,128)(2,1)S(1)}, u32[]{:S(2)}, u32[]{:S(2)}) collective-permute-start(bf16[2,64,256]{2,1,0:T(8,128)(2,1)S(1)} %get-tuple-element.29), channel_id=1, source_target_pairs={{2,0},{32,1},{34,2},{0,3},{38,4},{4,5},{6,6},{36,7},{11,8},{41,9},... | collective-permute-start | bytes 196616 | tf_op jit(solution)/shard_map/ppermute | solution.py:365
  68.5 7.2 %collective-permute-start.12 = (bf16[2,64,256]{2,1,0:T(8,128)(2,1)S(1)}, bf16[2,64,256]{2,1,0:T(8,128)(2,1)S(1)}, u32[]{:S(2)}, u32[]{:S(2)}) collective-permute-start(bf16[2,64,256]{2,1,0:T(8,128)(2,1)S(1)} %get-tuple-element.30), channel_id=1, source_target_pairs={{32,0},{34,1},{0,2},{2,3},{4,4},{6,5},{36,6},{38,7},{41,8},{43,9},... | collective-permute-start | bytes 196616 | tf_op jit(solution)/shard_map/ppermute | solution.py:365
  69.2 8.3 %collective-permute-start.13 = (bf16[2,64,256]{2,1,0:T(8,128)(2,1)S(1)}, bf16[2,64,256]{2,1,0:T(8,128)(2,1)S(1)}, u32[]{:S(2)}, u32[]{:S(2)}) collective-permute-start(bf16[2,64,256]{2,1,0:T(8,128)(2,1)S(1)} %get-tuple-element.31), channel_id=1, source_target_pairs={{34,0},{0,1},{2,2},{32,3},{6,4},{36,5},{38,6},{4,7},{43,8},{9,9},{... | collective-permute-start | bytes 196616 | tf_op jit(solution)/shard_map/ppermute | solution.py:365
  77.5 8.3 %collective-permute-start.14 = (bf16[64,256]{1,0:T(8,128)(2,1)S(1)}, bf16[64,256]{1,0:T(8,128)(2,1)S(1)}, u32[]{:S(2)}, u32[]{:S(2)}) collective-permute-start(bf16[64,256]{1,0:T(8,128)(2,1)S(1)} %get-tuple-element.33), channel_id=1, source_target_pairs={{0,8},{8,0},{16,24},{24,16},{1,9},{9,1},{17,25},{25,17},{2,10},{10... | collective-permute-start | bytes 98312 | tf_op jit(solution)/shard_map/ppermute | solution.py:367

commit v6 on v5

--- a/solution.py
+++ b/solution.py
@@ -39,24 +39,17 @@
     return jax.ShapeDtypeStruct(dims, dtype)
 
 
-LINE = ("zh", "x", "core", "zl")
-
-
-def line_pairs(k):
-    pairs = []
-    for zh in range(2):
-        for x in range(4):
-            for core in range(2):
-                for zl in range(4):
-                    z = 2 * ((zl + k + 2 * core) % 4) + (zh + x) % 2
-                    to = ((z // 4 * 4 + x) * 2 + core) * 4 + z % 4
-                    pairs.append((((zh * 4 + x) * 2 + core) * 4 + zl, to))
-    return pairs
-
-
-def row_block(k, core):
-    step = 2 * lax.axis_index("zh") + lax.axis_index("zl") // 2
-    return (step + 4 - k + 2 * core) % 4
+LINE = ("zh", "x", "zl")
+MIRROR = [
+    ((zh * 4 + x) * 4 + zl, ((1 - zh) * 4 + x) * 4 + 3 - zl)
+    for zh in range(2)
+    for x in (1, 3)
+    for zl in range(4)
+]
+
+
+def turn(k):
+    return [(i, i ^ k) for i in range(4)]
 
 
 NEXT = [(0, 1), (1, 0), (2, 3), (3, 2)]
@@ -79,10 +72,6 @@
     return lax.all_to_all(
         chunks, AXES, split_axis=0, concat_axis=0, tiled=True, axis_index_groups=groups
     )
-
-
-def inverse(pairs):
-    return [(b, a) for a, b in pairs]
 
 
 def pieces(value):
@@ -156,7 +145,7 @@
 
 def slot_columns(s):
     y, x = peer(s, lax.axis_index("core"))
-    zh = (lax.axis_index("zl") + x) % 2
+    zh = (lax.axis_index("zh") + x) % 2
     return pl.ds(pl.multiple_of((4 * y + 2 * zh + x // 2) * DH, DH), DH)
 
 
@@ -198,7 +187,7 @@
 
 
 def join_kernel(chunks, own, other, keys, values, queries):
-    queries[...] = (own[...] + other[...].astype(F32)).astype(BF16)
+    queries[...] = (own[...].astype(F32) + other[...].astype(F32)).astype(BF16)
     for s in range(16):
         columns = slot_columns(s)
         keys[:, columns] = chunks[s, 0]
@@ -221,14 +210,14 @@
     mine, theirs, (qt, out, stat, dt, sem) = refs[:4], refs[4:8], refs[8:]
     core = lax.axis_index("core")
     for k in range(4):
-        for ref, c in ((mine[k], core), (theirs[(k + 2) % 4], 1 - core)):
-            zl = row_block(k, core)
+        zl = k
+        for ref, c in ((mine[k], core), (theirs[k], 1 - core)):
             for xl in range(2):
                 to = pl.ds(pl.multiple_of((2 * xl + c) * PART, PART), PART)
                 qt[zl, to, :] = ref[xl * PART : (xl + 1) * PART, :]
                 dt[zl, to, :] = ref[(2 + xl) * PART : (3 + xl) * PART, :]
         one = mine[k][4 * PART :, :].astype(F32)
-        both = one + theirs[(k + 2) % 4][4 * PART :, :].astype(F32)
+        both = one + theirs[k][4 * PART :, :].astype(F32)
         stat[zl, 0:1, :] = both[0:1] + both[1:2] + both[2:3]
         stat[zl, 1:2, :] = (one[3:4] + one[4:5] + one[5:6]) * LOG2E
     copy = pltpu.make_async_copy(dt, out, sem)
@@ -284,12 +273,12 @@
     for zl in range(4):
         dq[zl] = dot(keys, ds[zl], 0, 0) * FACTOR
     for k in range(4):
-        zl = row_block(k, core)
+        zl = k
         for xl in range(2):
             at = pl.ds(pl.multiple_of((2 * xl + core) * PART, PART), PART)
             own[k, xl] = dq[zl, at, :]
             at = pl.ds(pl.multiple_of((2 * xl + 1 - core) * PART, PART), PART)
-            other[(k + 2) % 4, xl] = dq[zl, at, :].astype(BF16)
+            other[k, xl] = dq[zl, at, :].astype(BF16)
     for copy in writes:
         copy.wait()
 
@@ -336,18 +325,51 @@
 
 
 def line_sum_kernel(*refs):
-    parts, own, other = refs[:4], refs[4], refs[5]
+    total = refs[0][...].astype(F32)
+    for part in refs[1:4]:
+        total = total + part[...].astype(F32)
+    refs[4][...] = total.astype(BF16)
+
+
+def line_sum(parts):
+    out = shape(2, PART, ROWS)
+    return call(line_sum_kernel, out, [VMEM] * 4, VMEM, 4, "line_sum")(*parts)
+
+
+def pick_kernel(kept, crossed, own, other):
     odd = lax.rem(lax.axis_index("x"), 2)
-    for out, place in ((own, odd), (other, 1 - odd)):
-        total = parts[0][place].astype(F32)
-        for part in parts[1:]:
-            total = total + part[place].astype(F32)
-        out[...] = total.astype(out.dtype)
-
-
-def line_sum(parts):
-    outs = [shape(PART, ROWS, dtype=F32), shape(PART, ROWS)]
-    return call(line_sum_kernel, outs, [VMEM] * 4, [VMEM] * 2, 4, "line_sum")(*parts)
+
+    @pl.when(odd == 0)
+    def _():
+        own[...] = kept[0]
+        other[...] = kept[1]
+
+    @pl.when(odd == 1)
+    def _():
+        own[...] = crossed[1]
+        other[...] = crossed[0]
+
+
+def pick(kept, crossed):
+    outs = [shape(PART, ROWS)] * 2
+    return call(pick_kernel, outs, [VMEM] * 2, [VMEM] * 2, 4, "pick")(kept, crossed)
+
+
+def choose_kernel(kept, crossed, out):
+    odd = lax.rem(lax.axis_index("x"), 2)
+
+    @pl.when(odd == 0)
+    def _():
+        out[...] = kept[...]
+
+    @pl.when(odd == 1)
+    def _():
+        out[...] = crossed[...]
+
+
+def choose(kept, crossed):
+    out = shape(*kept.shape)
+    return call(choose_kernel, out, [VMEM] * 2, VMEM, 4, "choose")(kept, crossed)
 
 
 def local(queries, outputs, cotangent, log_norms, memory_keys, memory_values):
@@ -357,13 +379,15 @@
     chunks, other = lax.optimization_barrier((chunks, other))
     received = exchange(chunks)
     part = bundle(message, other)
-    mine = [lax.ppermute(part, LINE, line_pairs(k)) for k in range(4)]
+    part = choose(part, lax.ppermute(part, LINE, MIRROR))
+    mine = [part] + [lax.ppermute(part, "zl", turn(k)) for k in (1, 2, 3)]
     theirs = [lax.ppermute(part, "core", SWAP) for part in mine]
     grads, own, other = attention(*assemble(mine, theirs), received)
     returned = exchange(grads)
     sums = core_sum(own, lax.ppermute(other, "core", SWAP))
-    sums = [lax.ppermute(sums[k], LINE, inverse(line_pairs(k))) for k in range(4)]
-    own, other = line_sum(sums)
+    sums = [sums[0]] + [lax.ppermute(sums[k], "zl", turn(k)) for k in (1, 2, 3)]
+    total = line_sum(sums)
+    own, other = pick(total, lax.ppermute(total, LINE, MIRROR))
     other = lax.ppermute(other, "x", NEXT)
     key_grads, value_grads, query_grads = join(returned, own, other)
     return query_grads.T, key_grads, value_grads

time: 88 us -> 87.7 us (level)
  starting transfers between devices: 59.9 us -> 36.3 us
  waiting for transfers between devices: 13.6 us -> 36.8 us
    ppermute x8, starting transfers between devices: 34.4 us -> 9.77 us  [the longest x3 4.81 us: local(): mine = [part] + [lax.ppermute(part, 'zl', turn(k)) for k in (1, 2, 3)]]
    ppermute x8, waiting for transfers between devices: 2.33 us -> 15.2 us  [the longest x3 11.1 us: local(): mine = [part] + [lax.ppermute(part, 'zl', turn(k)) for k in (1, 2, 3)]]
    all_to_all x2, waiting for transfers between devices: 1.6 us -> 7.3 us  [exchange(): lax.all_to_all(chunks, AXES, split_axis=0, concat_axis=0, tiled=True, axi...]
    ppermute x1, waiting for transfers between devices: 6.75 us -> 11.8 us  [local(): other = lax.ppermute(other, 'x', NEXT)]
    ppermute x1, starting transfers between devices: 1.55 us -> 5.79 us  [local(): other = lax.ppermute(other, 'x', NEXT)]
    ppermute x4, starting transfers between devices: 2.66 us -> 0.52 us  [local(): theirs = [lax.ppermute(part, 'core', SWAP) for part in mine]]
    all_to_all x2, starting transfers between devices: 19.1 us -> 18.1 us  [exchange(): lax.all_to_all(chunks, AXES, split_axis=0, concat_axis=0, tiled=True, axi...]
  transfers between devices with their start and end apart: 17 -> 17, of which waited for: 7 -> 10; matrix products, arithmetic and copies ran while one was open for 0% -> 0% of each run, Pallas kernels for 4% -> 4%
where the time goes in v6:
time: 87.7 us; the launch traced here: 87.3 us
  waiting for transfers between devices  36.8 us (42%)
  starting transfers between devices  36.3 us (41%)
  Pallas kernels  13.3 us (15%)
    all_to_all x2, starting transfers between devices, exchange(): lax.all_to_all(chunks, AXES, split_axis=0, concat_axis=0, tiled=True, axi...  18.1 us
    ppermute x1, waiting for transfers between devices, local(): other = lax.ppermute(other, 'x', NEXT)  11.8 us
    ppermute x3, waiting for transfers between devices, local(): mine = [part] + [lax.ppermute(part, 'zl', turn(k)) for k in (1, 2, 3)]  11.1 us
    all_to_all x2, waiting for transfers between devices, exchange(): lax.all_to_all(chunks, AXES, split_axis=0, concat_axis=0, tiled=True, axi...  7.3 us
    pallas_call x1, Pallas kernels, attention(): call(attention_kernel, [pltpu.HBM((16, 2, KEYS, DH), BF16), shape(*part,...  6.94 us
    ppermute x1, starting transfers between devices, local(): other = lax.ppermute(other, 'x', NEXT)  5.79 us
    ppermute x3, starting transfers between devices, local(): mine = [part] + [lax.ppermute(part, 'zl', turn(k)) for k in (1, 2, 3)]  4.81 us
    ppermute x3, waiting for transfers between devices, local(): sums = [sums[0]] + [lax.ppermute(sums[k], 'zl', turn(k)) for k in (1, 2, 3)]  4.1 us
  transfers between devices with their start and end apart: 17, of which 10 were waited for; matrix products, arithmetic and copies ran while one was open for 0% of the time, Pallas kernels for 4%

profile of v6, /device:TPU:1, one launch (start us, length us, event | category | flops | bytes accessed | tf_op | source)
XLA Modules:
  0.0 87.3 jit_solution(15249883838096775953)
XLA Ops:
  0.6 0.9 message.1.own
  1.5 2.1 %collective-permute-start = (bf16[144,256]{1,0:T(8,128)(2,1)S(1)}, bf16[144,256]{1,0:T(8,128)(2,1)S(1)}, u32[]{:S(2)}, u32[]{:S(2)}) collective-permute-start(bf16[144,256]{1,0:T(8,128)(2,1)S(1)} %message.1.own), channel_id=1, source_target_pairs={{0,8},{8,0},{16,24},{24,16},{1,9},{9,1},{17,25},{25,17},{2,10},{10... | collective-permute-start | bytes 221192 | tf_op jit(solution)/shard_map/ppermute | solution.py:377
  3.6 2.8 %split.1 = bf16[16,2,128,256]{3,2,1,0:T(8,128)(2,1)} custom-call(bf16[128,4096]{1,0:T(8,128)(2,1)} %keys.1, bf16[128,4096]{1,0:T(8,128)(2,1)} %values.1), custom_call_target="tpu_custom_call" | custom-call | bytes 8388608 | tf_op jit(solution)/shard_map/split/pallas_call | solution.py:173
  6.5 0.0 collective-permute-done.other
  6.5 8.7 %all-to-all-start = ((bf16[16,2,128,256]{3,2,1,0:T(8,128)(2,1)}), bf16[16,2,128,256]{3,2,1,0:T(8,128)(2,1)S(1)}, u32[]{:S(2)}, u32[]{:S(2)}) async-start(bf16[16,2,128,256]{3,2,1,0:T(8,128)(2,1)} %split.1), calls=%async_computation | async-start | bytes 4194304 | tf_op jit(solution)/shard_map/all_to_all | solution.py:72
  15.2 0.7 collective-permute-start.1
  15.8 0.0 collective-permute-done.1.crossed
  15.9 4.4 %collective-permute-start.4 = (bf16[272,256]{1,0:T(8,128)(2,1)S(1)}, bf16[272,256]{1,0:T(8,128)(2,1)S(1)}, u32[]{:S(2)}, u32[]{:S(2)}) collective-permute-start(bf16[272,256]{1,0:T(8,128)(2,1)S(1)} %choose.1.refs_0_), channel_id=1, source_target_pairs={{0,3},{1,2},{2,1},{3,0},{4,7},{5,6},{6,5},{7,4},{8,11},{9,10},{10,... | collective-permute-start | bytes 417800 | tf_op jit(solution)/shard_map/ppermute | solution.py:383
  20.3 0.0 collective-permute-start.3
  20.3 0.4 collective-permute-start.2
  20.7 0.0 collective-permute-start.5
  20.7 3.8 %collective-permute-done.4.refs_3_ = bf16[272,256]{1,0:T(8,128)(2,1)S(1)} collective-permute-done((bf16[272,256]{1,0:T(8,128)(2,1)S(1)}, bf16[272,256]{1,0:T(8,128)(2,1)S(1)}, u32[]{:S(2)}, u32[]{:S(2)}) %collective-permute-start.4) | collective-permute-done | bytes 139296 | tf_op jit(solution)/shard_map/ppermute | solution.py:383
  24.5 0.0 collective-permute-start.8
  24.5 7.3 %collective-permute-done.3.refs_2_ = bf16[272,256]{1,0:T(8,128)(2,1)S(1)} collective-permute-done((bf16[272,256]{1,0:T(8,128)(2,1)S(1)}, bf16[272,256]{1,0:T(8,128)(2,1)S(1)}, u32[]{:S(2)}, u32[]{:S(2)}) %collective-permute-start.3) | collective-permute-done | bytes 139296 | tf_op jit(solution)/shard_map/ppermute | solution.py:383
  31.8 0.1 collective-permute-start.7
  31.9 0.0 collective-permute-done.2.refs_1_
  31.9 0.4 collective-permute-start.6
  32.3 0.0 collective-permute-done.5.refs_4_
  32.3 0.0 collective-permute-done.8.refs_7_
  32.3 0.8 collective-permute-done.7.refs_6_
  33.2 0.2 collective-permute-done.6.refs_5_
  33.4 0.9 %assemble.1 = (bf16[4,256,256]{2,1,0:T(8,128)(2,1)S(1)}, bf16[4,256,256]{2,1,0:T(8,128)(2,1)}, f32[4,8,256]{2,1,0:T(8,128)S(1)}) custom-call(bf16[272,256]{1,0:T(8,128)(2,1)S(1)} %choose.1.refs_0_, bf16[272,256]{1,0:T(8,128)(2,1)S(1)} %collective-permute-done.2.refs_1_, bf16[272,256]{1,0:T(8,128)(2,1)S(1)} %collective-permute-done.3.refs_2_, ...), custom_call_target="tpu_custom_call" | custom-call | tf_op jit(solution)/shard_map/assemble/pallas_call | solution.py:230
  34.2 7.1 %all-to-all-done.kv = bf16[16,2,128,256]{3,2,1,0:T(8,128)(2,1)S(1)} async-done(((bf16[16,2,128,256]{3,2,1,0:T(8,128)(2,1)}), bf16[16,2,128,256]{3,2,1,0:T(8,128)(2,1)S(1)}, u32[]{:S(2)}, u32[]{:S(2)}) %all-to-all-start) | async-done | bytes 2097184 | tf_op jit(solution)/shard_map/all_to_all | solution.py:72
  41.4 6.9 %attention.1 = (bf16[16,2,128,256]{3,2,1,0:T(8,128)(2,1)}, f32[4,2,64,256]{3,2,1,0:T(8,128)S(1)}, bf16[4,2,64,256]{3,2,1,0:T(8,128)(2,1)S(1)}) custom-call(bf16[4,256,256]{2,1,0:T(8,128)(2,1)S(1)} %get-tuple-element.21.qt, bf16[4,256,256]{2,1,0:T(8,128)(2,1)} %get-tuple-element.22.cotangent, f32[4,8,256]{2,1,0:T(8,128)S(1)} %get-tuple-element.23.stat, ...), custom_call_target="tpu_custom_call" | custom-call | flops 5368709120 | bytes 8388608 | tf_op jit(solution)/shard_map/attention/pallas_call | solution.py:288
  48.3 9.5 %all-to-all-start.1 = ((bf16[16,2,128,256]{3,2,1,0:T(8,128)(2,1)}), bf16[16,2,128,256]{3,2,1,0:T(8,128)(2,1)S(1)}, u32[]{:S(2)}, u32[]{:S(2)}) async-start(bf16[16,2,128,256]{3,2,1,0:T(8,128)(2,1)} %get-tuple-element.25), calls=%async_computation.1 | async-start | bytes 4194304 | tf_op jit(solution)/shard_map/all_to_all | solution.py:72
  57.8 0.0 collective-permute-start.9
  57.8 1.5 %collective-permute-done.9.other = bf16[4,2,64,256]{3,2,1,0:T(8,128)(2,1)S(1)} collective-permute-done((bf16[4,2,64,256]{3,2,1,0:T(8,128)(2,1)S(1)}, bf16[4,2,64,256]{3,2,1,0:T(8,128)(2,1)S(1)}, u32[]{:S(2)}, u32[]{:S(2)}) %collective-permute-start.9) | collective-permute-done | bytes 262176 | tf_op jit(solution)/shard_map/ppermute | solution.py:387
  59.4 0.1 collective-permute-start.10
  59.5 2.4 %collective-permute-start.11 = (bf16[2,64,256]{2,1,0:T(8,128)(2,1)S(1)}, bf16[2,64,256]{2,1,0:T(8,128)(2,1)S(1)}, u32[]{:S(2)}, u32[]{:S(2)}) collective-permute-start(bf16[2,64,256]{2,1,0:T(8,128)(2,1)S(1)} %get-tuple-element.30), channel_id=1, source_target_pairs={{0,2},{1,3},{2,0},{3,1},{4,6},{5,7},{6,4},{7,5},{8,10},{9,11},{10,... | collective-permute-start | bytes 196616 | tf_op jit(solution)/shard_map/ppermute | solution.py:388
  61.9 1.1 %collective-permute-start.12 = (bf16[2,64,256]{2,1,0:T(8,128)(2,1)S(1)}, bf16[2,64,256]{2,1,0:T(8,128)(2,1)S(1)}, u32[]{:S(2)}, u32[]{:S(2)}) collective-permute-start(bf16[2,64,256]{2,1,0:T(8,128)(2,1)S(1)} %get-tuple-element.31), channel_id=1, source_target_pairs={{0,3},{1,2},{2,1},{3,0},{4,7},{5,6},{6,5},{7,4},{8,11},{9,10},{10,... | collective-permute-start | bytes 196616 | tf_op jit(solution)/shard_map/ppermute | solution.py:388
  63.0 0.0 collective-permute-done.10.refs_1_
  63.0 1.0 %collective-permute-done.11.refs_2_ = bf16[2,64,256]{2,1,0:T(8,128)(2,1)S(1)} collective-permute-done((bf16[2,64,256]{2,1,0:T(8,128)(2,1)S(1)}, bf16[2,64,256]{2,1,0:T(8,128)(2,1)S(1)}, u32[]{:S(2)}, u32[]{:S(2)}) %collective-permute-start.11) | collective-permute-done | bytes 65568 | tf_op jit(solution)/shard_map/ppermute | solution.py:388
  64.0 3.1 %collective-permute-done.12.refs_3_ = bf16[2,64,256]{2,1,0:T(8,128)(2,1)S(1)} collective-permute-done((bf16[2,64,256]{2,1,0:T(8,128)(2,1)S(1)}, bf16[2,64,256]{2,1,0:T(8,128)(2,1)S(1)}, u32[]{:S(2)}, u32[]{:S(2)}) %collective-permute-start.12) | collective-permute-done | bytes 65568 | tf_op jit(solution)/shard_map/ppermute | solution.py:388
  67.1 0.7 collective-permute-start.13
  67.8 0.0 collective-permute-done.13.crossed
  67.9 5.8 %collective-permute-start.14 = (bf16[64,256]{1,0:T(8,128)(2,1)S(1)}, bf16[64,256]{1,0:T(8,128)(2,1)S(1)}, u32[]{:S(2)}, u32[]{:S(2)}) collective-permute-start(bf16[64,256]{1,0:T(8,128)(2,1)S(1)} %get-tuple-element.33), channel_id=1, source_target_pairs={{0,8},{8,0},{16,24},{24,16},{1,9},{9,1},{17,25},{25,17},{2,10},{10... | collective-permute-start | bytes 98312 | tf_op jit(solution)/shard_map/ppermute | solution.py:391
  73.6 11.8 %collective-permute-done.14.other = bf16[64,256]{1,0:T(8,128)(2,1)S(1)} collective-permute-done((bf16[64,256]{1,0:T(8,128)(2,1)S(1)}, bf16[64,256]{1,0:T(8,128)(2,1)S(1)}, u32[]{:S(2)}, u32[]{:S(2)}) %collective-permute-start.14) | collective-permute-done | bytes 32800 | tf_op jit(solution)/shard_map/ppermute | solution.py:391
  85.4 0.2 all-to-all-done.1.chunks
  85.6 1.7 %join.1 = (bf16[128,4096]{1,0:T(8,128)(2,1)}, bf16[128,4096]{1,0:T(8,128)(2,1)}, bf16[64,256]{1,0:T(8,128)(2,1)}) custom-call(bf16[16,2,128,256]{3,2,1,0:T(8,128)(2,1)S(1)} %all-to-all-done.1.chunks, bf16[64,256]{1,0:T(8,128)(2,1)S(1)} %get-tuple-element.32.own, bf16[64,256]{1,0:T(8,128)(2,1)S(1)} %collective-permute-done.14.other), custom_call_target="tpu_custom_call" | custom-call | tf_op jit(solution)/shard_map/join/pallas_call | solution.py:200
  (5 shorter events, 0.2 us)
Async XLA Ops:
  1.5 5.0 %collective-permute-start = (bf16[144,256]{1,0:T(8,128)(2,1)S(1)}, bf16[144,256]{1,0:T(8,128)(2,1)S(1)}, u32[]{:S(2)}, u32[]{:S(2)}) collective-permute-start(bf16[144,256]{1,0:T(8,128)(2,1)S(1)} %message.1.own), channel_id=1, source_target_pairs={{0,8},{8,0},{16,24},{24,16},{1,9},{9,1},{17,25},{25,17},{2,10},{10... | collective-permute-start | bytes 221192 | tf_op jit(solution)/shard_map/ppermute | solution.py:377
  6.5 34.9 %all-to-all-start = ((bf16[16,2,128,256]{3,2,1,0:T(8,128)(2,1)}), bf16[16,2,128,256]{3,2,1,0:T(8,128)(2,1)S(1)}, u32[]{:S(2)}, u32[]{:S(2)}) async-start(bf16[16,2,128,256]{3,2,1,0:T(8,128)(2,1)} %split.1), calls=%async_computation | async-start | bytes 4194304 | tf_op jit(solution)/shard_map/all_to_all | solution.py:72
  15.2 0.7 collective-permute-start.1
  15.9 8.6 %collective-permute-start.4 = (bf16[272,256]{1,0:T(8,128)(2,1)S(1)}, bf16[272,256]{1,0:T(8,128)(2,1)S(1)}, u32[]{:S(2)}, u32[]{:S(2)}) collective-permute-start(bf16[272,256]{1,0:T(8,128)(2,1)S(1)} %choose.1.refs_0_), channel_id=1, source_target_pairs={{0,3},{1,2},{2,1},{3,0},{4,7},{5,6},{6,5},{7,4},{8,11},{9,10},{10,... | collective-permute-start | bytes 417800 | tf_op jit(solution)/shard_map/ppermute | solution.py:383
  20.3 11.5 %collective-permute-start.3 = (bf16[272,256]{1,0:T(8,128)(2,1)S(1)}, bf16[272,256]{1,0:T(8,128)(2,1)S(1)}, u32[]{:S(2)}, u32[]{:S(2)}) collective-permute-start(bf16[272,256]{1,0:T(8,128)(2,1)S(1)} %choose.1.refs_0_), channel_id=1, source_target_pairs={{0,2},{1,3},{2,0},{3,1},{4,6},{5,7},{6,4},{7,5},{8,10},{9,11},{10,... | collective-permute-start | bytes 417800 | tf_op jit(solution)/shard_map/ppermute | solution.py:383
  20.3 11.6 %collective-permute-start.2 = (bf16[272,256]{1,0:T(8,128)(2,1)S(1)}, bf16[272,256]{1,0:T(8,128)(2,1)S(1)}, u32[]{:S(2)}, u32[]{:S(2)}) collective-permute-start(bf16[272,256]{1,0:T(8,128)(2,1)S(1)} %choose.1.refs_0_), channel_id=1, source_target_pairs={{0,1},{1,0},{2,3},{3,2},{4,5},{5,4},{6,7},{7,6},{8,9},{9,8},{10,11... | collective-permute-start | bytes 417800 | tf_op jit(solution)/shard_map/ppermute | solution.py:383
  20.7 11.6 %collective-permute-start.5 = (bf16[272,256]{1,0:T(8,128)(2,1)S(1)}, bf16[272,256]{1,0:T(8,128)(2,1)S(1)}, u32[]{:S(2)}, u32[]{:S(2)}) collective-permute-start(bf16[272,256]{1,0:T(8,128)(2,1)S(1)} %choose.1.refs_0_), channel_id=1, source_target_pairs={{0,4},{4,0},{1,5},{5,1},{2,6},{6,2},{3,7},{7,3},{8,12},{12,8},{9,1... | collective-permute-start | bytes 417800 | tf_op jit(solution)/shard_map/ppermute | solution.py:384
  24.5 7.8 %collective-permute-start.8 = (bf16[272,256]{1,0:T(8,128)(2,1)S(1)}, bf16[272,256]{1,0:T(8,128)(2,1)S(1)}, u32[]{:S(2)}, u32[]{:S(2)}) collective-permute-start(bf16[272,256]{1,0:T(8,128)(2,1)S(1)} %collective-permute-done.4.refs_3_), channel_id=1, source_target_pairs={{0,4},{4,0},{1,5},{5,1},{2,6},{6,2},{3,7},{7,3},{8,12},{12,8},{9,1... | collective-permute-start | bytes 417800 | tf_op jit(solution)/shard_map/ppermute | solution.py:384
  31.8 1.4 %collective-permute-start.7 = (bf16[272,256]{1,0:T(8,128)(2,1)S(1)}, bf16[272,256]{1,0:T(8,128)(2,1)S(1)}, u32[]{:S(2)}, u32[]{:S(2)}) collective-permute-start(bf16[272,256]{1,0:T(8,128)(2,1)S(1)} %collective-permute-done.3.refs_2_), channel_id=1, source_target_pairs={{0,4},{4,0},{1,5},{5,1},{2,6},{6,2},{3,7},{7,3},{8,12},{12,8},{9,1... | collective-permute-start | bytes 417800 | tf_op jit(solution)/shard_map/ppermute | solution.py:384
  31.9 1.4 %collective-permute-start.6 = (bf16[272,256]{1,0:T(8,128)(2,1)S(1)}, bf16[272,256]{1,0:T(8,128)(2,1)S(1)}, u32[]{:S(2)}, u32[]{:S(2)}) collective-permute-start(bf16[272,256]{1,0:T(8,128)(2,1)S(1)} %collective-permute-done.2.refs_1_), channel_id=1, source_target_pairs={{0,4},{4,0},{1,5},{5,1},{2,6},{6,2},{3,7},{7,3},{8,12},{12,8},{9,1... | collective-permute-start | bytes 417800 | tf_op jit(solution)/shard_map/ppermute | solution.py:384
  48.3 37.3 %all-to-all-start.1 = ((bf16[16,2,128,256]{3,2,1,0:T(8,128)(2,1)}), bf16[16,2,128,256]{3,2,1,0:T(8,128)(2,1)S(1)}, u32[]{:S(2)}, u32[]{:S(2)}) async-start(bf16[16,2,128,256]{3,2,1,0:T(8,128)(2,1)} %get-tuple-element.25), calls=%async_computation.1 | async-start | bytes 4194304 | tf_op jit(solution)/shard_map/all_to_all | solution.py:72
  57.8 1.5 %collective-permute-start.9 = (bf16[4,2,64,256]{3,2,1,0:T(8,128)(2,1)S(1)}, bf16[4,2,64,256]{3,2,1,0:T(8,128)(2,1)S(1)}, u32[]{:S(2)}, u32[]{:S(2)}) collective-permute-start(bf16[4,2,64,256]{3,2,1,0:T(8,128)(2,1)S(1)} %get-tuple-element.27), channel_id=1, source_target_pairs={{0,4},{4,0},{1,5},{5,1},{2,6},{6,2},{3,7},{7,3},{8,12},{12,8},{9,1... | collective-permute-start | bytes 786440 | tf_op jit(solution)/shard_map/ppermute | solution.py:387
  59.4 3.6 %collective-permute-start.10 = (bf16[2,64,256]{2,1,0:T(8,128)(2,1)S(1)}, bf16[2,64,256]{2,1,0:T(8,128)(2,1)S(1)}, u32[]{:S(2)}, u32[]{:S(2)}) collective-permute-start(bf16[2,64,256]{2,1,0:T(8,128)(2,1)S(1)} %get-tuple-element.29), channel_id=1, source_target_pairs={{0,1},{1,0},{2,3},{3,2},{4,5},{5,4},{6,7},{7,6},{8,9},{9,8},{10,11... | collective-permute-start | bytes 196616 | tf_op jit(solution)/shard_map/ppermute | solution.py:388
  59.5 4.5 %collective-permute-start.11 = (bf16[2,64,256]{2,1,0:T(8,128)(2,1)S(1)}, bf16[2,64,256]{2,1,0:T(8,128)(2,1)S(1)}, u32[]{:S(2)}, u32[]{:S(2)}) collective-permute-start(bf16[2,64,256]{2,1,0:T(8,128)(2,1)S(1)} %get-tuple-element.30), channel_id=1, source_target_pairs={{0,2},{1,3},{2,0},{3,1},{4,6},{5,7},{6,4},{7,5},{8,10},{9,11},{10,... | collective-permute-start | bytes 196616 | tf_op jit(solution)/shard_map/ppermute | solution.py:388
  61.9 5.2 %collective-permute-start.12 = (bf16[2,64,256]{2,1,0:T(8,128)(2,1)S(1)}, bf16[2,64,256]{2,1,0:T(8,128)(2,1)S(1)}, u32[]{:S(2)}, u32[]{:S(2)}) collective-permute-start(bf16[2,64,256]{2,1,0:T(8,128)(2,1)S(1)} %get-tuple-element.31), channel_id=1, source_target_pairs={{0,3},{1,2},{2,1},{3,0},{4,7},{5,6},{6,5},{7,4},{8,11},{9,10},{10,... | collective-permute-start | bytes 196616 | tf_op jit(solution)/shard_map/ppermute | solution.py:388
  67.1 0.7 collective-permute-start.13
  67.9 17.6 %collective-permute-start.14 = (bf16[64,256]{1,0:T(8,128)(2,1)S(1)}, bf16[64,256]{1,0:T(8,128)(2,1)S(1)}, u32[]{:S(2)}, u32[]{:S(2)}) collective-permute-start(bf16[64,256]{1,0:T(8,128)(2,1)S(1)} %get-tuple-element.33), channel_id=1, source_target_pairs={{0,8},{8,0},{16,24},{24,16},{1,9},{9,1},{17,25},{25,17},{2,10},{10... | collective-permute-start | bytes 98312 | tf_op jit(solution)/shard_map/ppermute | solution.py:391

commit v7 on v6

--- a/solution.py
+++ b/solution.py
@@ -246,10 +246,10 @@
     read.start()
     read.wait()
     writes = []
-    for block in range(8):
-        rows = slice(block * 2 * KEYS, (block + 1) * 2 * KEYS)
-        keys = kv[2 * block : 2 * block + 2, 0].reshape(2 * KEYS, DH)
-        values = kv[2 * block : 2 * block + 2, 1].reshape(2 * KEYS, DH)
+    for block in range(4):
+        rows = slice(block * 4 * KEYS, (block + 1) * 4 * KEYS)
+        keys = kv[4 * block : 4 * block + 4, 0].reshape(4 * KEYS, DH)
+        values = kv[4 * block : 4 * block + 4, 1].reshape(4 * KEYS, DH)
         weights, slopes = [], []
         for zl in range(4):
             score = dot(keys, qt[zl], 1, 0)
@@ -261,12 +261,12 @@
             ds[zl, rows, :] = grad
         value_grad = sum(dot(weights[zl], dt[zl], 1, 1) for zl in range(4))
         key_grad = sum(dot(slopes[zl], qt[zl], 1, 1) for zl in range(4)) * FACTOR
-        for half in range(2):
-            part = slice(half * KEYS, (half + 1) * KEYS)
-            dkv[2 * block + half, 0] = key_grad[part].astype(BF16)
-            dkv[2 * block + half, 1] = value_grad[part].astype(BF16)
-        pair = slice(2 * block, 2 * block + 2)
-        copy = pltpu.make_async_copy(dkv.at[pair], grads.at[pair], sem.at[block])
+        for place in range(4):
+            part = slice(place * KEYS, (place + 1) * KEYS)
+            dkv[4 * block + place, 0] = key_grad[part].astype(BF16)
+            dkv[4 * block + place, 1] = value_grad[part].astype(BF16)
+        slots = slice(4 * block, 4 * block + 4)
+        copy = pltpu.make_async_copy(dkv.at[slots], grads.at[slots], sem.at[block])
         copy.start()
         writes.append(copy)
     keys = kv[:, 0].reshape(16 * KEYS, DH)

time: 87.7 us -> 87.7 us (level)
  no operation moved by 1% of the time
where the time goes in v7:
time: 87.7 us; the launch traced here: 87.2 us
  waiting for transfers between devices  36.9 us (42%)
  starting transfers between devices  36.3 us (41%)
  Pallas kernels  13.3 us (15%)
    all_to_all x2, starting transfers between devices, exchange(): lax.all_to_all(chunks, AXES, split_axis=0, concat_axis=0, tiled=True, axi...  18.1 us
    ppermute x1, waiting for transfers between devices, local(): other = lax.ppermute(other, 'x', NEXT)  11.8 us
    ppermute x3, waiting for transfers between devices, local(): mine = [part] + [lax.ppermute(part, 'zl', turn(k)) for k in (1, 2, 3)]  11.1 us
    all_to_all x2, waiting for transfers between devices, exchange(): lax.all_to_all(chunks, AXES, split_axis=0, concat_axis=0, tiled=True, axi...  7.3 us
    pallas_call x1, Pallas kernels, attention(): call(attention_kernel, [pltpu.HBM((16, 2, KEYS, DH), BF16), shape(*part,...  6.89 us
    ppermute x1, starting transfers between devices, local(): other = lax.ppermute(other, 'x', NEXT)  5.77 us
    ppermute x3, starting transfers between devices, local(): mine = [part] + [lax.ppermute(part, 'zl', turn(k)) for k in (1, 2, 3)]  4.81 us
    ppermute x3, waiting for transfers between devices, local(): sums = [sums[0]] + [lax.ppermute(sums[k], 'zl', turn(k)) for k in (1, 2, 3)]  4.12 us
  transfers between devices with their start and end apart: 17, of which 10 were waited for; matrix products, arithmetic and copies ran while one was open for 0% of the time, Pallas kernels for 4%

profile of v7, /device:TPU:1, one launch (start us, length us, event | category | flops | bytes accessed | tf_op | source)
XLA Modules:
  0.0 87.2 jit_solution(13102711516194458996)
XLA Ops:
  0.6 0.9 message.1.own
  1.5 2.1 %collective-permute-start = (bf16[144,256]{1,0:T(8,128)(2,1)S(1)}, bf16[144,256]{1,0:T(8,128)(2,1)S(1)}, u32[]{:S(2)}, u32[]{:S(2)}) collective-permute-start(bf16[144,256]{1,0:T(8,128)(2,1)S(1)} %message.1.own), channel_id=1, source_target_pairs={{0,8},{8,0},{16,24},{24,16},{1,9},{9,1},{17,25},{25,17},{2,10},{10... | collective-permute-start | bytes 221192 | tf_op jit(solution)/shard_map/ppermute | solution.py:377
  3.6 2.8 %split.1 = bf16[16,2,128,256]{3,2,1,0:T(8,128)(2,1)} custom-call(bf16[128,4096]{1,0:T(8,128)(2,1)} %keys.1, bf16[128,4096]{1,0:T(8,128)(2,1)} %values.1), custom_call_target="tpu_custom_call" | custom-call | bytes 8388608 | tf_op jit(solution)/shard_map/split/pallas_call | solution.py:173
  6.5 0.0 collective-permute-done.other
  6.5 8.7 %all-to-all-start = ((bf16[16,2,128,256]{3,2,1,0:T(8,128)(2,1)}), bf16[16,2,128,256]{3,2,1,0:T(8,128)(2,1)S(1)}, u32[]{:S(2)}, u32[]{:S(2)}) async-start(bf16[16,2,128,256]{3,2,1,0:T(8,128)(2,1)} %split.1), calls=%async_computation | async-start | bytes 4194304 | tf_op jit(solution)/shard_map/all_to_all | solution.py:72
  15.2 0.7 collective-permute-start.1
  15.8 0.0 collective-permute-done.1.crossed
  15.9 4.4 %collective-permute-start.4 = (bf16[272,256]{1,0:T(8,128)(2,1)S(1)}, bf16[272,256]{1,0:T(8,128)(2,1)S(1)}, u32[]{:S(2)}, u32[]{:S(2)}) collective-permute-start(bf16[272,256]{1,0:T(8,128)(2,1)S(1)} %choose.1.refs_0_), channel_id=1, source_target_pairs={{0,3},{1,2},{2,1},{3,0},{4,7},{5,6},{6,5},{7,4},{8,11},{9,10},{10,... | collective-permute-start | bytes 417800 | tf_op jit(solution)/shard_map/ppermute | solution.py:383
  20.3 0.0 collective-permute-start.3
  20.3 0.4 collective-permute-start.2
  20.7 0.0 collective-permute-start.5
  20.7 3.8 %collective-permute-done.4.refs_3_ = bf16[272,256]{1,0:T(8,128)(2,1)S(1)} collective-permute-done((bf16[272,256]{1,0:T(8,128)(2,1)S(1)}, bf16[272,256]{1,0:T(8,128)(2,1)S(1)}, u32[]{:S(2)}, u32[]{:S(2)}) %collective-permute-start.4) | collective-permute-done | bytes 139296 | tf_op jit(solution)/shard_map/ppermute | solution.py:383
  24.5 0.0 collective-permute-start.8
  24.5 7.3 %collective-permute-done.3.refs_2_ = bf16[272,256]{1,0:T(8,128)(2,1)S(1)} collective-permute-done((bf16[272,256]{1,0:T(8,128)(2,1)S(1)}, bf16[272,256]{1,0:T(8,128)(2,1)S(1)}, u32[]{:S(2)}, u32[]{:S(2)}) %collective-permute-start.3) | collective-permute-done | bytes 139296 | tf_op jit(solution)/shard_map/ppermute | solution.py:383
  31.8 0.1 collective-permute-start.7
  31.9 0.0 collective-permute-done.2.refs_1_
  31.9 0.4 collective-permute-start.6
  32.3 0.0 collective-permute-done.5.refs_4_
  32.3 0.0 collective-permute-done.8.refs_7_
  32.3 0.8 collective-permute-done.7.refs_6_
  33.2 0.2 collective-permute-done.6.refs_5_
  33.4 0.9 %assemble.1 = (bf16[4,256,256]{2,1,0:T(8,128)(2,1)S(1)}, bf16[4,256,256]{2,1,0:T(8,128)(2,1)}, f32[4,8,256]{2,1,0:T(8,128)S(1)}) custom-call(bf16[272,256]{1,0:T(8,128)(2,1)S(1)} %choose.1.refs_0_, bf16[272,256]{1,0:T(8,128)(2,1)S(1)} %collective-permute-done.2.refs_1_, bf16[272,256]{1,0:T(8,128)(2,1)S(1)} %collective-permute-done.3.refs_2_, ...), custom_call_target="tpu_custom_call" | custom-call | tf_op jit(solution)/shard_map/assemble/pallas_call | solution.py:230
  34.2 7.1 %all-to-all-done.kv = bf16[16,2,128,256]{3,2,1,0:T(8,128)(2,1)S(1)} async-done(((bf16[16,2,128,256]{3,2,1,0:T(8,128)(2,1)}), bf16[16,2,128,256]{3,2,1,0:T(8,128)(2,1)S(1)}, u32[]{:S(2)}, u32[]{:S(2)}) %all-to-all-start) | async-done | bytes 2097184 | tf_op jit(solution)/shard_map/all_to_all | solution.py:72
  41.4 6.9 %attention.1 = (bf16[16,2,128,256]{3,2,1,0:T(8,128)(2,1)}, f32[4,2,64,256]{3,2,1,0:T(8,128)S(1)}, bf16[4,2,64,256]{3,2,1,0:T(8,128)(2,1)S(1)}) custom-call(bf16[4,256,256]{2,1,0:T(8,128)(2,1)S(1)} %get-tuple-element.21.qt, bf16[4,256,256]{2,1,0:T(8,128)(2,1)} %get-tuple-element.22.cotangent, f32[4,8,256]{2,1,0:T(8,128)S(1)} %get-tuple-element.23.stat, ...), custom_call_target="tpu_custom_call" | custom-call | flops 5368709120 | bytes 8388608 | tf_op jit(solution)/shard_map/attention/pallas_call | solution.py:288
  48.3 9.5 %all-to-all-start.1 = ((bf16[16,2,128,256]{3,2,1,0:T(8,128)(2,1)}), bf16[16,2,128,256]{3,2,1,0:T(8,128)(2,1)S(1)}, u32[]{:S(2)}, u32[]{:S(2)}) async-start(bf16[16,2,128,256]{3,2,1,0:T(8,128)(2,1)} %get-tuple-element.25), calls=%async_computation.1 | async-start | bytes 4194304 | tf_op jit(solution)/shard_map/all_to_all | solution.py:72
  57.7 0.0 collective-permute-start.9
  57.7 1.5 %collective-permute-done.9.other = bf16[4,2,64,256]{3,2,1,0:T(8,128)(2,1)S(1)} collective-permute-done((bf16[4,2,64,256]{3,2,1,0:T(8,128)(2,1)S(1)}, bf16[4,2,64,256]{3,2,1,0:T(8,128)(2,1)S(1)}, u32[]{:S(2)}, u32[]{:S(2)}) %collective-permute-start.9) | collective-permute-done | bytes 262176 | tf_op jit(solution)/shard_map/ppermute | solution.py:387
  59.3 0.1 collective-permute-start.10
  59.4 2.4 %collective-permute-start.11 = (bf16[2,64,256]{2,1,0:T(8,128)(2,1)S(1)}, bf16[2,64,256]{2,1,0:T(8,128)(2,1)S(1)}, u32[]{:S(2)}, u32[]{:S(2)}) collective-permute-start(bf16[2,64,256]{2,1,0:T(8,128)(2,1)S(1)} %get-tuple-element.30), channel_id=1, source_target_pairs={{0,2},{1,3},{2,0},{3,1},{4,6},{5,7},{6,4},{7,5},{8,10},{9,11},{10,... | collective-permute-start | bytes 196616 | tf_op jit(solution)/shard_map/ppermute | solution.py:388
  61.9 1.1 %collective-permute-start.12 = (bf16[2,64,256]{2,1,0:T(8,128)(2,1)S(1)}, bf16[2,64,256]{2,1,0:T(8,128)(2,1)S(1)}, u32[]{:S(2)}, u32[]{:S(2)}) collective-permute-start(bf16[2,64,256]{2,1,0:T(8,128)(2,1)S(1)} %get-tuple-element.31), channel_id=1, source_target_pairs={{0,3},{1,2},{2,1},{3,0},{4,7},{5,6},{6,5},{7,4},{8,11},{9,10},{10,... | collective-permute-start | bytes 196616 | tf_op jit(solution)/shard_map/ppermute | solution.py:388
  63.0 0.0 collective-permute-done.10.refs_1_
  63.0 1.0 %collective-permute-done.11.refs_2_ = bf16[2,64,256]{2,1,0:T(8,128)(2,1)S(1)} collective-permute-done((bf16[2,64,256]{2,1,0:T(8,128)(2,1)S(1)}, bf16[2,64,256]{2,1,0:T(8,128)(2,1)S(1)}, u32[]{:S(2)}, u32[]{:S(2)}) %collective-permute-start.11) | collective-permute-done | bytes 65568 | tf_op jit(solution)/shard_map/ppermute | solution.py:388
  64.0 3.1 %collective-permute-done.12.refs_3_ = bf16[2,64,256]{2,1,0:T(8,128)(2,1)S(1)} collective-permute-done((bf16[2,64,256]{2,1,0:T(8,128)(2,1)S(1)}, bf16[2,64,256]{2,1,0:T(8,128)(2,1)S(1)}, u32[]{:S(2)}, u32[]{:S(2)}) %collective-permute-start.12) | collective-permute-done | bytes 65568 | tf_op jit(solution)/shard_map/ppermute | solution.py:388
  67.1 0.7 collective-permute-start.13
  67.8 0.0 collective-permute-done.13.crossed
  67.8 5.8 %collective-permute-start.14 = (bf16[64,256]{1,0:T(8,128)(2,1)S(1)}, bf16[64,256]{1,0:T(8,128)(2,1)S(1)}, u32[]{:S(2)}, u32[]{:S(2)}) collective-permute-start(bf16[64,256]{1,0:T(8,128)(2,1)S(1)} %get-tuple-element.33), channel_id=1, source_target_pairs={{0,8},{8,0},{16,24},{24,16},{1,9},{9,1},{17,25},{25,17},{2,10},{10... | collective-permute-start | bytes 98312 | tf_op jit(solution)/shard_map/ppermute | solution.py:391
  73.6 11.8 %collective-permute-done.14.other = bf16[64,256]{1,0:T(8,128)(2,1)S(1)} collective-permute-done((bf16[64,256]{1,0:T(8,128)(2,1)S(1)}, bf16[64,256]{1,0:T(8,128)(2,1)S(1)}, u32[]{:S(2)}, u32[]{:S(2)}) %collective-permute-start.14) | collective-permute-done | bytes 32800 | tf_op jit(solution)/shard_map/ppermute | solution.py:391
  85.4 0.2 all-to-all-done.1.chunks
  85.6 1.7 %join.1 = (bf16[128,4096]{1,0:T(8,128)(2,1)}, bf16[128,4096]{1,0:T(8,128)(2,1)}, bf16[64,256]{1,0:T(8,128)(2,1)}) custom-call(bf16[16,2,128,256]{3,2,1,0:T(8,128)(2,1)S(1)} %all-to-all-done.1.chunks, bf16[64,256]{1,0:T(8,128)(2,1)S(1)} %get-tuple-element.32.own, bf16[64,256]{1,0:T(8,128)(2,1)S(1)} %collective-permute-done.14.other), custom_call_target="tpu_custom_call" | custom-call | tf_op jit(solution)/shard_map/join/pallas_call | solution.py:200
  (5 shorter events, 0.2 us)
Async XLA Ops:
  1.5 5.0 %collective-permute-start = (bf16[144,256]{1,0:T(8,128)(2,1)S(1)}, bf16[144,256]{1,0:T(8,128)(2,1)S(1)}, u32[]{:S(2)}, u32[]{:S(2)}) collective-permute-start(bf16[144,256]{1,0:T(8,128)(2,1)S(1)} %message.1.own), channel_id=1, source_target_pairs={{0,8},{8,0},{16,24},{24,16},{1,9},{9,1},{17,25},{25,17},{2,10},{10... | collective-permute-start | bytes 221192 | tf_op jit(solution)/shard_map/ppermute | solution.py:377
  6.5 34.9 %all-to-all-start = ((bf16[16,2,128,256]{3,2,1,0:T(8,128)(2,1)}), bf16[16,2,128,256]{3,2,1,0:T(8,128)(2,1)S(1)}, u32[]{:S(2)}, u32[]{:S(2)}) async-start(bf16[16,2,128,256]{3,2,1,0:T(8,128)(2,1)} %split.1), calls=%async_computation | async-start | bytes 4194304 | tf_op jit(solution)/shard_map/all_to_all | solution.py:72
  15.2 0.7 collective-permute-start.1
  15.9 8.6 %collective-permute-start.4 = (bf16[272,256]{1,0:T(8,128)(2,1)S(1)}, bf16[272,256]{1,0:T(8,128)(2,1)S(1)}, u32[]{:S(2)}, u32[]{:S(2)}) collective-permute-start(bf16[272,256]{1,0:T(8,128)(2,1)S(1)} %choose.1.refs_0_), channel_id=1, source_target_pairs={{0,3},{1,2},{2,1},{3,0},{4,7},{5,6},{6,5},{7,4},{8,11},{9,10},{10,... | collective-permute-start | bytes 417800 | tf_op jit(solution)/shard_map/ppermute | solution.py:383
  20.3 11.5 %collective-permute-start.3 = (bf16[272,256]{1,0:T(8,128)(2,1)S(1)}, bf16[272,256]{1,0:T(8,128)(2,1)S(1)}, u32[]{:S(2)}, u32[]{:S(2)}) collective-permute-start(bf16[272,256]{1,0:T(8,128)(2,1)S(1)} %choose.1.refs_0_), channel_id=1, source_target_pairs={{0,2},{1,3},{2,0},{3,1},{4,6},{5,7},{6,4},{7,5},{8,10},{9,11},{10,... | collective-permute-start | bytes 417800 | tf_op jit(solution)/shard_map/ppermute | solution.py:383
  20.3 11.6 %collective-permute-start.2 = (bf16[272,256]{1,0:T(8,128)(2,1)S(1)}, bf16[272,256]{1,0:T(8,128)(2,1)S(1)}, u32[]{:S(2)}, u32[]{:S(2)}) collective-permute-start(bf16[272,256]{1,0:T(8,128)(2,1)S(1)} %choose.1.refs_0_), channel_id=1, source_target_pairs={{0,1},{1,0},{2,3},{3,2},{4,5},{5,4},{6,7},{7,6},{8,9},{9,8},{10,11... | collective-permute-start | bytes 417800 | tf_op jit(solution)/shard_map/ppermute | solution.py:383
  20.7 11.6 %collective-permute-start.5 = (bf16[272,256]{1,0:T(8,128)(2,1)S(1)}, bf16[272,256]{1,0:T(8,128)(2,1)S(1)}, u32[]{:S(2)}, u32[]{:S(2)}) collective-permute-start(bf16[272,256]{1,0:T(8,128)(2,1)S(1)} %choose.1.refs_0_), channel_id=1, source_target_pairs={{0,4},{4,0},{1,5},{5,1},{2,6},{6,2},{3,7},{7,3},{8,12},{12,8},{9,1... | collective-permute-start | bytes 417800 | tf_op jit(solution)/shard_map/ppermute | solution.py:384
  24.5 7.8 %collective-permute-start.8 = (bf16[272,256]{1,0:T(8,128)(2,1)S(1)}, bf16[272,256]{1,0:T(8,128)(2,1)S(1)}, u32[]{:S(2)}, u32[]{:S(2)}) collective-permute-start(bf16[272,256]{1,0:T(8,128)(2,1)S(1)} %collective-permute-done.4.refs_3_), channel_id=1, source_target_pairs={{0,4},{4,0},{1,5},{5,1},{2,6},{6,2},{3,7},{7,3},{8,12},{12,8},{9,1... | collective-permute-start | bytes 417800 | tf_op jit(solution)/shard_map/ppermute | solution.py:384
  31.8 1.4 %collective-permute-start.7 = (bf16[272,256]{1,0:T(8,128)(2,1)S(1)}, bf16[272,256]{1,0:T(8,128)(2,1)S(1)}, u32[]{:S(2)}, u32[]{:S(2)}) collective-permute-start(bf16[272,256]{1,0:T(8,128)(2,1)S(1)} %collective-permute-done.3.refs_2_), channel_id=1, source_target_pairs={{0,4},{4,0},{1,5},{5,1},{2,6},{6,2},{3,7},{7,3},{8,12},{12,8},{9,1... | collective-permute-start | bytes 417800 | tf_op jit(solution)/shard_map/ppermute | solution.py:384
  31.9 1.4 %collective-permute-start.6 = (bf16[272,256]{1,0:T(8,128)(2,1)S(1)}, bf16[272,256]{1,0:T(8,128)(2,1)S(1)}, u32[]{:S(2)}, u32[]{:S(2)}) collective-permute-start(bf16[272,256]{1,0:T(8,128)(2,1)S(1)} %collective-permute-done.2.refs_1_), channel_id=1, source_target_pairs={{0,4},{4,0},{1,5},{5,1},{2,6},{6,2},{3,7},{7,3},{8,12},{12,8},{9,1... | collective-permute-start | bytes 417800 | tf_op jit(solution)/shard_map/ppermute | solution.py:384
  48.3 37.3 %all-to-all-start.1 = ((bf16[16,2,128,256]{3,2,1,0:T(8,128)(2,1)}), bf16[16,2,128,256]{3,2,1,0:T(8,128)(2,1)S(1)}, u32[]{:S(2)}, u32[]{:S(2)}) async-start(bf16[16,2,128,256]{3,2,1,0:T(8,128)(2,1)} %get-tuple-element.25), calls=%async_computation.1 | async-start | bytes 4194304 | tf_op jit(solution)/shard_map/all_to_all | solution.py:72
  57.7 1.5 %collective-permute-start.9 = (bf16[4,2,64,256]{3,2,1,0:T(8,128)(2,1)S(1)}, bf16[4,2,64,256]{3,2,1,0:T(8,128)(2,1)S(1)}, u32[]{:S(2)}, u32[]{:S(2)}) collective-permute-start(bf16[4,2,64,256]{3,2,1,0:T(8,128)(2,1)S(1)} %get-tuple-element.27), channel_id=1, source_target_pairs={{0,4},{4,0},{1,5},{5,1},{2,6},{6,2},{3,7},{7,3},{8,12},{12,8},{9,1... | collective-permute-start | bytes 786440 | tf_op jit(solution)/shard_map/ppermute | solution.py:387
  59.3 3.6 %collective-permute-start.10 = (bf16[2,64,256]{2,1,0:T(8,128)(2,1)S(1)}, bf16[2,64,256]{2,1,0:T(8,128)(2,1)S(1)}, u32[]{:S(2)}, u32[]{:S(2)}) collective-permute-start(bf16[2,64,256]{2,1,0:T(8,128)(2,1)S(1)} %get-tuple-element.29), channel_id=1, source_target_pairs={{0,1},{1,0},{2,3},{3,2},{4,5},{5,4},{6,7},{7,6},{8,9},{9,8},{10,11... | collective-permute-start | bytes 196616 | tf_op jit(solution)/shard_map/ppermute | solution.py:388
  59.4 4.5 %collective-permute-start.11 = (bf16[2,64,256]{2,1,0:T(8,128)(2,1)S(1)}, bf16[2,64,256]{2,1,0:T(8,128)(2,1)S(1)}, u32[]{:S(2)}, u32[]{:S(2)}) collective-permute-start(bf16[2,64,256]{2,1,0:T(8,128)(2,1)S(1)} %get-tuple-element.30), channel_id=1, source_target_pairs={{0,2},{1,3},{2,0},{3,1},{4,6},{5,7},{6,4},{7,5},{8,10},{9,11},{10,... | collective-permute-start | bytes 196616 | tf_op jit(solution)/shard_map/ppermute | solution.py:388
  61.9 5.2 %collective-permute-start.12 = (bf16[2,64,256]{2,1,0:T(8,128)(2,1)S(1)}, bf16[2,64,256]{2,1,0:T(8,128)(2,1)S(1)}, u32[]{:S(2)}, u32[]{:S(2)}) collective-permute-start(bf16[2,64,256]{2,1,0:T(8,128)(2,1)S(1)} %get-tuple-element.31), channel_id=1, source_target_pairs={{0,3},{1,2},{2,1},{3,0},{4,7},{5,6},{6,5},{7,4},{8,11},{9,10},{10,... | collective-permute-start | bytes 196616 | tf_op jit(solution)/shard_map/ppermute | solution.py:388
  67.1 0.7 collective-permute-start.13
  67.8 17.6 %collective-permute-start.14 = (bf16[64,256]{1,0:T(8,128)(2,1)S(1)}, bf16[64,256]{1,0:T(8,128)(2,1)S(1)}, u32[]{:S(2)}, u32[]{:S(2)}) collective-permute-start(bf16[64,256]{1,0:T(8,128)(2,1)S(1)} %get-tuple-element.33), channel_id=1, source_target_pairs={{0,8},{8,0},{16,24},{24,16},{1,9},{9,1},{17,25},{25,17},{2,10},{10... | collective-permute-start | bytes 98312 | tf_op jit(solution)/shard_map/ppermute | solution.py:391

commit v8 on v7

--- a/solution.py
+++ b/solution.py
@@ -258,7 +258,7 @@
             grad = (weight * (slope - stat[zl, 0:1, :])).astype(BF16)
             weights.append(weight.astype(BF16))
             slopes.append(grad)
-            ds[zl, rows, :] = grad
+            ds[rows, zl * ROWS : (zl + 1) * ROWS] = grad
         value_grad = sum(dot(weights[zl], dt[zl], 1, 1) for zl in range(4))
         key_grad = sum(dot(slopes[zl], qt[zl], 1, 1) for zl in range(4)) * FACTOR
         for place in range(4):
@@ -270,15 +270,14 @@
         copy.start()
         writes.append(copy)
     keys = kv[:, 0].reshape(16 * KEYS, DH)
-    for zl in range(4):
-        dq[zl] = dot(keys, ds[zl], 0, 0) * FACTOR
+    dq[...] = dot(keys, ds[...], 0, 0) * FACTOR
     for k in range(4):
         zl = k
         for xl in range(2):
             at = pl.ds(pl.multiple_of((2 * xl + core) * PART, PART), PART)
-            own[k, xl] = dq[zl, at, :]
+            own[k, xl] = dq[at, zl * ROWS : (zl + 1) * ROWS]
             at = pl.ds(pl.multiple_of((2 * xl + 1 - core) * PART, PART), PART)
-            other[k, xl] = dq[zl, at, :].astype(BF16)
+            other[k, xl] = dq[at, zl * ROWS : (zl + 1) * ROWS].astype(BF16)
     for copy in writes:
         copy.wait()
 
@@ -295,8 +294,8 @@
         [
             pltpu.VMEM((4, DH, ROWS), BF16),
             pltpu.VMEM((16, 2, KEYS, DH), BF16),
-            pltpu.VMEM((4, DH, ROWS), F32),
-            pltpu.VMEM((4, 16 * KEYS, ROWS), BF16),
+            pltpu.VMEM((DH, 4 * ROWS), F32),
+            pltpu.VMEM((16 * KEYS, 4 * ROWS), BF16),
             pltpu.SemaphoreType.DMA((8,)),
             pltpu.SemaphoreType.DMA,
         ],

time: 87.7 us -> 87.7 us (level)
  no operation moved by 1% of the time
where the time goes in v8:
time: 87.7 us; the launch traced here: 87.2 us
  waiting for transfers between devices  36.9 us (42%)
  starting transfers between devices  36.3 us (41%)
  Pallas kernels  13.3 us (15%)
    all_to_all x2, starting transfers between devices, exchange(): lax.all_to_all(chunks, AXES, split_axis=0, concat_axis=0, tiled=True, axi...  18.1 us
    ppermute x1, waiting for transfers between devices, local(): other = lax.ppermute(other, 'x', NEXT)  11.8 us
    ppermute x3, waiting for transfers between devices, local(): mine = [part] + [lax.ppermute(part, 'zl', turn(k)) for k in (1, 2, 3)]  11.1 us
    all_to_all x2, waiting for transfers between devices, exchange(): lax.all_to_all(chunks, AXES, split_axis=0, concat_axis=0, tiled=True, axi...  7.3 us
    pallas_call x1, Pallas kernels, attention(): call(attention_kernel, [pltpu.HBM((16, 2, KEYS, DH), BF16), shape(*part,...  6.86 us
    ppermute x1, starting transfers between devices, local(): other = lax.ppermute(other, 'x', NEXT)  5.78 us
    ppermute x3, starting transfers between devices, local(): mine = [part] + [lax.ppermute(part, 'zl', turn(k)) for k in (1, 2, 3)]  4.81 us
    ppermute x3, waiting for transfers between devices, local(): sums = [sums[0]] + [lax.ppermute(sums[k], 'zl', turn(k)) for k in (1, 2, 3)]  4.11 us
  transfers between devices with their start and end apart: 17, of which 10 were waited for; matrix products, arithmetic and copies ran while one was open for 0% of the time, Pallas kernels for 4%

profile of v8, /device:TPU:1, one launch (start us, length us, event | category | flops | bytes accessed | tf_op | source)
XLA Modules:
  0.0 87.2 jit_solution(13340866982384871161)
XLA Ops:
  0.6 0.9 message.1.own
  1.5 2.1 %collective-permute-start = (bf16[144,256]{1,0:T(8,128)(2,1)S(1)}, bf16[144,256]{1,0:T(8,128)(2,1)S(1)}, u32[]{:S(2)}, u32[]{:S(2)}) collective-permute-start(bf16[144,256]{1,0:T(8,128)(2,1)S(1)} %message.1.own), channel_id=1, source_target_pairs={{0,8},{8,0},{16,24},{24,16},{1,9},{9,1},{17,25},{25,17},{2,10},{10... | collective-permute-start | bytes 221192 | tf_op jit(solution)/shard_map/ppermute | solution.py:376
  3.6 2.8 %split.1 = bf16[16,2,128,256]{3,2,1,0:T(8,128)(2,1)} custom-call(bf16[128,4096]{1,0:T(8,128)(2,1)} %keys.1, bf16[128,4096]{1,0:T(8,128)(2,1)} %values.1), custom_call_target="tpu_custom_call" | custom-call | bytes 8388608 | tf_op jit(solution)/shard_map/split/pallas_call | solution.py:173
  6.5 0.0 collective-permute-done.other
  6.5 8.7 %all-to-all-start = ((bf16[16,2,128,256]{3,2,1,0:T(8,128)(2,1)}), bf16[16,2,128,256]{3,2,1,0:T(8,128)(2,1)S(1)}, u32[]{:S(2)}, u32[]{:S(2)}) async-start(bf16[16,2,128,256]{3,2,1,0:T(8,128)(2,1)} %split.1), calls=%async_computation | async-start | bytes 4194304 | tf_op jit(solution)/shard_map/all_to_all | solution.py:72
  15.2 0.7 collective-permute-start.1
  15.8 0.0 collective-permute-done.1.crossed
  15.9 4.4 %collective-permute-start.4 = (bf16[272,256]{1,0:T(8,128)(2,1)S(1)}, bf16[272,256]{1,0:T(8,128)(2,1)S(1)}, u32[]{:S(2)}, u32[]{:S(2)}) collective-permute-start(bf16[272,256]{1,0:T(8,128)(2,1)S(1)} %choose.1.refs_0_), channel_id=1, source_target_pairs={{0,3},{1,2},{2,1},{3,0},{4,7},{5,6},{6,5},{7,4},{8,11},{9,10},{10,... | collective-permute-start | bytes 417800 | tf_op jit(solution)/shard_map/ppermute | solution.py:382
  20.3 0.0 collective-permute-start.3
  20.3 0.4 collective-permute-start.2
  20.7 0.0 collective-permute-start.5
  20.7 3.8 %collective-permute-done.4.refs_3_ = bf16[272,256]{1,0:T(8,128)(2,1)S(1)} collective-permute-done((bf16[272,256]{1,0:T(8,128)(2,1)S(1)}, bf16[272,256]{1,0:T(8,128)(2,1)S(1)}, u32[]{:S(2)}, u32[]{:S(2)}) %collective-permute-start.4) | collective-permute-done | bytes 139296 | tf_op jit(solution)/shard_map/ppermute | solution.py:382
  24.5 0.0 collective-permute-start.8
  24.5 7.3 %collective-permute-done.3.refs_2_ = bf16[272,256]{1,0:T(8,128)(2,1)S(1)} collective-permute-done((bf16[272,256]{1,0:T(8,128)(2,1)S(1)}, bf16[272,256]{1,0:T(8,128)(2,1)S(1)}, u32[]{:S(2)}, u32[]{:S(2)}) %collective-permute-start.3) | collective-permute-done | bytes 139296 | tf_op jit(solution)/shard_map/ppermute | solution.py:382
  31.8 0.1 collective-permute-start.7
  31.9 0.0 collective-permute-done.2.refs_1_
  31.9 0.4 collective-permute-start.6
  32.3 0.0 collective-permute-done.5.refs_4_
  32.3 0.0 collective-permute-done.8.refs_7_
  32.3 0.8 collective-permute-done.7.refs_6_
  33.2 0.2 collective-permute-done.6.refs_5_
  33.4 0.9 %assemble.1 = (bf16[4,256,256]{2,1,0:T(8,128)(2,1)S(1)}, bf16[4,256,256]{2,1,0:T(8,128)(2,1)}, f32[4,8,256]{2,1,0:T(8,128)S(1)}) custom-call(bf16[272,256]{1,0:T(8,128)(2,1)S(1)} %choose.1.refs_0_, bf16[272,256]{1,0:T(8,128)(2,1)S(1)} %collective-permute-done.2.refs_1_, bf16[272,256]{1,0:T(8,128)(2,1)S(1)} %collective-permute-done.3.refs_2_, ...), custom_call_target="tpu_custom_call" | custom-call | tf_op jit(solution)/shard_map/assemble/pallas_call | solution.py:230
  34.2 7.1 %all-to-all-done.kv = bf16[16,2,128,256]{3,2,1,0:T(8,128)(2,1)S(1)} async-done(((bf16[16,2,128,256]{3,2,1,0:T(8,128)(2,1)}), bf16[16,2,128,256]{3,2,1,0:T(8,128)(2,1)S(1)}, u32[]{:S(2)}, u32[]{:S(2)}) %all-to-all-start) | async-done | bytes 2097184 | tf_op jit(solution)/shard_map/all_to_all | solution.py:72
  41.4 6.9 %attention.1 = (bf16[16,2,128,256]{3,2,1,0:T(8,128)(2,1)}, f32[4,2,64,256]{3,2,1,0:T(8,128)S(1)}, bf16[4,2,64,256]{3,2,1,0:T(8,128)(2,1)S(1)}) custom-call(bf16[4,256,256]{2,1,0:T(8,128)(2,1)S(1)} %get-tuple-element.21.qt, bf16[4,256,256]{2,1,0:T(8,128)(2,1)} %get-tuple-element.22.cotangent, f32[4,8,256]{2,1,0:T(8,128)S(1)} %get-tuple-element.23.stat, ...), custom_call_target="tpu_custom_call" | custom-call | flops 5368709120 | bytes 8388608 | tf_op jit(solution)/shard_map/attention/pallas_call | solution.py:287
  48.2 9.5 %all-to-all-start.1 = ((bf16[16,2,128,256]{3,2,1,0:T(8,128)(2,1)}), bf16[16,2,128,256]{3,2,1,0:T(8,128)(2,1)S(1)}, u32[]{:S(2)}, u32[]{:S(2)}) async-start(bf16[16,2,128,256]{3,2,1,0:T(8,128)(2,1)} %get-tuple-element.25), calls=%async_computation.1 | async-start | bytes 4194304 | tf_op jit(solution)/shard_map/all_to_all | solution.py:72
  57.7 0.0 collective-permute-start.9
  57.7 1.5 %collective-permute-done.9.other = bf16[4,2,64,256]{3,2,1,0:T(8,128)(2,1)S(1)} collective-permute-done((bf16[4,2,64,256]{3,2,1,0:T(8,128)(2,1)S(1)}, bf16[4,2,64,256]{3,2,1,0:T(8,128)(2,1)S(1)}, u32[]{:S(2)}, u32[]{:S(2)}) %collective-permute-start.9) | collective-permute-done | bytes 262176 | tf_op jit(solution)/shard_map/ppermute | solution.py:386
  59.3 0.1 collective-permute-start.10
  59.4 2.4 %collective-permute-start.11 = (bf16[2,64,256]{2,1,0:T(8,128)(2,1)S(1)}, bf16[2,64,256]{2,1,0:T(8,128)(2,1)S(1)}, u32[]{:S(2)}, u32[]{:S(2)}) collective-permute-start(bf16[2,64,256]{2,1,0:T(8,128)(2,1)S(1)} %get-tuple-element.30), channel_id=1, source_target_pairs={{0,2},{1,3},{2,0},{3,1},{4,6},{5,7},{6,4},{7,5},{8,10},{9,11},{10,... | collective-permute-start | bytes 196616 | tf_op jit(solution)/shard_map/ppermute | solution.py:387
  61.8 1.1 %collective-permute-start.12 = (bf16[2,64,256]{2,1,0:T(8,128)(2,1)S(1)}, bf16[2,64,256]{2,1,0:T(8,128)(2,1)S(1)}, u32[]{:S(2)}, u32[]{:S(2)}) collective-permute-start(bf16[2,64,256]{2,1,0:T(8,128)(2,1)S(1)} %get-tuple-element.31), channel_id=1, source_target_pairs={{0,3},{1,2},{2,1},{3,0},{4,7},{5,6},{6,5},{7,4},{8,11},{9,10},{10,... | collective-permute-start | bytes 196616 | tf_op jit(solution)/shard_map/ppermute | solution.py:387
  62.9 0.0 collective-permute-done.10.refs_1_
  62.9 1.0 %collective-permute-done.11.refs_2_ = bf16[2,64,256]{2,1,0:T(8,128)(2,1)S(1)} collective-permute-done((bf16[2,64,256]{2,1,0:T(8,128)(2,1)S(1)}, bf16[2,64,256]{2,1,0:T(8,128)(2,1)S(1)}, u32[]{:S(2)}, u32[]{:S(2)}) %collective-permute-start.11) | collective-permute-done | bytes 65568 | tf_op jit(solution)/shard_map/ppermute | solution.py:387
  63.9 3.1 %collective-permute-done.12.refs_3_ = bf16[2,64,256]{2,1,0:T(8,128)(2,1)S(1)} collective-permute-done((bf16[2,64,256]{2,1,0:T(8,128)(2,1)S(1)}, bf16[2,64,256]{2,1,0:T(8,128)(2,1)S(1)}, u32[]{:S(2)}, u32[]{:S(2)}) %collective-permute-start.12) | collective-permute-done | bytes 65568 | tf_op jit(solution)/shard_map/ppermute | solution.py:387
  67.1 0.7 collective-permute-start.13
  67.7 0.0 collective-permute-done.13.crossed
  67.8 5.8 %collective-permute-start.14 = (bf16[64,256]{1,0:T(8,128)(2,1)S(1)}, bf16[64,256]{1,0:T(8,128)(2,1)S(1)}, u32[]{:S(2)}, u32[]{:S(2)}) collective-permute-start(bf16[64,256]{1,0:T(8,128)(2,1)S(1)} %get-tuple-element.33), channel_id=1, source_target_pairs={{0,8},{8,0},{16,24},{24,16},{1,9},{9,1},{17,25},{25,17},{2,10},{10... | collective-permute-start | bytes 98312 | tf_op jit(solution)/shard_map/ppermute | solution.py:390
  73.6 11.8 %collective-permute-done.14.other = bf16[64,256]{1,0:T(8,128)(2,1)S(1)} collective-permute-done((bf16[64,256]{1,0:T(8,128)(2,1)S(1)}, bf16[64,256]{1,0:T(8,128)(2,1)S(1)}, u32[]{:S(2)}, u32[]{:S(2)}) %collective-permute-start.14) | collective-permute-done | bytes 32800 | tf_op jit(solution)/shard_map/ppermute | solution.py:390
  85.4 0.2 all-to-all-done.1.chunks
  85.5 1.7 %join.1 = (bf16[128,4096]{1,0:T(8,128)(2,1)}, bf16[128,4096]{1,0:T(8,128)(2,1)}, bf16[64,256]{1,0:T(8,128)(2,1)}) custom-call(bf16[16,2,128,256]{3,2,1,0:T(8,128)(2,1)S(1)} %all-to-all-done.1.chunks, bf16[64,256]{1,0:T(8,128)(2,1)S(1)} %get-tuple-element.32.own, bf16[64,256]{1,0:T(8,128)(2,1)S(1)} %collective-permute-done.14.other), custom_call_target="tpu_custom_call" | custom-call | tf_op jit(solution)/shard_map/join/pallas_call | solution.py:200
  (5 shorter events, 0.2 us)
Async XLA Ops:
  1.5 5.0 %collective-permute-start = (bf16[144,256]{1,0:T(8,128)(2,1)S(1)}, bf16[144,256]{1,0:T(8,128)(2,1)S(1)}, u32[]{:S(2)}, u32[]{:S(2)}) collective-permute-start(bf16[144,256]{1,0:T(8,128)(2,1)S(1)} %message.1.own), channel_id=1, source_target_pairs={{0,8},{8,0},{16,24},{24,16},{1,9},{9,1},{17,25},{25,17},{2,10},{10... | collective-permute-start | bytes 221192 | tf_op jit(solution)/shard_map/ppermute | solution.py:376
  6.5 34.9 %all-to-all-start = ((bf16[16,2,128,256]{3,2,1,0:T(8,128)(2,1)}), bf16[16,2,128,256]{3,2,1,0:T(8,128)(2,1)S(1)}, u32[]{:S(2)}, u32[]{:S(2)}) async-start(bf16[16,2,128,256]{3,2,1,0:T(8,128)(2,1)} %split.1), calls=%async_computation | async-start | bytes 4194304 | tf_op jit(solution)/shard_map/all_to_all | solution.py:72
  15.2 0.7 collective-permute-start.1
  15.9 8.6 %collective-permute-start.4 = (bf16[272,256]{1,0:T(8,128)(2,1)S(1)}, bf16[272,256]{1,0:T(8,128)(2,1)S(1)}, u32[]{:S(2)}, u32[]{:S(2)}) collective-permute-start(bf16[272,256]{1,0:T(8,128)(2,1)S(1)} %choose.1.refs_0_), channel_id=1, source_target_pairs={{0,3},{1,2},{2,1},{3,0},{4,7},{5,6},{6,5},{7,4},{8,11},{9,10},{10,... | collective-permute-start | bytes 417800 | tf_op jit(solution)/shard_map/ppermute | solution.py:382
  20.3 11.5 %collective-permute-start.3 = (bf16[272,256]{1,0:T(8,128)(2,1)S(1)}, bf16[272,256]{1,0:T(8,128)(2,1)S(1)}, u32[]{:S(2)}, u32[]{:S(2)}) collective-permute-start(bf16[272,256]{1,0:T(8,128)(2,1)S(1)} %choose.1.refs_0_), channel_id=1, source_target_pairs={{0,2},{1,3},{2,0},{3,1},{4,6},{5,7},{6,4},{7,5},{8,10},{9,11},{10,... | collective-permute-start | bytes 417800 | tf_op jit(solution)/shard_map/ppermute | solution.py:382
  20.3 11.6 %collective-permute-start.2 = (bf16[272,256]{1,0:T(8,128)(2,1)S(1)}, bf16[272,256]{1,0:T(8,128)(2,1)S(1)}, u32[]{:S(2)}, u32[]{:S(2)}) collective-permute-start(bf16[272,256]{1,0:T(8,128)(2,1)S(1)} %choose.1.refs_0_), channel_id=1, source_target_pairs={{0,1},{1,0},{2,3},{3,2},{4,5},{5,4},{6,7},{7,6},{8,9},{9,8},{10,11... | collective-permute-start | bytes 417800 | tf_op jit(solution)/shard_map/ppermute | solution.py:382
  20.7 11.6 %collective-permute-start.5 = (bf16[272,256]{1,0:T(8,128)(2,1)S(1)}, bf16[272,256]{1,0:T(8,128)(2,1)S(1)}, u32[]{:S(2)}, u32[]{:S(2)}) collective-permute-start(bf16[272,256]{1,0:T(8,128)(2,1)S(1)} %choose.1.refs_0_), channel_id=1, source_target_pairs={{0,4},{4,0},{1,5},{5,1},{2,6},{6,2},{3,7},{7,3},{8,12},{12,8},{9,1... | collective-permute-start | bytes 417800 | tf_op jit(solution)/shard_map/ppermute | solution.py:383
  24.5 7.8 %collective-permute-start.8 = (bf16[272,256]{1,0:T(8,128)(2,1)S(1)}, bf16[272,256]{1,0:T(8,128)(2,1)S(1)}, u32[]{:S(2)}, u32[]{:S(2)}) collective-permute-start(bf16[272,256]{1,0:T(8,128)(2,1)S(1)} %collective-permute-done.4.refs_3_), channel_id=1, source_target_pairs={{0,4},{4,0},{1,5},{5,1},{2,6},{6,2},{3,7},{7,3},{8,12},{12,8},{9,1... | collective-permute-start | bytes 417800 | tf_op jit(solution)/shard_map/ppermute | solution.py:383
  31.8 1.4 %collective-permute-start.7 = (bf16[272,256]{1,0:T(8,128)(2,1)S(1)}, bf16[272,256]{1,0:T(8,128)(2,1)S(1)}, u32[]{:S(2)}, u32[]{:S(2)}) collective-permute-start(bf16[272,256]{1,0:T(8,128)(2,1)S(1)} %collective-permute-done.3.refs_2_), channel_id=1, source_target_pairs={{0,4},{4,0},{1,5},{5,1},{2,6},{6,2},{3,7},{7,3},{8,12},{12,8},{9,1... | collective-permute-start | bytes 417800 | tf_op jit(solution)/shard_map/ppermute | solution.py:383
  31.9 1.4 %collective-permute-start.6 = (bf16[272,256]{1,0:T(8,128)(2,1)S(1)}, bf16[272,256]{1,0:T(8,128)(2,1)S(1)}, u32[]{:S(2)}, u32[]{:S(2)}) collective-permute-start(bf16[272,256]{1,0:T(8,128)(2,1)S(1)} %collective-permute-done.2.refs_1_), channel_id=1, source_target_pairs={{0,4},{4,0},{1,5},{5,1},{2,6},{6,2},{3,7},{7,3},{8,12},{12,8},{9,1... | collective-permute-start | bytes 417800 | tf_op jit(solution)/shard_map/ppermute | solution.py:383
  48.2 37.3 %all-to-all-start.1 = ((bf16[16,2,128,256]{3,2,1,0:T(8,128)(2,1)}), bf16[16,2,128,256]{3,2,1,0:T(8,128)(2,1)S(1)}, u32[]{:S(2)}, u32[]{:S(2)}) async-start(bf16[16,2,128,256]{3,2,1,0:T(8,128)(2,1)} %get-tuple-element.25), calls=%async_computation.1 | async-start | bytes 4194304 | tf_op jit(solution)/shard_map/all_to_all | solution.py:72
  57.7 1.5 %collective-permute-start.9 = (bf16[4,2,64,256]{3,2,1,0:T(8,128)(2,1)S(1)}, bf16[4,2,64,256]{3,2,1,0:T(8,128)(2,1)S(1)}, u32[]{:S(2)}, u32[]{:S(2)}) collective-permute-start(bf16[4,2,64,256]{3,2,1,0:T(8,128)(2,1)S(1)} %get-tuple-element.27), channel_id=1, source_target_pairs={{0,4},{4,0},{1,5},{5,1},{2,6},{6,2},{3,7},{7,3},{8,12},{12,8},{9,1... | collective-permute-start | bytes 786440 | tf_op jit(solution)/shard_map/ppermute | solution.py:386
  59.3 3.6 %collective-permute-start.10 = (bf16[2,64,256]{2,1,0:T(8,128)(2,1)S(1)}, bf16[2,64,256]{2,1,0:T(8,128)(2,1)S(1)}, u32[]{:S(2)}, u32[]{:S(2)}) collective-permute-start(bf16[2,64,256]{2,1,0:T(8,128)(2,1)S(1)} %get-tuple-element.29), channel_id=1, source_target_pairs={{0,1},{1,0},{2,3},{3,2},{4,5},{5,4},{6,7},{7,6},{8,9},{9,8},{10,11... | collective-permute-start | bytes 196616 | tf_op jit(solution)/shard_map/ppermute | solution.py:387
  59.4 4.5 %collective-permute-start.11 = (bf16[2,64,256]{2,1,0:T(8,128)(2,1)S(1)}, bf16[2,64,256]{2,1,0:T(8,128)(2,1)S(1)}, u32[]{:S(2)}, u32[]{:S(2)}) collective-permute-start(bf16[2,64,256]{2,1,0:T(8,128)(2,1)S(1)} %get-tuple-element.30), channel_id=1, source_target_pairs={{0,2},{1,3},{2,0},{3,1},{4,6},{5,7},{6,4},{7,5},{8,10},{9,11},{10,... | collective-permute-start | bytes 196616 | tf_op jit(solution)/shard_map/ppermute | solution.py:387
  61.8 5.2 %collective-permute-start.12 = (bf16[2,64,256]{2,1,0:T(8,128)(2,1)S(1)}, bf16[2,64,256]{2,1,0:T(8,128)(2,1)S(1)}, u32[]{:S(2)}, u32[]{:S(2)}) collective-permute-start(bf16[2,64,256]{2,1,0:T(8,128)(2,1)S(1)} %get-tuple-element.31), channel_id=1, source_target_pairs={{0,3},{1,2},{2,1},{3,0},{4,7},{5,6},{6,5},{7,4},{8,11},{9,10},{10,... | collective-permute-start | bytes 196616 | tf_op jit(solution)/shard_map/ppermute | solution.py:387
  67.1 0.7 collective-permute-start.13
  67.8 17.6 %collective-permute-start.14 = (bf16[64,256]{1,0:T(8,128)(2,1)S(1)}, bf16[64,256]{1,0:T(8,128)(2,1)S(1)}, u32[]{:S(2)}, u32[]{:S(2)}) collective-permute-start(bf16[64,256]{1,0:T(8,128)(2,1)S(1)} %get-tuple-element.33), channel_id=1, source_target_pairs={{0,8},{8,0},{16,24},{24,16},{1,9},{9,1},{17,25},{25,17},{2,10},{10... | collective-permute-start | bytes 98312 | tf_op jit(solution)/shard_map/ppermute | solution.py:390

commit v9 on v8

--- a/solution.py
+++ b/solution.py
@@ -246,10 +246,10 @@
     read.start()
     read.wait()
     writes = []
-    for block in range(4):
-        rows = slice(block * 4 * KEYS, (block + 1) * 4 * KEYS)
-        keys = kv[4 * block : 4 * block + 4, 0].reshape(4 * KEYS, DH)
-        values = kv[4 * block : 4 * block + 4, 1].reshape(4 * KEYS, DH)
+    for block in range(2):
+        rows = slice(block * 8 * KEYS, (block + 1) * 8 * KEYS)
+        keys = kv[8 * block : 8 * block + 8, 0].reshape(8 * KEYS, DH)
+        values = kv[8 * block : 8 * block + 8, 1].reshape(8 * KEYS, DH)
         weights, slopes = [], []
         for zl in range(4):
             score = dot(keys, qt[zl], 1, 0)
@@ -261,11 +261,11 @@
             ds[rows, zl * ROWS : (zl + 1) * ROWS] = grad
         value_grad = sum(dot(weights[zl], dt[zl], 1, 1) for zl in range(4))
         key_grad = sum(dot(slopes[zl], qt[zl], 1, 1) for zl in range(4)) * FACTOR
-        for place in range(4):
+        for place in range(8):
             part = slice(place * KEYS, (place + 1) * KEYS)
-            dkv[4 * block + place, 0] = key_grad[part].astype(BF16)
-            dkv[4 * block + place, 1] = value_grad[part].astype(BF16)
-        slots = slice(4 * block, 4 * block + 4)
+            dkv[8 * block + place, 0] = key_grad[part].astype(BF16)
+            dkv[8 * block + place, 1] = value_grad[part].astype(BF16)
+        slots = slice(8 * block, 8 * block + 8)
         copy = pltpu.make_async_copy(dkv.at[slots], grads.at[slots], sem.at[block])
         copy.start()
         writes.append(copy)

time: 87.7 us -> 87.7 us (level)
  no operation moved by 1% of the time
where the time goes in v9:
time: 87.7 us; the launch traced here: 87.2 us
  waiting for transfers between devices  36.9 us (42%)
  starting transfers between devices  36.3 us (41%)
  Pallas kernels  13.3 us (15%)
    all_to_all x2, starting transfers between devices, exchange(): lax.all_to_all(chunks, AXES, split_axis=0, concat_axis=0, tiled=True, axi...  18.1 us
    ppermute x1, waiting for transfers between devices, local(): other = lax.ppermute(other, 'x', NEXT)  11.8 us
    ppermute x3, waiting for transfers between devices, local(): mine = [part] + [lax.ppermute(part, 'zl', turn(k)) for k in (1, 2, 3)]  11.1 us
    all_to_all x2, waiting for transfers between devices, exchange(): lax.all_to_all(chunks, AXES, split_axis=0, concat_axis=0, tiled=True, axi...  7.31 us
    pallas_call x1, Pallas kernels, attention(): call(attention_kernel, [pltpu.HBM((16, 2, KEYS, DH), BF16), shape(*part,...  6.88 us
    ppermute x1, starting transfers between devices, local(): other = lax.ppermute(other, 'x', NEXT)  5.78 us
    ppermute x3, starting transfers between devices, local(): mine = [part] + [lax.ppermute(part, 'zl', turn(k)) for k in (1, 2, 3)]  4.81 us
    ppermute x3, waiting for transfers between devices, local(): sums = [sums[0]] + [lax.ppermute(sums[k], 'zl', turn(k)) for k in (1, 2, 3)]  4.11 us
  transfers between devices with their start and end apart: 17, of which 10 were waited for; matrix products, arithmetic and copies ran while one was open for 0% of the time, Pallas kernels for 4%

profile of v9, /device:TPU:1, one launch (start us, length us, event | category | flops | bytes accessed | tf_op | source)
XLA Modules:
  0.0 87.2 jit_solution(2008028090600453617)
XLA Ops:
  0.6 0.9 message.1.own
  1.5 2.1 %collective-permute-start = (bf16[144,256]{1,0:T(8,128)(2,1)S(1)}, bf16[144,256]{1,0:T(8,128)(2,1)S(1)}, u32[]{:S(2)}, u32[]{:S(2)}) collective-permute-start(bf16[144,256]{1,0:T(8,128)(2,1)S(1)} %message.1.own), channel_id=1, source_target_pairs={{0,8},{8,0},{16,24},{24,16},{1,9},{9,1},{17,25},{25,17},{2,10},{10... | collective-permute-start | bytes 221192 | tf_op jit(solution)/shard_map/ppermute | solution.py:376
  3.6 2.8 %split.1 = bf16[16,2,128,256]{3,2,1,0:T(8,128)(2,1)} custom-call(bf16[128,4096]{1,0:T(8,128)(2,1)} %keys.1, bf16[128,4096]{1,0:T(8,128)(2,1)} %values.1), custom_call_target="tpu_custom_call" | custom-call | bytes 8388608 | tf_op jit(solution)/shard_map/split/pallas_call | solution.py:173
  6.5 0.0 collective-permute-done.other
  6.5 8.7 %all-to-all-start = ((bf16[16,2,128,256]{3,2,1,0:T(8,128)(2,1)}), bf16[16,2,128,256]{3,2,1,0:T(8,128)(2,1)S(1)}, u32[]{:S(2)}, u32[]{:S(2)}) async-start(bf16[16,2,128,256]{3,2,1,0:T(8,128)(2,1)} %split.1), calls=%async_computation | async-start | bytes 4194304 | tf_op jit(solution)/shard_map/all_to_all | solution.py:72
  15.2 0.7 collective-permute-start.1
  15.8 0.0 collective-permute-done.1.crossed
  15.9 4.4 %collective-permute-start.4 = (bf16[272,256]{1,0:T(8,128)(2,1)S(1)}, bf16[272,256]{1,0:T(8,128)(2,1)S(1)}, u32[]{:S(2)}, u32[]{:S(2)}) collective-permute-start(bf16[272,256]{1,0:T(8,128)(2,1)S(1)} %choose.1.refs_0_), channel_id=1, source_target_pairs={{0,3},{1,2},{2,1},{3,0},{4,7},{5,6},{6,5},{7,4},{8,11},{9,10},{10,... | collective-permute-start | bytes 417800 | tf_op jit(solution)/shard_map/ppermute | solution.py:382
  20.3 0.0 collective-permute-start.3
  20.3 0.4 collective-permute-start.2
  20.7 0.0 collective-permute-start.5
  20.7 3.8 %collective-permute-done.4.refs_3_ = bf16[272,256]{1,0:T(8,128)(2,1)S(1)} collective-permute-done((bf16[272,256]{1,0:T(8,128)(2,1)S(1)}, bf16[272,256]{1,0:T(8,128)(2,1)S(1)}, u32[]{:S(2)}, u32[]{:S(2)}) %collective-permute-start.4) | collective-permute-done | bytes 139296 | tf_op jit(solution)/shard_map/ppermute | solution.py:382
  24.5 0.0 collective-permute-start.8
  24.5 7.3 %collective-permute-done.3.refs_2_ = bf16[272,256]{1,0:T(8,128)(2,1)S(1)} collective-permute-done((bf16[272,256]{1,0:T(8,128)(2,1)S(1)}, bf16[272,256]{1,0:T(8,128)(2,1)S(1)}, u32[]{:S(2)}, u32[]{:S(2)}) %collective-permute-start.3) | collective-permute-done | bytes 139296 | tf_op jit(solution)/shard_map/ppermute | solution.py:382
  31.8 0.1 collective-permute-start.7
  31.9 0.0 collective-permute-done.2.refs_1_
  31.9 0.4 collective-permute-start.6
  32.3 0.0 collective-permute-done.5.refs_4_
  32.3 0.0 collective-permute-done.8.refs_7_
  32.3 0.8 collective-permute-done.7.refs_6_
  33.2 0.2 collective-permute-done.6.refs_5_
  33.4 0.9 %assemble.1 = (bf16[4,256,256]{2,1,0:T(8,128)(2,1)S(1)}, bf16[4,256,256]{2,1,0:T(8,128)(2,1)}, f32[4,8,256]{2,1,0:T(8,128)S(1)}) custom-call(bf16[272,256]{1,0:T(8,128)(2,1)S(1)} %choose.1.refs_0_, bf16[272,256]{1,0:T(8,128)(2,1)S(1)} %collective-permute-done.2.refs_1_, bf16[272,256]{1,0:T(8,128)(2,1)S(1)} %collective-permute-done.3.refs_2_, ...), custom_call_target="tpu_custom_call" | custom-call | tf_op jit(solution)/shard_map/assemble/pallas_call | solution.py:230
  34.2 7.1 %all-to-all-done.kv = bf16[16,2,128,256]{3,2,1,0:T(8,128)(2,1)S(1)} async-done(((bf16[16,2,128,256]{3,2,1,0:T(8,128)(2,1)}), bf16[16,2,128,256]{3,2,1,0:T(8,128)(2,1)S(1)}, u32[]{:S(2)}, u32[]{:S(2)}) %all-to-all-start) | async-done | bytes 2097184 | tf_op jit(solution)/shard_map/all_to_all | solution.py:72
  41.4 6.9 %attention.1 = (bf16[16,2,128,256]{3,2,1,0:T(8,128)(2,1)}, f32[4,2,64,256]{3,2,1,0:T(8,128)S(1)}, bf16[4,2,64,256]{3,2,1,0:T(8,128)(2,1)S(1)}) custom-call(bf16[4,256,256]{2,1,0:T(8,128)(2,1)S(1)} %get-tuple-element.21.qt, bf16[4,256,256]{2,1,0:T(8,128)(2,1)} %get-tuple-element.22.cotangent, f32[4,8,256]{2,1,0:T(8,128)S(1)} %get-tuple-element.23.stat, ...), custom_call_target="tpu_custom_call" | custom-call | flops 5368709120 | bytes 8388608 | tf_op jit(solution)/shard_map/attention/pallas_call | solution.py:287
  48.2 9.5 %all-to-all-start.1 = ((bf16[16,2,128,256]{3,2,1,0:T(8,128)(2,1)}), bf16[16,2,128,256]{3,2,1,0:T(8,128)(2,1)S(1)}, u32[]{:S(2)}, u32[]{:S(2)}) async-start(bf16[16,2,128,256]{3,2,1,0:T(8,128)(2,1)} %get-tuple-element.25), calls=%async_computation.1 | async-start | bytes 4194304 | tf_op jit(solution)/shard_map/all_to_all | solution.py:72
  57.7 0.0 collective-permute-start.9
  57.7 1.5 %collective-permute-done.9.other = bf16[4,2,64,256]{3,2,1,0:T(8,128)(2,1)S(1)} collective-permute-done((bf16[4,2,64,256]{3,2,1,0:T(8,128)(2,1)S(1)}, bf16[4,2,64,256]{3,2,1,0:T(8,128)(2,1)S(1)}, u32[]{:S(2)}, u32[]{:S(2)}) %collective-permute-start.9) | collective-permute-done | bytes 262176 | tf_op jit(solution)/shard_map/ppermute | solution.py:386
  59.3 0.1 collective-permute-start.10
  59.4 2.4 %collective-permute-start.11 = (bf16[2,64,256]{2,1,0:T(8,128)(2,1)S(1)}, bf16[2,64,256]{2,1,0:T(8,128)(2,1)S(1)}, u32[]{:S(2)}, u32[]{:S(2)}) collective-permute-start(bf16[2,64,256]{2,1,0:T(8,128)(2,1)S(1)} %get-tuple-element.30), channel_id=1, source_target_pairs={{0,2},{1,3},{2,0},{3,1},{4,6},{5,7},{6,4},{7,5},{8,10},{9,11},{10,... | collective-permute-start | bytes 196616 | tf_op jit(solution)/shard_map/ppermute | solution.py:387
  61.8 1.1 %collective-permute-start.12 = (bf16[2,64,256]{2,1,0:T(8,128)(2,1)S(1)}, bf16[2,64,256]{2,1,0:T(8,128)(2,1)S(1)}, u32[]{:S(2)}, u32[]{:S(2)}) collective-permute-start(bf16[2,64,256]{2,1,0:T(8,128)(2,1)S(1)} %get-tuple-element.31), channel_id=1, source_target_pairs={{0,3},{1,2},{2,1},{3,0},{4,7},{5,6},{6,5},{7,4},{8,11},{9,10},{10,... | collective-permute-start | bytes 196616 | tf_op jit(solution)/shard_map/ppermute | solution.py:387
  62.9 0.0 collective-permute-done.10.refs_1_
  62.9 1.0 %collective-permute-done.11.refs_2_ = bf16[2,64,256]{2,1,0:T(8,128)(2,1)S(1)} collective-permute-done((bf16[2,64,256]{2,1,0:T(8,128)(2,1)S(1)}, bf16[2,64,256]{2,1,0:T(8,128)(2,1)S(1)}, u32[]{:S(2)}, u32[]{:S(2)}) %collective-permute-start.11) | collective-permute-done | bytes 65568 | tf_op jit(solution)/shard_map/ppermute | solution.py:387
  63.9 3.1 %collective-permute-done.12.refs_3_ = bf16[2,64,256]{2,1,0:T(8,128)(2,1)S(1)} collective-permute-done((bf16[2,64,256]{2,1,0:T(8,128)(2,1)S(1)}, bf16[2,64,256]{2,1,0:T(8,128)(2,1)S(1)}, u32[]{:S(2)}, u32[]{:S(2)}) %collective-permute-start.12) | collective-permute-done | bytes 65568 | tf_op jit(solution)/shard_map/ppermute | solution.py:387
  67.1 0.7 collective-permute-start.13
  67.8 0.0 collective-permute-done.13.crossed
  67.8 5.8 %collective-permute-start.14 = (bf16[64,256]{1,0:T(8,128)(2,1)S(1)}, bf16[64,256]{1,0:T(8,128)(2,1)S(1)}, u32[]{:S(2)}, u32[]{:S(2)}) collective-permute-start(bf16[64,256]{1,0:T(8,128)(2,1)S(1)} %get-tuple-element.33), channel_id=1, source_target_pairs={{0,8},{8,0},{16,24},{24,16},{1,9},{9,1},{17,25},{25,17},{2,10},{10... | collective-permute-start | bytes 98312 | tf_op jit(solution)/shard_map/ppermute | solution.py:390
  73.6 11.8 %collective-permute-done.14.other = bf16[64,256]{1,0:T(8,128)(2,1)S(1)} collective-permute-done((bf16[64,256]{1,0:T(8,128)(2,1)S(1)}, bf16[64,256]{1,0:T(8,128)(2,1)S(1)}, u32[]{:S(2)}, u32[]{:S(2)}) %collective-permute-start.14) | collective-permute-done | bytes 32800 | tf_op jit(solution)/shard_map/ppermute | solution.py:390
  85.4 0.2 all-to-all-done.1.chunks
  85.6 1.7 %join.1 = (bf16[128,4096]{1,0:T(8,128)(2,1)}, bf16[128,4096]{1,0:T(8,128)(2,1)}, bf16[64,256]{1,0:T(8,128)(2,1)}) custom-call(bf16[16,2,128,256]{3,2,1,0:T(8,128)(2,1)S(1)} %all-to-all-done.1.chunks, bf16[64,256]{1,0:T(8,128)(2,1)S(1)} %get-tuple-element.32.own, bf16[64,256]{1,0:T(8,128)(2,1)S(1)} %collective-permute-done.14.other), custom_call_target="tpu_custom_call" | custom-call | tf_op jit(solution)/shard_map/join/pallas_call | solution.py:200
  (5 shorter events, 0.2 us)
Async XLA Ops:
  1.5 5.0 %collective-permute-start = (bf16[144,256]{1,0:T(8,128)(2,1)S(1)}, bf16[144,256]{1,0:T(8,128)(2,1)S(1)}, u32[]{:S(2)}, u32[]{:S(2)}) collective-permute-start(bf16[144,256]{1,0:T(8,128)(2,1)S(1)} %message.1.own), channel_id=1, source_target_pairs={{0,8},{8,0},{16,24},{24,16},{1,9},{9,1},{17,25},{25,17},{2,10},{10... | collective-permute-start | bytes 221192 | tf_op jit(solution)/shard_map/ppermute | solution.py:376
  6.5 34.9 %all-to-all-start = ((bf16[16,2,128,256]{3,2,1,0:T(8,128)(2,1)}), bf16[16,2,128,256]{3,2,1,0:T(8,128)(2,1)S(1)}, u32[]{:S(2)}, u32[]{:S(2)}) async-start(bf16[16,2,128,256]{3,2,1,0:T(8,128)(2,1)} %split.1), calls=%async_computation | async-start | bytes 4194304 | tf_op jit(solution)/shard_map/all_to_all | solution.py:72
  15.2 0.7 collective-permute-start.1
  15.9 8.6 %collective-permute-start.4 = (bf16[272,256]{1,0:T(8,128)(2,1)S(1)}, bf16[272,256]{1,0:T(8,128)(2,1)S(1)}, u32[]{:S(2)}, u32[]{:S(2)}) collective-permute-start(bf16[272,256]{1,0:T(8,128)(2,1)S(1)} %choose.1.refs_0_), channel_id=1, source_target_pairs={{0,3},{1,2},{2,1},{3,0},{4,7},{5,6},{6,5},{7,4},{8,11},{9,10},{10,... | collective-permute-start | bytes 417800 | tf_op jit(solution)/shard_map/ppermute | solution.py:382
  20.3 11.5 %collective-permute-start.3 = (bf16[272,256]{1,0:T(8,128)(2,1)S(1)}, bf16[272,256]{1,0:T(8,128)(2,1)S(1)}, u32[]{:S(2)}, u32[]{:S(2)}) collective-permute-start(bf16[272,256]{1,0:T(8,128)(2,1)S(1)} %choose.1.refs_0_), channel_id=1, source_target_pairs={{0,2},{1,3},{2,0},{3,1},{4,6},{5,7},{6,4},{7,5},{8,10},{9,11},{10,... | collective-permute-start | bytes 417800 | tf_op jit(solution)/shard_map/ppermute | solution.py:382
  20.3 11.6 %collective-permute-start.2 = (bf16[272,256]{1,0:T(8,128)(2,1)S(1)}, bf16[272,256]{1,0:T(8,128)(2,1)S(1)}, u32[]{:S(2)}, u32[]{:S(2)}) collective-permute-start(bf16[272,256]{1,0:T(8,128)(2,1)S(1)} %choose.1.refs_0_), channel_id=1, source_target_pairs={{0,1},{1,0},{2,3},{3,2},{4,5},{5,4},{6,7},{7,6},{8,9},{9,8},{10,11... | collective-permute-start | bytes 417800 | tf_op jit(solution)/shard_map/ppermute | solution.py:382
  20.7 11.6 %collective-permute-start.5 = (bf16[272,256]{1,0:T(8,128)(2,1)S(1)}, bf16[272,256]{1,0:T(8,128)(2,1)S(1)}, u32[]{:S(2)}, u32[]{:S(2)}) collective-permute-start(bf16[272,256]{1,0:T(8,128)(2,1)S(1)} %choose.1.refs_0_), channel_id=1, source_target_pairs={{0,4},{4,0},{1,5},{5,1},{2,6},{6,2},{3,7},{7,3},{8,12},{12,8},{9,1... | collective-permute-start | bytes 417800 | tf_op jit(solution)/shard_map/ppermute | solution.py:383
  24.5 7.8 %collective-permute-start.8 = (bf16[272,256]{1,0:T(8,128)(2,1)S(1)}, bf16[272,256]{1,0:T(8,128)(2,1)S(1)}, u32[]{:S(2)}, u32[]{:S(2)}) collective-permute-start(bf16[272,256]{1,0:T(8,128)(2,1)S(1)} %collective-permute-done.4.refs_3_), channel_id=1, source_target_pairs={{0,4},{4,0},{1,5},{5,1},{2,6},{6,2},{3,7},{7,3},{8,12},{12,8},{9,1... | collective-permute-start | bytes 417800 | tf_op jit(solution)/shard_map/ppermute | solution.py:383
  31.8 1.4 %collective-permute-start.7 = (bf16[272,256]{1,0:T(8,128)(2,1)S(1)}, bf16[272,256]{1,0:T(8,128)(2,1)S(1)}, u32[]{:S(2)}, u32[]{:S(2)}) collective-permute-start(bf16[272,256]{1,0:T(8,128)(2,1)S(1)} %collective-permute-done.3.refs_2_), channel_id=1, source_target_pairs={{0,4},{4,0},{1,5},{5,1},{2,6},{6,2},{3,7},{7,3},{8,12},{12,8},{9,1... | collective-permute-start | bytes 417800 | tf_op jit(solution)/shard_map/ppermute | solution.py:383
  31.9 1.4 %collective-permute-start.6 = (bf16[272,256]{1,0:T(8,128)(2,1)S(1)}, bf16[272,256]{1,0:T(8,128)(2,1)S(1)}, u32[]{:S(2)}, u32[]{:S(2)}) collective-permute-start(bf16[272,256]{1,0:T(8,128)(2,1)S(1)} %collective-permute-done.2.refs_1_), channel_id=1, source_target_pairs={{0,4},{4,0},{1,5},{5,1},{2,6},{6,2},{3,7},{7,3},{8,12},{12,8},{9,1... | collective-permute-start | bytes 417800 | tf_op jit(solution)/shard_map/ppermute | solution.py:383
  48.2 37.3 %all-to-all-start.1 = ((bf16[16,2,128,256]{3,2,1,0:T(8,128)(2,1)}), bf16[16,2,128,256]{3,2,1,0:T(8,128)(2,1)S(1)}, u32[]{:S(2)}, u32[]{:S(2)}) async-start(bf16[16,2,128,256]{3,2,1,0:T(8,128)(2,1)} %get-tuple-element.25), calls=%async_computation.1 | async-start | bytes 4194304 | tf_op jit(solution)/shard_map/all_to_all | solution.py:72
  57.7 1.5 %collective-permute-start.9 = (bf16[4,2,64,256]{3,2,1,0:T(8,128)(2,1)S(1)}, bf16[4,2,64,256]{3,2,1,0:T(8,128)(2,1)S(1)}, u32[]{:S(2)}, u32[]{:S(2)}) collective-permute-start(bf16[4,2,64,256]{3,2,1,0:T(8,128)(2,1)S(1)} %get-tuple-element.27), channel_id=1, source_target_pairs={{0,4},{4,0},{1,5},{5,1},{2,6},{6,2},{3,7},{7,3},{8,12},{12,8},{9,1... | collective-permute-start | bytes 786440 | tf_op jit(solution)/shard_map/ppermute | solution.py:386
  59.3 3.6 %collective-permute-start.10 = (bf16[2,64,256]{2,1,0:T(8,128)(2,1)S(1)}, bf16[2,64,256]{2,1,0:T(8,128)(2,1)S(1)}, u32[]{:S(2)}, u32[]{:S(2)}) collective-permute-start(bf16[2,64,256]{2,1,0:T(8,128)(2,1)S(1)} %get-tuple-element.29), channel_id=1, source_target_pairs={{0,1},{1,0},{2,3},{3,2},{4,5},{5,4},{6,7},{7,6},{8,9},{9,8},{10,11... | collective-permute-start | bytes 196616 | tf_op jit(solution)/shard_map/ppermute | solution.py:387
  59.4 4.5 %collective-permute-start.11 = (bf16[2,64,256]{2,1,0:T(8,128)(2,1)S(1)}, bf16[2,64,256]{2,1,0:T(8,128)(2,1)S(1)}, u32[]{:S(2)}, u32[]{:S(2)}) collective-permute-start(bf16[2,64,256]{2,1,0:T(8,128)(2,1)S(1)} %get-tuple-element.30), channel_id=1, source_target_pairs={{0,2},{1,3},{2,0},{3,1},{4,6},{5,7},{6,4},{7,5},{8,10},{9,11},{10,... | collective-permute-start | bytes 196616 | tf_op jit(solution)/shard_map/ppermute | solution.py:387
  61.8 5.2 %collective-permute-start.12 = (bf16[2,64,256]{2,1,0:T(8,128)(2,1)S(1)}, bf16[2,64,256]{2,1,0:T(8,128)(2,1)S(1)}, u32[]{:S(2)}, u32[]{:S(2)}) collective-permute-start(bf16[2,64,256]{2,1,0:T(8,128)(2,1)S(1)} %get-tuple-element.31), channel_id=1, source_target_pairs={{0,3},{1,2},{2,1},{3,0},{4,7},{5,6},{6,5},{7,4},{8,11},{9,10},{10,... | collective-permute-start | bytes 196616 | tf_op jit(solution)/shard_map/ppermute | solution.py:387
  67.1 0.7 collective-permute-start.13
  67.8 17.6 %collective-permute-start.14 = (bf16[64,256]{1,0:T(8,128)(2,1)S(1)}, bf16[64,256]{1,0:T(8,128)(2,1)S(1)}, u32[]{:S(2)}, u32[]{:S(2)}) collective-permute-start(bf16[64,256]{1,0:T(8,128)(2,1)S(1)} %get-tuple-element.33), channel_id=1, source_target_pairs={{0,8},{8,0},{16,24},{24,16},{1,9},{9,1},{17,25},{25,17},{2,10},{10... | collective-permute-start | bytes 98312 | tf_op jit(solution)/shard_map/ppermute | solution.py:390
